TPU v7x, 128 devices: a whole 4x4x4 slice. The times are simulated.
128 devices in a mesh: member: 8 (over y, z_lo), token: 16 (over z_hi, x, core).
Axes of the slice: x: 4, y: 4, z: 4 (z_hi: 2, z_lo: 2; z = z_hi * 2 + z_lo), core: 2. Of those that a mesh axis runs over, the one named last changes fastest.
Arguments:
- latents: bfloat16 [2048, 1024], P('token', 'member'), may hold values from -6 to 6
- noise: bfloat16 [32, 2048, 128], P('member', 'token'), may hold values from -6 to 6
- noise_weight: bfloat16 [128, 1024], replicated, may hold values from -0.5 to 0.5
- gain: bfloat16 [1024], replicated, may hold values from 0.25 to 1.75
- w_in: bfloat16 [1024, 4096], replicated, may hold values from -0.1875 to 0.1875
- w_out: bfloat16 [4096, 768], replicated, may hold values from -0.09375 to 0.09375
- observed: bfloat16 [2048, 768], P(('token', 'member')), may hold values from -6 to 6
Outputs:
- grad_w_out: float32 [4096, 768], P(('member', 'token'))
- grad_latents: float32 [2048, 1024], P('token', 'member')
All inputs are finite; a program needn't handle non-finite values.
Results may differ from a plain program's by a relative error of at most 0.0012.
Values may be sent and summed in bfloat16 or wider, within the bound.
No kernel may reach another device: no remote copies, remote signals or barrier semaphores. Data moves between devices by JAX's collectives and lax.ppermute only.
A program may use at most 128 MiB of HBM per device.

v0:
```python
import jax
import jax.numpy as jnp
from jax import lax
from jax.sharding import PartitionSpec as P


def gelu_tanh(values):
    return jax.nn.gelu(values, approximate=True)


def score_one(own, every, target):
    err = own - target
    enorm = jnp.sqrt(jnp.mean(err * err, axis=-1, keepdims=True) + 1e-06)
    diff = own[None] - every
    dist = jnp.sqrt(jnp.mean(diff * diff, axis=-1, keepdims=True) + 1e-06)
    spread = jnp.sum(diff / dist, axis=0) / every.shape[0]
    return err / enorm - spread


def score_many(owned, every, target):
    return jax.vmap(lambda own: score_one(own, every, target))(owned)


def per_device(latents, noise, noise_weight, gain, w_in, w_out, observed):
    whole = lax.all_gather(latents, "member", axis=1, tiled=True)
    members_here, tok_rows, _ = noise.shape
    width = whole.shape[1]
    fields = w_out.shape[1]
    cond = whole.astype(jnp.float32)[None] + jnp.einsum(
        "mte,ed->mtd", noise, noise_weight, preferred_element_type=jnp.float32
    )
    cond = cond.reshape(members_here * tok_rows, width)
    gain_f = gain.astype(jnp.float32)
    scale = lax.rsqrt(jnp.mean(cond * cond, axis=-1, keepdims=True) + 1e-05)
    normed = (cond * scale * gain_f).astype(jnp.bfloat16)
    pre = jnp.dot(normed, w_in, preferred_element_type=jnp.float32)
    hidden = gelu_tanh(pre).astype(jnp.bfloat16)
    pred = jnp.dot(hidden, w_out, preferred_element_type=jnp.float32).astype(jnp.bfloat16)
    pred = pred.reshape(members_here, tok_rows, fields)
    gathered = lax.all_to_all(pred, "member", split_axis=1, concat_axis=0, tiled=True)
    every = gathered.astype(jnp.float32)
    local_grad = score_many(every, every, observed.astype(jnp.float32))
    score_grad = lax.all_to_all(local_grad, "member", split_axis=0, concat_axis=1, tiled=True)
    flat_grad = score_grad.reshape(members_here * tok_rows, fields)
    columns = hidden.astype(jnp.float32)
    grad_w_out = lax.psum_scatter(
        lax.dot_general(
            columns,
            flat_grad,
            (((0,), (0,)), ((), ())),
            preferred_element_type=jnp.float32,
            precision=lax.Precision.HIGHEST,
        ),
        ("member", "token"),
        scatter_dimension=0,
        tiled=True,
    )
    dhidden = lax.dot_general(
        flat_grad,
        w_out.astype(jnp.float32),
        (((1,), (1,)), ((), ())),
        preferred_element_type=jnp.float32,
        precision=lax.Precision.HIGHEST,
    )
    _, pullback = jax.vjp(gelu_tanh, pre)
    dpre = pullback(dhidden)[0].astype(jnp.bfloat16)
    dnormed = lax.dot_general(
        dpre, w_in, (((1,), (1,)), ((), ())), preferred_element_type=jnp.float32
    )
    weighted = dnormed * gain_f
    dcond = scale * weighted - cond * scale**3 * jnp.mean(weighted * cond, axis=-1, keepdims=True)
    member_sum = jnp.sum(dcond.reshape(members_here, tok_rows, width), axis=0)
    grad_latents = lax.psum_scatter(member_sum, "member", scatter_dimension=1, tiled=True)
    return (grad_w_out, grad_latents)


def solution(mesh):
    placed = (
        P("token", "member"),
        P("member", "token", None),
        P(),
        P(),
        P(),
        P(),
        P(("token", "member"), None),
    )
    return jax.shard_map(
        per_device,
        mesh=mesh,
        in_specs=placed,
        out_specs=(P(("member", "token"), None), P("token", "member")),
        check_vma=False,
    )
```

profile of v0, /device:TPU:0, one launch (start us, length us, event | category | flops | bytes accessed | tf_op | source)
XLA Modules:
  0.0 842.3 jit_solution(16935620155593598353)
XLA Ops:
  7.2 0.0 copy-start
  7.2 0.7 convert_element_type.49
  7.9 25.4 %all_gather.3 = bf16[128,1024]{1,0:T(8,128)(2,1)S(1)} all-gather(bf16[128,128]{1,0:T(8,128)(2,1)} %param.7), channel_id=1, replica_groups=mesh['member'=8,'token'=16] {'member'}, dimensions={1}, use_global_device_ids=true | all-gather | bytes 294912 | tf_op jit(solution)/shard_map/all_gather | solution.py:25
  33.3 0.0 copy-done
  33.3 1.4 multiply_reduce_fusion
  34.8 0.0 slice-start
  34.8 0.2 fusion.12
  35.0 0.0 slice-start.1
  35.0 7.1 fusion.27
  42.1 0.0 slice-done
  42.2 0.0 slice-done.1
  42.2 0.0 copy-start.4
  42.2 0.0 copy-start.3
  42.2 5.2 convolution_convert_fusion
  47.4 0.0 copy-done.4
  47.4 1.5 copy.21
  48.9 3.9 all-to-all-start
  52.8 0.0 reduce-scatter.5.cloned.1.call-start
  52.9 0.0 copy-done.3
  52.9 9.5 %all-to-all-done = bf16[4,128,768]{2,0,1:T(4,128)(2,1)S(1)} async-done(((bf16[4,128,768]{2,0,1:T(4,128)(2,1)}), bf16[4,128,768]{2,0,1:T(4,128)(2,1)S(1)}, u32[]{:S(2)}, u32[]{:S(2)}) %all-to-all-start) | async-done | bytes 786464 | tf_op jit(solution)/shard_map/all_to_all | solution.py:40
  62.4 0.2 fusion.26
  62.6 0.3 fusion.17
  62.9 0.1 copy.23
  63.0 14.1 %fusion.1 = f32[32,32,16]{2,1,0:T(8,128)S(1)} fusion(f32[32,16,768]{2,1,0:T(8,128)S(1)} %bitcast.47), kind=kLoop, calls=%fused_computation.3 | loop fusion | flops 37732352 | bytes 1638400 | tf_op jit(solution)/shard_map/vmap()/reduce_sum | solution.py:15
  77.1 0.2 add_sqrt_fusion
  77.3 0.0 slice-start.2
  77.3 8.5 %fusion = f32[32,16,768]{2,1,0:T(8,128)S(1)} fusion(f32[32,32,16]{2,1,0:T(8,128)S(1)} %add_sqrt_fusion, f32[32,16,768]{2,1,0:T(8,128)S(1)} %bitcast.48), kind=kLoop, calls=%fused_computation.2 | loop fusion | flops 37355520 | bytes 3211264 | tf_op jit(solution)/shard_map/vmap()/reduce_sum | solution.py:16
  85.8 0.0 slice-start.3
  85.8 0.4 multiply_subtract_fusion
  86.2 18.3 %all_to_all.24 = f32[32,16,768]{2,1,0:T(8,128)S(1)} all-to-all(f32[32,16,768]{2,1,0:T(8,128)S(1)} %multiply_subtract_fusion), channel_id=1, replica_groups=mesh['member'=8,'token'=16] {'member'}, dimensions={0} | all-to-all | bytes 3145728 | tf_op jit(solution)/shard_map/all_to_all | solution.py:43
  104.5 0.1 copy.25
  104.7 0.0 copy-start.2
  104.7 1.2 copy-done.2
  105.9 0.0 slice-done.2
  105.9 0.0 slice-done.3
  105.9 12.5 %fusion.28 = f32[512,4096]{1,0:T(8,128)} fusion(f32[512,768]{1,0:T(8,128)S(1)} %bitcast.55, bf16[4096,768]{1,0:T(8,128)(2,1)S(1)} %bitcast.54), kind=kOutput, calls=%fused_computation.46 | convolution fusion | flops 19327352832 | bytes 16252928 | tf_op jit(solution)/shard_map/dot_general | solution.py:58
  118.4 14.6 %fusion.15 = (f32[512]{0:T(512)S(1)}, f32[512,1024]{1,0:T(8,128)S(1)}) fusion(f32[4,128,1024]{2,1,0:T(8,128)S(1)} %get-tuple-element.5, f32[1024]{0:T(1024)S(1)} %convert_element_type.49, bf16[1024,4096]{1,0:T(8,128)(2,1)} %param.11, f32[512,4096]{1,0:T(8,128)} %copy-done.4, f32[512,4096]{1,0:T(8,128)} %fusion.28), kind=kOutput, calls=%fused_computation.22 | convolution fusion | flops 4338482688 | bytes 29366272 | tf_op jit(solution)/shard_map/dot_general | solution.py:67
  133.0 1.8 fusion.14
  134.8 2.6 reduce_sum.62
  137.4 0.0 reduce-scatter.5.cloned.1.call-update
  137.4 0.3 reduce-scatter.3.cloned.1.call-start
  137.7 0.0 copy-start.1
  137.7 17.8 %fusion.25 = f32[4096,768]{1,0:T(8,128)} fusion(f32[512,768]{1,0:T(8,128)} %bitcast.56, f32[512,4096]{1,0:T(8,128)} %copy-done.4), kind=kOutput, calls=%fused_computation.43 | convolution fusion | flops 19346227200 | bytes 22544384 | tf_op jit(solution)/shard_map/dot_general | solution.py:47
  155.5 0.0 reduce-scatter.3.cloned.1.call-update
  155.5 20.3 %reduce-scatter.5.cloned.1.call-done = f32[128,128]{1,0:T(8,128)} async-done(((f32[128,1024]{1,0:T(8,128)}), f32[128,128]{1,0:T(8,128)}) %reduce-scatter.5.cloned.1.call-update) | async-done | bytes 65552 | tf_op jit(solution)/shard_map/reduce_scatter | solution.py:73
  175.8 659.7 %reduce-scatter.3.cloned.1.call-done = f32[32,768]{1,0:T(8,128)} async-done(((f32[4096,768]{1,0:T(8,128)}), f32[32,768]{1,0:T(8,128)}) %reduce-scatter.3.cloned.1.call-update) | async-done | bytes 98320 | tf_op jit(solution)/shard_map/reduce_scatter | solution.py:46
  835.5 0.0 copy-done.1
  (8 shorter events, 0.1 us)
Async XLA Ops:
  7.2 26.2 %copy-start = (bf16[128,1024]{1,0:T(8,128)(2,1)S(1)}, bf16[128,1024]{1,0:T(8,128)(2,1)}, u32[]{:S(2)}) copy-start(bf16[128,1024]{1,0:T(8,128)(2,1)} %param.9) | copy-start | bytes 786436
  34.8 7.4 slice-start
  35.0 7.1 slice-start.1
  42.2 5.2 copy-start.4
  42.2 10.7 %copy-start.3 = (bf16[16,768]{1,0:T(8,128)(2,1)S(1)}, bf16[16,768]{1,0:T(8,128)(2,1)}, u32[]{:S(2)}) copy-start(bf16[16,768]{1,0:T(8,128)(2,1)} %param.13) | copy-start | bytes 73732
  48.9 13.5 %all-to-all-start = ((bf16[4,128,768]{2,0,1:T(4,128)(2,1)}), bf16[4,128,768]{2,0,1:T(4,128)(2,1)S(1)}, u32[]{:S(2)}, u32[]{:S(2)}) async-start(bf16[4,128,768]{2,0,1:T(4,128)(2,1)} %copy.21), calls=%async_computation | async-start | bytes 1572864 | tf_op jit(solution)/shard_map/all_to_all | solution.py:40
  52.8 122.9 %reduce-scatter.5.cloned.1.call-start = ((), (), s32[]{:S(2)}) async-start(), calls=%async_computation.5 | async-start | bytes 589824 | tf_op jit(solution)/shard_map/reduce_scatter | solution.py:73
  77.3 28.6 %slice-start.2 = ((s8[6291456]{0:T(1024)(128)(4,1)}), s8[4194304]{0:T(1024)(128)(4,1)S(1)}, s32[]{:S(2)}) async-start(s8[6291456]{0:T(1024)(128)(4,1)} %bitcast.53), calls=%async_computation.8 | async-start | bytes 8388608
  85.8 20.1 %slice-start.3 = ((s8[6291456]{0:T(1024)(128)(4,1)}), s8[2097152]{0:T(1024)(128)(4,1)S(1)}, s32[]{:S(2)}) async-start(s8[6291456]{0:T(1024)(128)(4,1)} %bitcast.53), calls=%async_computation.9 | async-start | bytes 4194304
  104.7 1.2 copy-start.2
  137.4 698.1 %reduce-scatter.3.cloned.1.call-start = ((), (), s32[]{:S(2)}) async-start(), calls=%async_computation.4 | async-start | bytes 12681216 | tf_op jit(solution)/shard_map/reduce_scatter | solution.py:46
  137.7 697.8 %copy-start.1 = (bf16[128,1024]{1,0:T(8,128)(2,1)S(1)}, bf16[128,1024]{1,0:T(8,128)(2,1)}, u32[]{:S(2)}) copy-start(bf16[128,1024]{1,0:T(8,128)(2,1)} %param.9) | copy-start | bytes 786436
Sparse Core Ops, SparseCore 0:
  137.5 38.1 reduce-scatter.4
  178.8 656.6 reduce-scatter.2
where the time goes:
time: 843 us; the launch traced here: 842 us
  waiting for transfers between devices  690 us (82%)
  matrix products  58.6 us (7%)
  blocking collectives  43.7 us (5%)
  other arithmetic  29.1 us (3%)
  between operations  14.3 us (2%)
    reduce_scatter x1, waiting for transfers between devices, per_device(): lax.psum_scatter(lax.dot_general(columns, flat_grad, (((0,), (0,)), ((),...  660 us
    all_gather x1, blocking collectives, per_device(): whole = lax.all_gather(latents, 'member', axis=1, tiled=True)  25.4 us
    reduce_scatter x1, waiting for transfers between devices, per_device(): lax.psum_scatter(member_sum, 'member', scatter_dimension=1, tiled=True)  20.3 us
    all_to_all x1, blocking collectives, per_device(): lax.all_to_all(local_grad, 'member', split_axis=0, concat_axis=1, tiled=T...  18.3 us
    dot_general x1, matrix products, per_device(): lax.dot_general(columns, flat_grad, (((0,), (0,)), ((), ())), preferred_e...  17.8 us
  transfers between devices with their start and end apart: 3, of which 3 were waited for; matrix products, arithmetic and copies ran while one was open for 2% of the time, Pallas kernels for 0%

commit v1 on v0

v1 whole, which is shorter than its diff:
```python
import functools

import jax
import jax.numpy as jnp
import numpy as np
from jax import lax
from jax.experimental import pallas as pl
from jax.experimental.pallas import tpu as pltpu
from jax.sharding import PartitionSpec as P

AXES = ("member", "token")
FIRST = (("x0", "y0", "z0"), ("x1", "y1", "z1"))
VMEM = 56 * 1024 * 1024


def coords(index):
    member, token = divmod(index, 16)
    y, z_lo = divmod(member, 2)
    z_hi, x, core = token // 8, token // 2 % 4, token % 2
    return {"x": x, "y": y, "z": 2 * z_hi + z_lo}, core


def index_of(place, core):
    return (place["y"] * 2 + place["z"] % 2) * 16 + (place["z"] // 2) * 8 + place["x"] * 2 + core


def chip_bits(chip):
    place, _ = coords(2 * chip)
    bits = {}
    for axis in "xyz":
        value = place[axis]
        bits[axis + "0"] = (value & 1) ^ (value >> 1)
        bits[axis + "1"] = value >> 1
    return bits


def order_of(core, part):
    first = FIRST[core]
    return first[part:] + first[:part] + FIRST[1 - core]


def positions():
    table = np.zeros((128, 3, 64), np.int32)
    bits = [chip_bits(chip) for chip in range(64)]
    for device in range(128):
        mine = bits[device // 2]
        for part in range(3):
            order = order_of(device % 2, part)
            for chip in range(64):
                place = 0
                for dim in order:
                    place = 2 * place + (mine[dim] ^ bits[chip][dim])
                table[device, part, chip] = place
    return table.reshape(128, 192)


def partner(index, dim):
    place, core = coords(index)
    place[dim[0]] ^= 1 if dim[1] == "0" else 3
    return index_of(place, core)


def swap_stage(values, part, stage):
    pairs = [(i, partner(i, order_of(i % 2, part)[stage])) for i in range(128)]
    return lax.ppermute(values, AXES, pairs)


def swap_core(values):
    return lax.ppermute(values, AXES, [(i, i ^ 1) for i in range(128)])


def params(**more):
    return pltpu.CompilerParams(vmem_limit_bytes=VMEM, **more)


def hidden_kernel(moved_ref, nw_ref, gain_ref, w_in_ref, cond_ref, scale_ref, hidden_ref, slope_ref, normed_ref):
    @pl.when(pl.program_id(0) == 0)
    def _():
        moved = moved_ref[...]
        noise = moved[:, :4].reshape(512, 128)
        latents = jnp.concatenate([moved[j, 4] for j in range(8)], axis=1).astype(jnp.float32)
        cond = jnp.dot(noise, nw_ref[...], preferred_element_type=jnp.float32)
        cond = (cond.reshape(32, 16, 1024) + latents[None]).reshape(512, 1024)
        scale = lax.rsqrt(jnp.mean(cond * cond, axis=-1, keepdims=True) + 1e-05)
        cond_ref[...] = cond
        scale_ref[...] = scale
        normed_ref[...] = (cond * scale * gain_ref[...].astype(jnp.float32)).astype(jnp.bfloat16)

    pre = jnp.dot(normed_ref[...], w_in_ref[...], preferred_element_type=jnp.float32)
    root = np.float32(np.sqrt(2 / np.pi))
    cubic = np.float32(np.sqrt(2 / np.pi) * 0.044715)
    square = pre * pre
    half = 0.5 * pre
    bend = jnp.tanh(pre * (root + cubic * square))
    hidden_ref[...] = (half + half * bend).astype(jnp.bfloat16)
    slope_ref[...] = 0.5 + 0.5 * bend + half * (1.0 - bend * bend) * (root + 3.0 * cubic * square)


def make_hidden(moved, noise_weight, gain, w_in, chunk=512):
    steps = 4096 // chunk
    whole = lambda *shape: pl.BlockSpec(shape, lambda i: (0,) * len(shape))
    return pl.pallas_call(
        hidden_kernel,
        grid=(steps,),
        in_specs=[
            whole(8, 5, 16, 128),
            whole(128, 1024),
            whole(1, 1024),
            pl.BlockSpec((1024, chunk), lambda i: (0, i)),
        ],
        out_specs=[
            whole(512, 1024),
            whole(512, 1),
            pl.BlockSpec((512, chunk), lambda i: (0, i)),
            pl.BlockSpec((512, chunk), lambda i: (0, i)),
        ],
        out_shape=[
            jax.ShapeDtypeStruct((512, 1024), jnp.float32),
            jax.ShapeDtypeStruct((512, 1), jnp.float32),
            jax.ShapeDtypeStruct((512, 4096), jnp.bfloat16),
            jax.ShapeDtypeStruct((512, 4096), jnp.float32),
        ],
        scratch_shapes=[pltpu.VMEM((512, 1024), jnp.bfloat16)],
        compiler_params=params(),
        cost_estimate=pl.CostEstimate(flops=2 * 512 * 1024 * 4096, bytes_accessed=24 << 20, transcendentals=1 << 21),
        name="hidden_rows",
    )(moved, noise_weight, gain, w_in)


def score_kernel(core_ref, hidden_ref, w_out_ref, target_ref, high_ref, low_ref, own_ref, other_ref, total_ref, pred_ref, grad_ref):
    step = pl.program_id(0)
    term = jnp.dot(hidden_ref[...], w_out_ref[...], preferred_element_type=jnp.float32)

    @pl.when(step == 0)
    def _():
        total_ref[...] = term

    @pl.when(step > 0)
    def _():
        total_ref[...] += term

    @pl.when(step == pl.num_programs(0) - 1)
    def _():
        pred_ref[...] = total_ref[...].astype(jnp.bfloat16).astype(jnp.float32).reshape(32, 16, 768)
        grad_ref[...] = jnp.zeros_like(grad_ref)

        def pair(member, own, other, total):
            diff = own - pred_ref[other]
            inverse = lax.rsqrt(jnp.mean(diff * diff, axis=-1, keepdims=True) + 1e-06)
            push = diff * inverse
            grad_ref[other] -= push
            return total + push

        def ring(member, carry):
            own = pred_ref[member]
            total = jnp.zeros((16, 768), jnp.float32)
            for offset in range(1, 16):
                total = pair(member, own, lax.rem(member + offset, 32), total)
            grad_ref[member] += total
            return carry

        def opposite(member, carry):
            grad_ref[member] += pair(member, pred_ref[member], member + 16, jnp.zeros((16, 768), jnp.float32))
            return carry

        lax.fori_loop(0, 32, ring, 0)
        lax.fori_loop(0, 16, opposite, 0)
        err = pred_ref[...] - target_ref[...].astype(jnp.float32)[None]
        inverse = lax.rsqrt(jnp.mean(err * err, axis=-1, keepdims=True) + 1e-06)
        grad = (err * inverse - grad_ref[...] * (1.0 / 32)).reshape(512, 768)
        high = grad.astype(jnp.bfloat16)
        low = (grad - high.astype(jnp.float32)).astype(jnp.bfloat16)
        high_ref[...] = high
        low_ref[...] = low

        def halves(mine_ref, yours_ref):
            mine_ref[:, :384] = high[:, :384]
            mine_ref[:, 384:] = low[:, :384]
            yours_ref[:, :384] = high[:, 384:]
            yours_ref[:, 384:] = low[:, 384:]

        @pl.when(core_ref[0] == 0)
        def _():
            halves(own_ref, other_ref)

        @pl.when(core_ref[0] == 1)
        def _():
            halves(other_ref, own_ref)


def make_score(core, hidden, w_out, observed, chunk=512):
    whole = lambda *shape: pl.BlockSpec(shape, lambda i, c: (0,) * len(shape))
    return pl.pallas_call(
        score_kernel,
        grid_spec=pltpu.PrefetchScalarGridSpec(
            num_scalar_prefetch=1,
            grid=(4096 // chunk,),
            in_specs=[
                pl.BlockSpec((512, chunk), lambda i, c: (0, i)),
                pl.BlockSpec((chunk, 768), lambda i, c: (i, 0)),
                whole(16, 768),
            ],
            out_specs=[whole(512, 768)] * 4,
            scratch_shapes=[
                pltpu.VMEM((512, 768), jnp.float32),
                pltpu.VMEM((32, 16, 768), jnp.float32),
                pltpu.VMEM((32, 16, 768), jnp.float32),
            ],
        ),
        out_shape=[jax.ShapeDtypeStruct((512, 768), jnp.bfloat16)] * 4,
        compiler_params=params(),
        cost_estimate=pl.CostEstimate(flops=2 * 512 * 768 * 4096 * 3, bytes_accessed=14 << 20, transcendentals=0),
        name="score_rows",
    )(core, hidden, w_out, observed)


def outer_kernel(places_ref, mine_ref, theirs_ref, own_ref, got_ref, *outs):
    sums = (((0,), (0,)), ((), ()))
    both = lax.dot_general(mine_ref[...], own_ref[...], sums, preferred_element_type=jnp.float32)
    both += lax.dot_general(theirs_ref[...], got_ref[...], sums, preferred_element_type=jnp.float32)
    result = both[:, :384] + both[:, 384:]
    blocks = result.shape[0] // 64
    for block in range(blocks):
        for part in range(3):
            place = places_ref[part * 64 + pl.program_id(0) * blocks + block]
            piece = result[block * 64 : block * 64 + 64, part * 128 : part * 128 + 128]

            @pl.when(place < 32)
            def _():
                outs[part][pl.ds(pl.multiple_of(place * 64, 64), 64), :] = piece

            @pl.when(place >= 32)
            def _():
                outs[3 + part][pl.ds(pl.multiple_of((place - 32) * 64, 64), 64), :] = piece


def make_outer(places, mine, theirs, own, got, chunk=256):
    whole = lambda *shape: pl.BlockSpec(shape, lambda i, c: (0,) * len(shape))
    return pl.pallas_call(
        outer_kernel,
        grid_spec=pltpu.PrefetchScalarGridSpec(
            num_scalar_prefetch=1,
            grid=(4096 // chunk,),
            in_specs=[
                pl.BlockSpec((512, chunk), lambda i, c: (0, i)),
                pl.BlockSpec((512, chunk), lambda i, c: (0, i)),
                whole(512, 768),
                whole(512, 768),
            ],
            out_specs=[whole(2048, 128)] * 6,
        ),
        out_shape=[jax.ShapeDtypeStruct((2048, 128), jnp.float32)] * 6,
        compiler_params=params(),
        cost_estimate=pl.CostEstimate(flops=2 * 1024 * 768 * 4096, bytes_accessed=16 << 20, transcendentals=0),
        name="outer_rows",
    )(places, mine, theirs, own, got)


def back_kernel(high_ref, low_ref, w_out_ref, w_in_ref, slope_ref, cond_ref, scale_ref, gain_ref, out_ref, total_ref):
    step = pl.program_id(0)
    last = (((1,), (1,)), ((), ()))
    w_out = w_out_ref[...]
    back = lax.dot_general(high_ref[...], w_out, last, preferred_element_type=jnp.float32)
    back += lax.dot_general(low_ref[...], w_out, last, preferred_element_type=jnp.float32)
    dpre = (back * slope_ref[...]).astype(jnp.bfloat16)
    term = lax.dot_general(dpre, w_in_ref[...], last, preferred_element_type=jnp.float32)

    @pl.when(step == 0)
    def _():
        total_ref[...] = term

    @pl.when(step > 0)
    def _():
        total_ref[...] += term

    @pl.when(step == pl.num_programs(0) - 1)
    def _():
        cond = cond_ref[...]
        scale = scale_ref[...]
        weighted = total_ref[...] * gain_ref[...].astype(jnp.float32)
        mean = jnp.mean(weighted * cond, axis=-1, keepdims=True)
        dcond = scale * weighted - cond * (scale * scale * scale * mean)
        out_ref[...] = jnp.sum(dcond.reshape(32, 16, 1024), axis=0)


def make_back(high, low, w_out, w_in, slope, cond, scale, gain, chunk=512):
    whole = lambda *shape: pl.BlockSpec(shape, lambda i: (0,) * len(shape))
    return pl.pallas_call(
        back_kernel,
        grid=(4096 // chunk,),
        in_specs=[
            whole(512, 768),
            whole(512, 768),
            pl.BlockSpec((chunk, 768), lambda i: (i, 0)),
            pl.BlockSpec((1024, chunk), lambda i: (0, i)),
            pl.BlockSpec((512, chunk), lambda i: (0, i)),
            whole(512, 1024),
            whole(512, 1),
            whole(1, 1024),
        ],
        out_specs=whole(16, 1024),
        out_shape=jax.ShapeDtypeStruct((16, 1024), jnp.float32),
        scratch_shapes=[pltpu.VMEM((512, 1024), jnp.float32)],
        compiler_params=params(),
        cost_estimate=pl.CostEstimate(flops=2 * 512 * 4096 * (768 * 2 + 1024), bytes_accessed=28 << 20, transcendentals=0),
        name="back_rows",
    )(high, low, w_out, w_in, slope, cond, scale, gain)


def per_device(latents, noise, noise_weight, gain, w_in, w_out, observed):
    device = lax.axis_index(AXES)
    places = lax.dynamic_index_in_dim(jnp.asarray(positions()), device, 0, keepdims=False)
    core = (device % 2).reshape(1)
    gain = gain.reshape(1, 1024)

    moved = jnp.concatenate([noise, latents[None]], axis=0)
    moved = lax.all_to_all(moved, "member", split_axis=1, concat_axis=0, tiled=True)
    cond, scale, hidden, slope = make_hidden(moved.reshape(8, 5, 16, 128), noise_weight, gain, w_in)
    theirs = swap_core(hidden)
    high, low, own, other = make_score(core, hidden, w_out, observed)
    got = swap_core(other)
    outs = make_outer(places, hidden, theirs, own, got)
    keep, send = list(outs[:3]), list(outs[3:])

    latent_sum = make_back(high, low, w_out, w_in, slope, cond, scale, gain)
    grad_latents = lax.all_to_all(latent_sum, "member", split_axis=1, concat_axis=0, tiled=True)

    for stage in range(2):
        came = [swap_stage(send[part], part, stage) for part in range(3)]
        rows = 1024 >> stage
        send = [keep[part][rows:] + came[part][rows:] for part in range(3)]
        keep = [keep[part][:rows] + came[part][:rows] for part in range(3)]
    came = [swap_stage(send[part], part, 2) for part in range(3)]
    rows = 256
    send = jnp.concatenate([keep[part][rows:] + came[part][rows:] for part in range(3)], axis=1)
    keep = jnp.concatenate([keep[part][:rows] + came[part][:rows] for part in range(3)], axis=1)
    for stage in range(3, 6):
        came = swap_stage(send, 0, stage)
        rows = rows // 2
        if stage < 5:
            send, keep = keep[rows:] + came[rows:], keep[:rows] + came[:rows]
    block = keep + came
    top, bottom = block[:32], block[32:]
    first = core[0] == 0
    mine = jnp.where(first, top, bottom)
    given = swap_core(jnp.where(first, bottom, top))
    grad_w_out = jnp.where(
        first, jnp.concatenate([mine, given], axis=1), jnp.concatenate([given, mine], axis=1)
    )
    return (grad_w_out, grad_latents)


def solution(mesh):
    placed = (
        P("token", "member"),
        P("member", "token", None),
        P(),
        P(),
        P(),
        P(),
        P(("token", "member"), None),
    )
    return jax.shard_map(
        per_device,
        mesh=mesh,
        in_specs=placed,
        out_specs=(P(("member", "token"), None), P("token", "member")),
        check_vma=False,
    )
```

time: 843 us -> 157 us (0.19)
  waiting for transfers between devices: 690 us -> 41.3 us
  Pallas kernels: 0 us -> 73.4 us
  matrix products: 58.6 us -> 0 us
  blocking collectives: 43.7 us -> 0 us
  other arithmetic: 29.1 us -> 4.62 us
  starting transfers between devices: 4.22 us -> 27.9 us
  between operations: 14.3 us -> 0.73 us
    reduce_scatter x2 -> x0, waiting for transfers between devices: 680 us -> none  [the longest x1 660 us: per_device(): lax.psum_scatter(lax.dot_general(columns, flat_grad, (((0,), (0,)), ((),...]
    pallas_call x0 -> x4, Pallas kernels: none -> 73.4 us  [the longest x1 20.3 us: make_score(): pl.pallas_call(score_kernel, grid_spec=pltpu.PrefetchScalarGridSpec(num_s...]
    dot_general x6 -> x0, matrix products: 58.6 us -> none  [the longest x1 17.8 us: per_device(): lax.dot_general(columns, flat_grad, (((0,), (0,)), ((), ())), preferred_e...]
    ppermute x0 -> x15, waiting for transfers between devices: none -> 29.2 us  [the longest x12 28.3 us: swap_stage(): return lax.ppermute(values, AXES, pairs)]
    reduce_sum x4 -> x0, other arithmetic: 25.5 us -> none  [the longest x1 14.1 us: score_one(): dist = jnp.sqrt(jnp.mean(diff * diff, axis=-1, keepdims=True) + 1e-06)]
    all_gather x1 -> x0, blocking collectives: 25.4 us -> none  [per_device(): whole = lax.all_gather(latents, 'member', axis=1, tiled=True)]
    all_to_all x1 -> x0, blocking collectives: 18.3 us -> none  [per_device(): lax.all_to_all(local_grad, 'member', split_axis=0, concat_axis=1, tiled=T...]
    ppermute x0 -> x15, starting transfers between devices: none -> 18 us  [the longest x12 17.5 us: swap_stage(): return lax.ppermute(values, AXES, pairs)]
  transfers between devices with their start and end apart: 3 -> 17, of which waited for: 3 -> 10; matrix products, arithmetic and copies ran while one was open for 2% -> 4% of each run, Pallas kernels for 0% -> 25%
where the time goes in v1:
time: 157 us; the launch traced here: 156 us
  Pallas kernels  73.4 us (47%)
  waiting for transfers between devices  41.3 us (26%)
  starting transfers between devices  27.9 us (18%)
  local copies, waits for them, and re-layouts  8.02 us (5%)
  other arithmetic  4.62 us (3%)
    ppermute x12, waiting for transfers between devices, swap_stage(): return lax.ppermute(values, AXES, pairs)  28.3 us
    pallas_call x1, Pallas kernels, make_score(): pl.pallas_call(score_kernel, grid_spec=pltpu.PrefetchScalarGridSpec(num_s...  20.3 us
    pallas_call x1, Pallas kernels, make_outer(): pl.pallas_call(outer_kernel, grid_spec=pltpu.PrefetchScalarGridSpec(num_s...  19.5 us
    pallas_call x1, Pallas kernels, make_back(): pl.pallas_call(back_kernel, grid=(4096 // chunk,), in_specs=[whole(512, 7...  18.9 us
    ppermute x12, starting transfers between devices, swap_stage(): return lax.ppermute(values, AXES, pairs)  17.5 us
    pallas_call x1, Pallas kernels, make_hidden(): pl.pallas_call(hidden_kernel, grid=(steps,), in_specs=[whole(8, 5, 16, 12...  14.7 us
    all_to_all x1, waiting for transfers between devices, per_device(): lax.all_to_all(latent_sum, 'member', split_axis=1, concat_axis=0, tiled=T...  6.11 us
    all_to_all x1, waiting for transfers between devices, per_device(): lax.all_to_all(moved, 'member', split_axis=1, concat_axis=0, tiled=True)  5.94 us
  transfers between devices with their start and end apart: 17, of which 10 were waited for; matrix products, arithmetic and copies ran while one was open for 4% of the time, Pallas kernels for 25%

profile of v1, /device:TPU:0, one launch (start us, length us, event | category | flops | bytes accessed | tf_op | source)
XLA Modules:
  0.0 155.9 jit_solution(1301224774686453059)
XLA Ops:
  0.6 0.8 copy.18
  1.4 1.0 copy.17
  2.5 0.8 pad_maximum_fusion.2
  3.3 5.9 %all-to-all-start = ((bf16[5,128,128]{2,0,1:T(8,128)(2,1)}), bf16[5,128,128]{2,0,1:T(8,128)(2,1)S(1)}, u32[]{:S(2)}, u32[]{:S(2)}) async-start(bf16[5,128,128]{2,0,1:T(8,128)(2,1)} %pad_maximum_fusion.2), calls=%async_computation | async-start | bytes 524288 | tf_op jit(solution)/shard_map/all_to_all | solution.py:317
  9.2 1.3 reshape.15.gain_ref
  10.5 5.9 %all-to-all-done = bf16[5,128,128]{2,0,1:T(8,128)(2,1)S(1)} async-done(((bf16[5,128,128]{2,0,1:T(8,128)(2,1)}), bf16[5,128,128]{2,0,1:T(8,128)(2,1)S(1)}, u32[]{:S(2)}, u32[]{:S(2)}) %all-to-all-start) | async-done | bytes 163872 | tf_op jit(solution)/shard_map/all_to_all | solution.py:317
  16.4 0.7 copy.27
  17.1 14.7 %hidden_rows.1 = (f32[512,1024]{1,0:T(8,128)}, f32[512,1]{1,0:T(8,128)}, bf16[512,4096]{1,0:T(8,128)(2,1)}, f32[512,4096]{1,0:T(8,128)}) custom-call(bf16[8,5,16,128]{3,2,1,0:T(8,128)(2,1)} %bitcast.17, bf16[128,1024]{1,0:T(8,128)(2,1)} %nw_ref.1, bf16[1,1024]{1,0:T(2,128)(2,1)} %reshape.15.gain_ref, bf16[1024,4096]{1,0:T(8,128)(2,1)} %w_in_ref.3), custom_call_target="tpu_custom_call" | custom-call | flops 4294967296 | bytes 25165824 | tf_op jit(solution)/shard_map/hidden_rows/pallas_call | solution.py:102
  31.8 0.0 collective-permute-start
  31.8 20.3 %score_rows.1 = (bf16[512,768]{1,0:T(8,128)(2,1)}, bf16[512,768]{1,0:T(8,128)(2,1)}, bf16[512,768]{1,0:T(8,128)(2,1)}, bf16[512,768]{1,0:T(8,128)(2,1)}) custom-call(s32[1]{0:T(128)} %bitcast.4.core_ref, bf16[512,4096]{1,0:T(8,128)(2,1)} %get-tuple-element.16.hidden_ref.mine_ref, bf16[4096,768]{1,0:T(8,128)(2,1)} %w_out_ref.3, bf16[16,768]{1,0:T(8,128)(2,1)} %target_ref.1), custom_call_target="tpu_custom_call" | custom-call | flops 9663676416 | bytes 14680064 | tf_op jit(solution)/shard_map/score_rows/pallas_call | solution.py:193
  52.1 0.5 collective-permute-start.1
  52.6 1.3 constant_dynamic-slice_fusion
  53.8 0.9 collective-permute-done.1.got_ref
  54.7 0.0 copy-start.1
  54.7 0.0 collective-permute-done.theirs_ref
  54.7 0.9 copy-done.1
  55.6 19.5 %outer_rows.1 = (f32[2048,128]{1,0:T(8,128)}, f32[2048,128]{1,0:T(8,128)}, f32[2048,128]{1,0:T(8,128)}, f32[2048,128]{1,0:T(8,128)}, f32[2048,128]{1,0:T(8,128)}, /*index=5*/f32[2048,128]{1,0:T(8,128)}) custom-call(s32[192]{0:T(256)} %bitcast.19, bf16[512,4096]{1,0:T(8,128)(2,1)} %get-tuple-element.16.hidden_ref.mine_ref, ...), custom_call_target="tpu_custom_call" | custom-call | flops 6442450944 | bytes 16777216 | tf_op jit(solution)/shard_map/outer_rows/pallas_call | solution.py:239
  75.1 0.0 copy-start
  75.1 1.5 collective-permute-start.2
  76.6 0.3 collective-permute-start.5
  76.9 1.2 collective-permute-start.8
  78.0 12.0 %collective-permute-done.2 = f32[2048,128]{1,0:T(8,128)S(1)} collective-permute-done((f32[2048,128]{1,0:T(8,128)}, f32[2048,128]{1,0:T(8,128)S(1)}, u32[]{:S(2)}, u32[]{:S(2)}) %collective-permute-start.2) | collective-permute-done | bytes 1048608 | tf_op jit(solution)/shard_map/ppermute | solution.py:65
  90.1 1.3 slice_add_fusion.5
  91.4 0.4 collective-permute-start.3
  91.8 0.0 collective-permute-done.5
  91.8 1.3 slice_add_fusion.3
  93.1 1.3 collective-permute-start.6
  94.4 0.0 collective-permute-done.8
  94.4 0.0 copy-done
  94.4 0.1 slice_add_fusion.1
  94.5 1.6 %collective-permute-start.9 = (f32[1024,128]{1,0:T(8,128)S(1)}, f32[1024,128]{1,0:T(8,128)S(1)}, u32[]{:S(2)}, u32[]{:S(2)}) collective-permute-start(f32[1024,128]{1,0:T(8,128)S(1)} %get-tuple-element.35), channel_id=1, source_target_pairs={{0,2},{1,7},{2,0},{3,5},{4,6},{5,3},{6,4},{7,1},{8,10},{9,15},{10,... | collective-permute-start | bytes 1572872 | tf_op jit(solution)/shard_map/ppermute | solution.py:65
  96.0 4.6 %collective-permute-done.3 = f32[1024,128]{1,0:T(8,128)S(1)} collective-permute-done((f32[1024,128]{1,0:T(8,128)S(1)}, f32[1024,128]{1,0:T(8,128)S(1)}, u32[]{:S(2)}, u32[]{:S(2)}) %collective-permute-start.3) | collective-permute-done | bytes 524320 | tf_op jit(solution)/shard_map/ppermute | solution.py:65
  100.6 0.1 slice_add_fusion.11
  100.7 1.0 collective-permute-start.4
  101.7 0.7 collective-permute-done.6
  102.4 0.1 slice_add_fusion.9
  102.4 1.6 %collective-permute-start.7 = (f32[512,128]{1,0:T(8,128)S(1)}, f32[512,128]{1,0:T(8,128)S(1)}, u32[]{:S(2)}, u32[]{:S(2)}) collective-permute-start(f32[512,128]{1,0:T(8,128)S(1)} %get-tuple-element.39), channel_id=1, source_target_pairs={{0,2},{1,7},{2,0},{3,5},{4,6},{5,3},{6,4},{7,1},{8,10},{9,15},{10,... | collective-permute-start | bytes 786440 | tf_op jit(solution)/shard_map/ppermute | solution.py:65
  104.0 0.0 collective-permute-done.9
  104.0 0.1 slice_add_fusion.7
  104.1 1.8 %collective-permute-start.10 = (f32[512,128]{1,0:T(8,128)S(1)}, f32[512,128]{1,0:T(8,128)S(1)}, u32[]{:S(2)}, u32[]{:S(2)}) collective-permute-start(f32[512,128]{1,0:T(8,128)S(1)} %get-tuple-element.41), channel_id=1, source_target_pairs={{0,32},{1,97},{2,34},{3,99},{4,36},{5,101},{6,38},{7,103},{8,40},{... | collective-permute-start | bytes 786440 | tf_op jit(solution)/shard_map/ppermute | solution.py:65
  105.8 1.3 collective-permute-done.4
  107.2 1.7 %collective-permute-done.7 = f32[512,128]{1,0:T(8,128)S(1)} collective-permute-done((f32[512,128]{1,0:T(8,128)S(1)}, f32[512,128]{1,0:T(8,128)S(1)}, u32[]{:S(2)}, u32[]{:S(2)}) %collective-permute-start.7) | collective-permute-done | bytes 262176 | tf_op jit(solution)/shard_map/ppermute | solution.py:65
  108.9 1.6 %collective-permute-done.10 = f32[512,128]{1,0:T(8,128)S(1)} collective-permute-done((f32[512,128]{1,0:T(8,128)S(1)}, f32[512,128]{1,0:T(8,128)S(1)}, u32[]{:S(2)}, u32[]{:S(2)}) %collective-permute-start.10) | collective-permute-done | bytes 262176 | tf_op jit(solution)/shard_map/ppermute | solution.py:65
  110.6 2.6 %collective-permute-start.11 = (f32[256,384]{1,0:T(8,128)S(1)}, f32[256,384]{1,0:T(8,128)S(1)}, u32[]{:S(2)}, u32[]{:S(2)}) collective-permute-start(f32[256,384]{1,0:T(8,128)S(1)} %pad_maximum_fusion.1), channel_id=1, source_target_pairs={{0,6},{1,3},{2,4},{3,1},{4,2},{5,7},{6,0},{7,5},{8,14},{9,11},{10,... | collective-permute-start | bytes 1179656 | tf_op jit(solution)/shard_map/ppermute | solution.py:65
  113.2 6.5 %collective-permute-done.11 = f32[256,384]{1,0:T(8,128)S(1)} collective-permute-done((f32[256,384]{1,0:T(8,128)S(1)}, f32[256,384]{1,0:T(8,128)S(1)}, u32[]{:S(2)}, u32[]{:S(2)}) %collective-permute-start.11) | collective-permute-done | bytes 393248 | tf_op jit(solution)/shard_map/ppermute | solution.py:65
  119.6 0.1 slice_add_fusion.13
  119.7 1.5 collective-permute-start.12
  121.2 18.9 %back_rows.1 = f32[16,1024]{1,0:T(8,128)} custom-call(bf16[512,768]{1,0:T(8,128)(2,1)} %get-tuple-element.25.high_ref, bf16[512,768]{1,0:T(8,128)(2,1)} %get-tuple-element.26.low_ref, bf16[4096,768]{1,0:T(8,128)(2,1)} %w_out_ref.3, bf16[1024,4096]{1,0:T(8,128)(2,1)} %w_in_ref.3, f32[512,4096]{1,0:T(8,128)} %get-tuple-element.27.slope_ref, ...), custom_call_target="tpu_custom_call" | custom-call | flops 10737418240 | bytes 29360128 | tf_op jit(solution)/shard_map/back_rows/pallas_call | solution.py:288
  140.1 0.0 collective-permute-done.12
  140.1 2.8 %collective-permute-start.13 = (f32[64,384]{1,0:T(8,128)S(1)}, f32[64,384]{1,0:T(8,128)S(1)}, u32[]{:S(2)}, u32[]{:S(2)}) collective-permute-start(f32[64,384]{1,0:T(8,128)S(1)} %slice_add_fusion.20), channel_id=1, source_target_pairs={{0,24},{1,17},{2,26},{3,19},{4,28},{5,21},{6,30},{7,23},{8,16},{9,... | collective-permute-start | bytes 294920 | tf_op jit(solution)/shard_map/ppermute | solution.py:65
  142.9 1.5 copy_bitcast_fusion.1
  144.4 4.0 %all-to-all-start.1 = ((f32[16,8,128]{2,0,1:T(8,128)}), f32[16,8,128]{2,0,1:T(8,128)S(1)}, u32[]{:S(2)}, u32[]{:S(2)}) async-start(f32[16,8,128]{2,0,1:T(8,128)} %copy_bitcast_fusion.1), calls=%async_computation.1 | async-start | bytes 131072 | tf_op jit(solution)/shard_map/all_to_all | solution.py:326
  148.3 0.0 collective-permute-done.13
  148.4 0.1 collective-permute-start.14
  148.5 6.1 %all-to-all-done.1 = f32[16,8,128]{2,0,1:T(8,128)S(1)} async-done(((f32[16,8,128]{2,0,1:T(8,128)}), f32[16,8,128]{2,0,1:T(8,128)S(1)}, u32[]{:S(2)}, u32[]{:S(2)}) %all-to-all-start.1) | async-done | bytes 65568 | tf_op jit(solution)/shard_map/all_to_all | solution.py:326
  154.6 0.0 collective-permute-done.14
  154.6 0.7 maximum_select_fusion
  155.3 0.6 copy.29
  (8 shorter events, 0.2 us)
Async XLA Ops:
  3.3 13.1 %all-to-all-start = ((bf16[5,128,128]{2,0,1:T(8,128)(2,1)}), bf16[5,128,128]{2,0,1:T(8,128)(2,1)S(1)}, u32[]{:S(2)}, u32[]{:S(2)}) async-start(bf16[5,128,128]{2,0,1:T(8,128)(2,1)} %pad_maximum_fusion.2), calls=%async_computation | async-start | bytes 524288 | tf_op jit(solution)/shard_map/all_to_all | solution.py:317
  31.8 22.9 %collective-permute-start = (bf16[512,4096]{1,0:T(8,128)(2,1)}, bf16[512,4096]{1,0:T(8,128)(2,1)}, u32[]{:S(2)}, u32[]{:S(2)}) collective-permute-start(bf16[512,4096]{1,0:T(8,128)(2,1)} %get-tuple-element.16.hidden_ref.mine_ref), channel_id=1, source_target_pairs={{0,1},{1,0},{2,3},{3,2},{4,5},{5,4},{6,7},{7,6},{8,9},{9,8},{10,11... | collective-permute-start | bytes 12582920 | tf_op jit(solution)/shard_map/ppermute | solution.py:69
  52.1 2.6 %collective-permute-start.1 = (bf16[512,768]{1,0:T(8,128)(2,1)}, bf16[512,768]{1,0:T(8,128)(2,1)S(1)}, u32[]{:S(2)}, u32[]{:S(2)}) collective-permute-start(bf16[512,768]{1,0:T(8,128)(2,1)} %get-tuple-element.18), channel_id=1, source_target_pairs={{0,1},{1,0},{2,3},{3,2},{4,5},{5,4},{6,7},{7,6},{8,9},{9,8},{10,11... | collective-permute-start | bytes 2359304 | tf_op jit(solution)/shard_map/ppermute | solution.py:69
  54.7 0.9 copy-start.1
  75.1 19.3 %copy-start = (f32[2048,128]{1,0:T(8,128)S(1)}, f32[2048,128]{1,0:T(8,128)}, u32[]{:S(2)}) copy-start(f32[2048,128]{1,0:T(8,128)} %get-tuple-element.23) | copy-start | bytes 3145732
  75.1 15.0 %collective-permute-start.2 = (f32[2048,128]{1,0:T(8,128)}, f32[2048,128]{1,0:T(8,128)S(1)}, u32[]{:S(2)}, u32[]{:S(2)}) collective-permute-start(f32[2048,128]{1,0:T(8,128)} %get-tuple-element.20), channel_id=1, source_target_pairs={{0,2},{1,7},{2,0},{3,5},{4,6},{5,3},{6,4},{7,1},{8,10},{9,15},{10,... | collective-permute-start | bytes 3145736 | tf_op jit(solution)/shard_map/ppermute | solution.py:65
  76.6 15.2 %collective-permute-start.5 = (f32[2048,128]{1,0:T(8,128)}, f32[2048,128]{1,0:T(8,128)S(1)}, u32[]{:S(2)}, u32[]{:S(2)}) collective-permute-start(f32[2048,128]{1,0:T(8,128)} %get-tuple-element.22), channel_id=1, source_target_pairs={{0,32},{1,97},{2,34},{3,99},{4,36},{5,101},{6,38},{7,103},{8,40},{... | collective-permute-start | bytes 3145736 | tf_op jit(solution)/shard_map/ppermute | solution.py:65
  76.9 17.5 %collective-permute-start.8 = (f32[2048,128]{1,0:T(8,128)}, f32[2048,128]{1,0:T(8,128)S(1)}, u32[]{:S(2)}, u32[]{:S(2)}) collective-permute-start(f32[2048,128]{1,0:T(8,128)} %get-tuple-element.24), channel_id=1, source_target_pairs={{0,16},{1,25},{2,18},{3,27},{4,20},{5,29},{6,22},{7,31},{8,24},{9,... | collective-permute-start | bytes 3145736 | tf_op jit(solution)/shard_map/ppermute | solution.py:65
  91.4 9.3 %collective-permute-start.3 = (f32[1024,128]{1,0:T(8,128)S(1)}, f32[1024,128]{1,0:T(8,128)S(1)}, u32[]{:S(2)}, u32[]{:S(2)}) collective-permute-start(f32[1024,128]{1,0:T(8,128)S(1)} %get-tuple-element.31), channel_id=1, source_target_pairs={{0,32},{1,97},{2,34},{3,99},{4,36},{5,101},{6,38},{7,103},{8,40},{... | collective-permute-start | bytes 1572872 | tf_op jit(solution)/shard_map/ppermute | solution.py:65
  93.1 9.3 %collective-permute-start.6 = (f32[1024,128]{1,0:T(8,128)S(1)}, f32[1024,128]{1,0:T(8,128)S(1)}, u32[]{:S(2)}, u32[]{:S(2)}) collective-permute-start(f32[1024,128]{1,0:T(8,128)S(1)} %get-tuple-element.33), channel_id=1, source_target_pairs={{0,16},{1,25},{2,18},{3,27},{4,20},{5,29},{6,22},{7,31},{8,24},{9,... | collective-permute-start | bytes 1572872 | tf_op jit(solution)/shard_map/ppermute | solution.py:65
  94.5 9.5 %collective-permute-start.9 = (f32[1024,128]{1,0:T(8,128)S(1)}, f32[1024,128]{1,0:T(8,128)S(1)}, u32[]{:S(2)}, u32[]{:S(2)}) collective-permute-start(f32[1024,128]{1,0:T(8,128)S(1)} %get-tuple-element.35), channel_id=1, source_target_pairs={{0,2},{1,7},{2,0},{3,5},{4,6},{5,3},{6,4},{7,1},{8,10},{9,15},{10,... | collective-permute-start | bytes 1572872 | tf_op jit(solution)/shard_map/ppermute | solution.py:65
  100.7 6.5 %collective-permute-start.4 = (f32[512,128]{1,0:T(8,128)S(1)}, f32[512,128]{1,0:T(8,128)S(1)}, u32[]{:S(2)}, u32[]{:S(2)}) collective-permute-start(f32[512,128]{1,0:T(8,128)S(1)} %get-tuple-element.37), channel_id=1, source_target_pairs={{0,16},{1,25},{2,18},{3,27},{4,20},{5,29},{6,22},{7,31},{8,24},{9,... | collective-permute-start | bytes 786440 | tf_op jit(solution)/shard_map/ppermute | solution.py:65
  102.4 6.5 %collective-permute-start.7 = (f32[512,128]{1,0:T(8,128)S(1)}, f32[512,128]{1,0:T(8,128)S(1)}, u32[]{:S(2)}, u32[]{:S(2)}) collective-permute-start(f32[512,128]{1,0:T(8,128)S(1)} %get-tuple-element.39), channel_id=1, source_target_pairs={{0,2},{1,7},{2,0},{3,5},{4,6},{5,3},{6,4},{7,1},{8,10},{9,15},{10,... | collective-permute-start | bytes 786440 | tf_op jit(solution)/shard_map/ppermute | solution.py:65
  104.1 6.5 %collective-permute-start.10 = (f32[512,128]{1,0:T(8,128)S(1)}, f32[512,128]{1,0:T(8,128)S(1)}, u32[]{:S(2)}, u32[]{:S(2)}) collective-permute-start(f32[512,128]{1,0:T(8,128)S(1)} %get-tuple-element.41), channel_id=1, source_target_pairs={{0,32},{1,97},{2,34},{3,99},{4,36},{5,101},{6,38},{7,103},{8,40},{... | collective-permute-start | bytes 786440 | tf_op jit(solution)/shard_map/ppermute | solution.py:65
  110.6 9.1 %collective-permute-start.11 = (f32[256,384]{1,0:T(8,128)S(1)}, f32[256,384]{1,0:T(8,128)S(1)}, u32[]{:S(2)}, u32[]{:S(2)}) collective-permute-start(f32[256,384]{1,0:T(8,128)S(1)} %pad_maximum_fusion.1), channel_id=1, source_target_pairs={{0,6},{1,3},{2,4},{3,1},{4,2},{5,7},{6,0},{7,5},{8,14},{9,11},{10,... | collective-permute-start | bytes 1179656 | tf_op jit(solution)/shard_map/ppermute | solution.py:65
  119.7 20.4 %collective-permute-start.12 = (f32[128,384]{1,0:T(8,128)S(1)}, f32[128,384]{1,0:T(8,128)S(1)}, u32[]{:S(2)}, u32[]{:S(2)}) collective-permute-start(f32[128,384]{1,0:T(8,128)S(1)} %get-tuple-element.43), channel_id=1, source_target_pairs={{0,96},{1,33},{2,98},{3,35},{4,100},{5,37},{6,102},{7,39},{8,104},... | collective-permute-start | bytes 589832 | tf_op jit(solution)/shard_map/ppermute | solution.py:65
  140.1 8.2 %collective-permute-start.13 = (f32[64,384]{1,0:T(8,128)S(1)}, f32[64,384]{1,0:T(8,128)S(1)}, u32[]{:S(2)}, u32[]{:S(2)}) collective-permute-start(f32[64,384]{1,0:T(8,128)S(1)} %slice_add_fusion.20), channel_id=1, source_target_pairs={{0,24},{1,17},{2,26},{3,19},{4,28},{5,21},{6,30},{7,23},{8,16},{9,... | collective-permute-start | bytes 294920 | tf_op jit(solution)/shard_map/ppermute | solution.py:65
  144.4 10.2 %all-to-all-start.1 = ((f32[16,8,128]{2,0,1:T(8,128)}), f32[16,8,128]{2,0,1:T(8,128)S(1)}, u32[]{:S(2)}, u32[]{:S(2)}) async-start(f32[16,8,128]{2,0,1:T(8,128)} %copy_bitcast_fusion.1), calls=%async_computation.1 | async-start | bytes 131072 | tf_op jit(solution)/shard_map/all_to_all | solution.py:326
  148.4 6.2 %collective-permute-start.14 = (f32[32,384]{1,0:T(8,128)S(1)}, f32[32,384]{1,0:T(8,128)S(1)}, u32[]{:S(2)}, u32[]{:S(2)}) collective-permute-start(f32[32,384]{1,0:T(8,128)S(1)} %get-tuple-element.51), channel_id=1, source_target_pairs={{0,1},{1,0},{2,3},{3,2},{4,5},{5,4},{6,7},{7,6},{8,9},{9,8},{10,11... | collective-permute-start | bytes 147464 | tf_op jit(solution)/shard_map/ppermute | solution.py:69

commit v2 on v0

v2 whole, which is shorter than its diff:
```python
import functools

import jax
import jax.numpy as jnp
import numpy as np
from jax import lax
from jax.experimental import pallas as pl
from jax.experimental.pallas import tpu as pltpu
from jax.sharding import PartitionSpec as P

AXES = ("member", "token")
FIRST = (("x0", "x1", "z1"), ("y0", "y1", "z0"))
CHUNK = 512
STEPS = 4096 // CHUNK
F32, BF16 = jnp.float32, jnp.bfloat16
LAST = (((1,), (1,)), ((), ()))


def coords(index):
    member, token = divmod(index, 16)
    y, z_lo = divmod(member, 2)
    z_hi, x, core = token // 8, token // 2 % 4, token % 2
    return {"x": x, "y": y, "z": 2 * z_hi + z_lo}, core


def index_of(place, core):
    return (place["y"] * 2 + place["z"] % 2) * 16 + (place["z"] // 2) * 8 + place["x"] * 2 + core


def chip_bits(chip):
    place, _ = coords(2 * chip)
    bits = {}
    for axis in "xyz":
        value = place[axis]
        bits[axis + "0"] = (value & 1) ^ (value >> 1)
        bits[axis + "1"] = value >> 1
    return bits


def order_of(core, part):
    return FIRST[core][part:] + FIRST[core][:part]


def group_place(index):
    place, core = coords(index)
    if core == 0:
        return (0, place["x"], place["z"] // 2), place["y"] * 2 + place["z"] % 2
    return (1, place["y"], place["z"] % 2 ^ place["z"] // 2), place["z"] // 2 * 4 + place["x"]


def last_groups():
    groups = {}
    for index in range(128):
        group, at = group_place(index)
        groups.setdefault(group, [None] * 8)[at] = index
    return [groups[name] for name in sorted(groups)]


def chip_table():
    table = np.zeros((128, 3, 64), np.int32)
    bits = [chip_bits(chip) for chip in range(64)]
    for device in range(128):
        mine, core = bits[device // 2], device % 2
        for part in range(3):
            for chip in range(64):
                place = 0
                for dim in order_of(core, part):
                    place = 2 * place + (mine[dim] ^ bits[chip][dim])
                table[device, part, 8 * place + group_place(2 * chip + core)[1]] = chip
    return table.reshape(128, 192)


def partner(index, dim):
    place, core = coords(index)
    place[dim[0]] ^= 1 if dim[1] == "0" else 3
    return index_of(place, core)


def swap_stage(values, part, stage):
    pairs = [(i, partner(i, order_of(i % 2, part)[stage])) for i in range(128)]
    return lax.ppermute(values, AXES, pairs)


def swap_core(values):
    return lax.ppermute(values, AXES, [(i, i ^ 1) for i in range(128)])


def call(body, name, outs, args, spaces, out_spaces, scratch=(), flops=0, limit=16):
    placed = [
        pltpu.with_memory_space_constraint(a, {"v": pltpu.VMEM, "a": pltpu.HBM}[space]) if space in "va" else a
        for a, space in zip(args, spaces)
    ]
    kinds = {"s": pltpu.SMEM, "v": pltpu.VMEM, "m": pltpu.VMEM, "a": pltpu.HBM, "h": pltpu.HBM}
    return pl.pallas_call(
        body,
        in_specs=[pl.BlockSpec(memory_space=kinds[space]) for space in spaces],
        out_specs=[pl.BlockSpec(memory_space=kinds[space]) for space in out_spaces],
        out_shape=[
            {"v": pltpu.VMEM, "h": pltpu.HBM, "m": jax.ShapeDtypeStruct}[space](shape, kind)
            for (shape, kind), space in zip(outs, out_spaces)
        ],
        scratch_shapes=list(scratch),
        compiler_params=pltpu.CompilerParams(vmem_limit_bytes=limit * 1024 * 1024),
        cost_estimate=pl.CostEstimate(
            flops=flops, bytes_accessed=sum(a.size * a.dtype.itemsize for a in args), transcendentals=0
        ),
        name=name,
    )(*placed)


def gather_kernel(noise_ref, latents_ref, out_ref):
    for j in range(8):
        rows = slice(j * 16, j * 16 + 16)
        for i in range(4):
            out_ref[j, i] = noise_ref[i, rows, :]
        out_ref[j, 4] = latents_ref[rows, :]


def forward_kernel(moved_ref, nw_hbm, gain_ref, w_in_hbm, w_out_hbm, cond_hbm, slope_hbm, pred_ref, *rest):
    turned = rest[:4]
    cond_ref, slope_ref, pre_ref, total_ref, out_sems, cond_sem = rest[4:10]
    w_in_ref, w_out_ref, nw_ref, in_sems, mid_sems, nw_sem = rest[10:]

    def columns(step):
        return slice(step * CHUNK, (step + 1) * CHUNK)

    def put(step):
        return pltpu.make_async_copy(slope_ref.at[step], slope_hbm.at[step], out_sems.at[step])

    def fetch_in(half):
        return [
            pltpu.make_async_copy(
                w_in_hbm.at[i * 256 : i * 256 + 256, half * 2048 : half * 2048 + 2048],
                w_in_ref.at[i * 256 : i * 256 + 256, half * 2048 : half * 2048 + 2048],
                in_sems.at[half, i],
            )
            for i in range(4)
        ]

    def fetch_out(step):
        return pltpu.make_async_copy(w_out_hbm.at[columns(step), :], w_out_ref.at[columns(step), :], mid_sems.at[step])

    fetch_nw = pltpu.make_async_copy(nw_hbm, nw_ref, nw_sem)
    fetch_nw.start()
    for copy in fetch_in(0):
        copy.start()
    for step in range(STEPS // 2):
        fetch_out(step).start()
    for copy in fetch_in(1):
        copy.start()
    for step in range(STEPS // 2, STEPS):
        fetch_out(step).start()
    moved = moved_ref[...]
    noise = moved[:, :4].reshape(512, 128)
    latents = jnp.concatenate([moved[j, 4] for j in range(8)], axis=1).astype(F32)
    fetch_nw.wait()
    cond = jnp.dot(noise, nw_ref[...], preferred_element_type=F32)
    cond = (cond.reshape(32, 16, 1024) + latents[None]).reshape(512, 1024)
    scale = lax.rsqrt(jnp.mean(cond * cond, axis=-1, keepdims=True) + 1e-05)
    cond_ref[...] = cond
    put_cond = pltpu.make_async_copy(cond_ref, cond_hbm, cond_sem)
    put_cond.start()
    normed = (cond * scale * gain_ref[...].astype(F32)).astype(BF16)
    root = np.float32(np.sqrt(2 / np.pi))
    cubic = np.float32(np.sqrt(2 / np.pi) * 0.044715)
    for step in range(STEPS + 1):
        if step in (0, STEPS // 2):
            for copy in fetch_in(step // (STEPS // 2)):
                copy.wait()
        if step < STEPS:
            pre_ref[step % 2] = jnp.dot(normed, w_in_ref[:, columns(step)], preferred_element_type=F32)
        if step > 0:
            done = step - 1
            pre = pre_ref[done % 2]
            square = pre * pre
            bend = jnp.tanh(pre * (root + cubic * square))
            cdf = 0.5 + 0.5 * bend
            value = pre * cdf
            hidden = value.astype(BF16)
            slope_ref[done] = cdf + (value - value * cdf) * (2.0 * root + 6.0 * cubic * square)
            flipped = hidden.T.reshape(8, 4, 16, 512)
            for i in range(4):
                turned[i][done * 128 : done * 128 + 128, :] = flipped[:, i].reshape(128, 512)
            put(done).start()
            fetch_out(done).wait()
            term = jnp.dot(hidden, w_out_ref[columns(done), :], preferred_element_type=F32)
            if done == 0:
                total_ref[...] = term
            elif done < STEPS - 1:
                total_ref[...] += term
            else:
                pred_ref[...] = (total_ref[...] + term).astype(BF16)
    put_cond.wait()
    for step in range(STEPS):
        put(step).wait()


def score_kernel(core_ref, pred_in_ref, target_ref, high_hbm, low_hbm, own_ref, other_ref, pred_ref, grad_ref, high_ref, low_ref, sems):
    pred_ref[...] = pred_in_ref[...].astype(F32).reshape(32, 16, 768)
    grad_ref[...] = jnp.zeros_like(grad_ref)

    def pair(own, other, total):
        diff = own - pred_ref[other]
        inverse = lax.rsqrt(jnp.mean(diff * diff, axis=-1, keepdims=True) + 1e-06)
        push = diff * inverse
        grad_ref[other] -= push
        return total + push

    def ring(member, carry):
        own = pred_ref[member]
        total = jnp.zeros((16, 768), F32)
        for offset in range(1, 16):
            total = pair(own, lax.rem(member + offset, 32), total)
        grad_ref[member] += total
        return carry

    def opposite(step, carry):
        for i in range(4):
            member = step * 4 + i
            grad_ref[member] += pair(pred_ref[member], member + 16, jnp.zeros((16, 768), F32))
        return carry

    lax.fori_loop(0, 32, ring, 0)
    lax.fori_loop(0, 4, opposite, 0)
    err = pred_ref[...] - target_ref[...].astype(F32)[None]
    inverse = lax.rsqrt(jnp.mean(err * err, axis=-1, keepdims=True) + 1e-06)
    grad = (err * inverse - grad_ref[...] * (1.0 / 32)).reshape(512, 768)
    high = grad.astype(BF16)
    low = (grad - high.astype(F32)).astype(BF16)
    high_ref[...] = high
    low_ref[...] = low
    copies = [
        pltpu.make_async_copy(high_ref, high_hbm, sems.at[0]),
        pltpu.make_async_copy(low_ref, low_hbm, sems.at[1]),
    ]
    for copy in copies:
        copy.start()

    def halves(mine_ref, yours_ref):
        for part in range(3):
            at = part * 128
            mine_ref[:, 2 * at : 2 * at + 128] = high[:, at : at + 128]
            mine_ref[:, 2 * at + 128 : 2 * at + 256] = low[:, at : at + 128]
            yours_ref[:, 2 * at : 2 * at + 128] = high[:, 384 + at : 512 + at]
            yours_ref[:, 2 * at + 128 : 2 * at + 256] = low[:, 384 + at : 512 + at]

    @pl.when(core_ref[0] == 0)
    def _():
        halves(own_ref, other_ref)

    @pl.when(core_ref[0] == 1)
    def _():
        halves(other_ref, own_ref)

    for copy in copies:
        copy.wait()


def outer_kernel(parts, side, chips_ref, own_ref, got_ref, *rest):
    mine, theirs, rest = rest[:4], rest[4:8], rest[8:]
    outs, (a_ref, b_ref) = rest[: len(parts)], rest[len(parts) :]
    for slot, part in enumerate(parts):
        fields = slice(part * 256, part * 256 + 256)
        for quarter in range(4):
            at = slice(quarter * 512, quarter * 512 + 512)
            for block in range(8):
                chip = chips_ref[part * 64 + side * 32 + quarter * 8 + block]
                rows = pl.ds(pl.multiple_of(chip * 16, 16), 16)
                for i in range(4):
                    first = quarter * 512 + block * 64 + i * 16
                    a_ref[first : first + 16, :] = mine[i][rows, :]
                    b_ref[first : first + 16, :] = theirs[i][rows, :]
            both = jnp.dot(a_ref[at, :], own_ref[:, fields], preferred_element_type=F32)
            both += jnp.dot(b_ref[at, :], got_ref[:, fields], preferred_element_type=F32)
            outs[slot][at, :] = both[:, :128] + both[:, 128:]


def make_outer(parts, side, chips, mine, theirs, own, got):
    n = len(parts)
    return call(
        functools.partial(outer_kernel, parts, side),
        "outer_send" if side else "outer_keep",
        [((2048, 128), F32)] * n,
        (chips, own, got, *mine, *theirs),
        "smm" + "m" * 8,
        "m" * n,
        [pltpu.VMEM((2048, 512), BF16)] * 2,
        flops=2 * 1024 * 256 * 2048 * n,
        limit=8,
    )


def back_kernel(begin, high_ref, low_ref, w_out_ref, w_in_ref, slope_ref, *rest):
    if begin == 0:
        (total_ref,) = rest
    else:
        before_ref, cond_ref, gain_ref, out_ref, total_ref = rest
    for step in range(begin, begin + STEPS // 2):
        columns = slice(step * CHUNK, (step + 1) * CHUNK)
        w_out = w_out_ref[columns, :]
        back = lax.dot_general(high_ref[...], w_out, LAST, preferred_element_type=F32)
        back += lax.dot_general(low_ref[...], w_out, LAST, preferred_element_type=F32)
        dpre = (back * slope_ref[step]).astype(BF16)
        term = lax.dot_general(dpre, w_in_ref[:, columns], LAST, preferred_element_type=F32)
        if step == 0:
            total_ref[...] = term
        elif step == begin:
            total_ref[...] = before_ref[...] + term
        else:
            total_ref[...] += term
    if begin == 0:
        return
    cond = cond_ref[...]
    scale = lax.rsqrt(jnp.mean(cond * cond, axis=-1, keepdims=True) + 1e-05)
    weighted = total_ref[...] * gain_ref[...].astype(F32)
    mean = jnp.mean(weighted * cond, axis=-1, keepdims=True)
    dcond = scale * weighted - cond * (scale * scale * scale * mean)
    total = jnp.sum(dcond.reshape(32, 16, 1024), axis=0)
    for j in range(8):
        out_ref[j] = total[:, j * 128 : j * 128 + 128]


def make_back(begin, high, low, w_out, w_in, slope, *more):
    (out,) = call(
        functools.partial(back_kernel, begin),
        "back_end" if begin else "back_begin",
        [((8, 16, 128) if begin else (512, 1024), F32)],
        (high, low, w_out, w_in, slope) + more,
        "m" * (5 + len(more)),
        "m",
        [pltpu.VMEM((512, 1024), F32)] if begin else [],
        flops=512 * 4096 * (768 * 2 + 1024),
        limit=10,
    )
    return out


def pack_kernel(*refs):
    keep, came, (mine_ref, theirs_ref, out_ref) = refs[:3], refs[3:6], refs[6:]
    for part in range(3):
        for j in range(8):
            rows = slice(j * 64, j * 64 + 64)
            out_ref[j, part * 64 : part * 64 + 64, :] = keep[part][rows, :] + came[part][rows, :]
    out_ref[:, 192:208, :] = mine_ref[...]
    out_ref[:, 208:224, :] = theirs_ref[...]


def sum_kernel(core_ref, got_ref, mine_ref, give_ref, latent_ref):
    total = got_ref[0, :192, :]
    for j in range(1, 8):
        total += got_ref[j, :192, :]
    latent_ref[...] = got_ref[:, 192:208, :].reshape(128, 128)
    give_ref[96:, :] = got_ref[:, 208:224, :].reshape(128, 128)
    low = core_ref[0] == 0
    for part in range(3):
        top = total[part * 64 : part * 64 + 32]
        bottom = total[part * 64 + 32 : part * 64 + 64]
        mine_ref[part * 32 : part * 32 + 32, :] = jnp.where(low, top, bottom)
        give_ref[part * 32 : part * 32 + 32, :] = jnp.where(low, bottom, top)


def place_kernel(core_ref, mine_ref, given_ref, latent_ref, grad_ref, out_ref):
    low = core_ref[0] == 0
    for part in range(3):
        mine = mine_ref[part * 32 : part * 32 + 32, :]
        given = given_ref[part * 32 : part * 32 + 32, :]
        grad_ref[:, part * 128 : part * 128 + 128] = jnp.where(low, mine, given)
        grad_ref[:, 384 + part * 128 : 512 + part * 128] = jnp.where(low, given, mine)
    out_ref[...] = jnp.where(low, latent_ref[...], given_ref[96:, :])


def per_device(latents, noise, noise_weight, gain, w_in, w_out, observed):
    device = lax.axis_index(AXES)
    chips = lax.dynamic_index_in_dim(jnp.asarray(chip_table()), device, 0, keepdims=False)
    core = (device % 2).reshape(1)
    gain = gain.reshape(1, 1024)

    noise, latents, chips, core = lax.optimization_barrier((noise, latents, chips, core))
    (moved,) = call(gather_kernel, "gather_in", [((8, 5, 16, 128), BF16)], (noise, latents), "mm", "m")
    moved = lax.all_to_all(moved, "member", split_axis=0, concat_axis=0, tiled=True)
    cond, slope, pred, *turned = call(
        forward_kernel,
        "forward_rows",
        [((512, 1024), F32), ((STEPS, 512, CHUNK), F32), ((512, 768), BF16)] + [((1024, 512), BF16)] * 4,
        (moved, noise_weight, gain, w_in, w_out),
        "mamaa",
        "hhmmmmm",
        [
            pltpu.VMEM((512, 1024), F32),
            pltpu.VMEM((STEPS, 512, CHUNK), F32),
            pltpu.VMEM((2, 512, CHUNK), F32),
            pltpu.VMEM((512, 768), F32),
            pltpu.SemaphoreType.DMA((STEPS,)),
            pltpu.SemaphoreType.DMA,
            pltpu.VMEM((1024, 4096), BF16),
            pltpu.VMEM((4096, 768), BF16),
            pltpu.VMEM((128, 1024), BF16),
            pltpu.SemaphoreType.DMA((2, 4)),
            pltpu.SemaphoreType.DMA((STEPS,)),
            pltpu.SemaphoreType.DMA,
        ],
        flops=2 * 512 * 4096 * (1024 + 768),
        limit=40,
    )
    theirs = [swap_core(piece) for piece in turned]
    high, low, own, other = call(
        score_kernel,
        "score_rows",
        [((512, 768), BF16)] * 4,
        (core, pred, observed),
        "smm",
        "hhmm",
        [pltpu.VMEM((32, 16, 768), F32)] * 2 + [pltpu.VMEM((512, 768), BF16)] * 2 + [pltpu.SemaphoreType.DMA((2,))],
        flops=2 * 512 * 4096 * 1024,
        limit=16,
    )
    got = swap_core(other)
    came = []
    for part in range(3):
        (send,) = make_outer((part,), 1, chips, turned, theirs, own, got)
        came.append(swap_stage(send, part, 0))
    keep = make_outer((0, 1, 2), 0, chips, turned, theirs, own, got)
    begun = make_back(0, high, low, w_out, w_in, slope)
    *came, begun = lax.optimization_barrier((*came, begun))

    send = [keep[part][1024:] + came[part][1024:] for part in range(3)]
    after = [swap_stage(send[part], part, 1) for part in range(3)]
    keep = [keep[part][:1024] + came[part][:1024] for part in range(3)]
    latent = make_back(STEPS // 2, high, low, w_out, w_in, slope, begun, cond, gain)
    *came, latent = lax.optimization_barrier((*after, latent))

    send = [keep[part][512:] + came[part][512:] for part in range(3)]
    after = [swap_stage(send[part], part, 2) for part in range(3)]
    keep = [keep[part][:512] + came[part][:512] for part in range(3)]
    beside = swap_core(latent)
    (packed,) = call(
        pack_kernel, "pack", [((8, 224, 128), F32)], (*keep, *after, latent, beside), "mmmmmmmm", "m"
    )
    got = lax.all_to_all(
        packed, AXES, split_axis=0, concat_axis=0, tiled=True, axis_index_groups=last_groups()
    )
    mine, give, latent = call(
        sum_kernel, "sum_blocks", [((96, 128), F32), ((224, 128), F32), ((128, 128), F32)], (core, got), "sm", "mmm"
    )
    given = swap_core(give)
    return tuple(
        call(
            place_kernel,
            "place_blocks",
            [((32, 768), F32), ((128, 128), F32)],
            (core, mine, given, latent),
            "smmm",
            "mm",
        )
    )


def solution(mesh):
    placed = (
        P("token", "member"),
        P("member", "token", None),
        P(),
        P(),
        P(),
        P(),
        P(("token", "member"), None),
    )
    return jax.shard_map(
        per_device,
        mesh=mesh,
        in_specs=placed,
        out_specs=(P(("member", "token"), None), P("token", "member")),
        check_vma=False,
    )
```

time: 843 us -> 114 us (0.14)
  waiting for transfers between devices: 690 us -> 22.9 us
  matrix products: 58.6 us -> 0 us
  Pallas kernels: 0 us -> 51.1 us
  blocking collectives: 43.7 us -> 13 us
  other arithmetic: 29.1 us -> 0.59 us
  starting transfers between devices: 4.22 us -> 21 us
  between operations: 14.3 us -> 0.91 us
    reduce_scatter x2 -> x0, waiting for transfers between devices: 680 us -> none  [the longest x1 660 us: per_device(): lax.psum_scatter(lax.dot_general(columns, flat_grad, (((0,), (0,)), ((),...]
    dot_general x6 -> x0, matrix products: 58.6 us -> none  [the longest x1 17.8 us: per_device(): lax.dot_general(columns, flat_grad, (((0,), (0,)), ((), ())), preferred_e...]
    pallas_call x0 -> x12, Pallas kernels: none -> 51.1 us  [call(): pl.pallas_call(body, in_specs=[pl.BlockSpec(memory_space=kinds[space]) fo...]
    reduce_sum x4 -> x0, other arithmetic: 25.5 us -> none  [the longest x1 14.1 us: score_one(): dist = jnp.sqrt(jnp.mean(diff * diff, axis=-1, keepdims=True) + 1e-06)]
    all_gather x1 -> x0, blocking collectives: 25.4 us -> none  [per_device(): whole = lax.all_gather(latents, 'member', axis=1, tiled=True)]
    ppermute x0 -> x16, waiting for transfers between devices: none -> 17 us  [the longest x9 12.2 us: swap_stage(): return lax.ppermute(values, AXES, pairs)]
    ppermute x0 -> x16, starting transfers between devices: none -> 15.1 us  [the longest x9 13.7 us: swap_stage(): return lax.ppermute(values, AXES, pairs)]
  transfers between devices with their start and end apart: 3 -> 17, of which waited for: 3 -> 8; matrix products, arithmetic and copies ran while one was open for 2% -> 1% of each run, Pallas kernels for 0% -> 25%
where the time goes in v2:
time: 114 us; the launch traced here: 113 us
  Pallas kernels  51.1 us (45%)
  waiting for transfers between devices  22.9 us (20%)
  starting transfers between devices  21 us (18%)
  blocking collectives  13 us (11%)
  local copies, waits for them, and re-layouts  3.11 us (3%)
    pallas_call x12, Pallas kernels, call(): pl.pallas_call(body, in_specs=[pl.BlockSpec(memory_space=kinds[space]) fo...  51.1 us
    ppermute x9, starting transfers between devices, swap_stage(): return lax.ppermute(values, AXES, pairs)  13.7 us
    all_to_all x1, blocking collectives, per_device(): lax.all_to_all(packed, AXES, split_axis=0, concat_axis=0, tiled=True, axi...  13 us
    ppermute x9, waiting for transfers between devices, swap_stage(): return lax.ppermute(values, AXES, pairs)  12.2 us
    all_to_all x1, starting transfers between devices, per_device(): lax.all_to_all(moved, 'member', split_axis=0, concat_axis=0, tiled=True)  5.91 us
    all_to_all x1, waiting for transfers between devices, per_device(): lax.all_to_all(moved, 'member', split_axis=0, concat_axis=0, tiled=True)  5.85 us
    ppermute x7, waiting for transfers between devices, swap_core(): return lax.ppermute(values, AXES, [(i, i ^ 1) for i in range(128)])  4.77 us
  transfers between devices with their start and end apart: 17, of which 8 were waited for; matrix products, arithmetic and copies ran while one was open for 1% of the time, Pallas kernels for 25%

profile of v2, /device:TPU:0, one launch (start us, length us, event | category | flops | bytes accessed | tf_op | source)
XLA Modules:
  0.0 112.5 jit_solution(17563330404253091057)
XLA Ops:
  0.6 0.7 constant_dynamic-slice_fusion
  1.4 0.9 copy-done.3
  2.3 0.8 copy-done.4
  3.0 0.7 gather_in.1
  3.7 5.9 %all-to-all-start = ((bf16[8,5,16,128]{3,2,1,0:T(8,128)(2,1)}), bf16[8,5,16,128]{3,2,1,0:T(8,128)(2,1)S(1)}, u32[]{:S(2)}, u32[]{:S(2)}) async-start(bf16[8,5,16,128]{3,2,1,0:T(8,128)(2,1)} %gather_in.1), calls=%async_computation | async-start | bytes 327680 | tf_op jit(solution)/shard_map/all_to_all | solution.py:380
  9.6 0.7 reshape.11.gain_ref.rest_2_
  10.3 5.8 %all-to-all-done.moved_ref = bf16[8,5,16,128]{3,2,1,0:T(8,128)(2,1)S(1)} async-done(((bf16[8,5,16,128]{3,2,1,0:T(8,128)(2,1)}), bf16[8,5,16,128]{3,2,1,0:T(8,128)(2,1)S(1)}, u32[]{:S(2)}, u32[]{:S(2)}) %all-to-all-start) | async-done | bytes 163872 | tf_op jit(solution)/shard_map/all_to_all | solution.py:380
  16.1 19.1 %forward_rows.1 = (f32[512,1024]{1,0:T(8,128)}, f32[8,512,512]{2,1,0:T(8,128)}, bf16[512,768]{1,0:T(8,128)(2,1)S(1)}, bf16[1024,512]{1,0:T(8,128)(2,1)S(1)}, bf1...) custom-call(bf16[8,5,16,128]{3,2,1,0:T(8,128)(2,1)S(1)} %all-to-all-done.moved_ref, ...), custom_call_target="tpu_custom_call" | custom-call | flops 7516192768 | bytes 15108096 | tf_op jit(solution)/shard_map/forward_rows/pallas_call | solution.py:94
  35.2 0.1 collective-permute-start.1
  35.3 0.5 collective-permute-start.2
  35.8 0.1 collective-permute-start.3
  35.9 0.4 collective-permute-start.4
  36.3 9.4 %score_rows.1 = (bf16[512,768]{1,0:T(8,128)(2,1)}, bf16[512,768]{1,0:T(8,128)(2,1)}, bf16[512,768]{1,0:T(8,128)(2,1)S(1)}, bf16[512,768]{1,0:T(8,128)(2,1)S(1)}) custom-call(s32[1]{0:T(128)} %bitcast.1.core_ref, bf16[512,768]{1,0:T(8,128)(2,1)S(1)} %get-tuple-element.35.pred_in_ref, bf16[16,768]{1,0:T(8,128)(2,1)S(1)} %copy-done.5), custom_call_target="tpu_custom_call" | custom-call | flops 4294967296 | bytes 811012 | tf_op jit(solution)/shard_map/score_rows/pallas_call | solution.py:94
  45.7 0.2 collective-permute-start
  45.9 2.2 %collective-permute-done.got_ref = bf16[512,768]{1,0:T(8,128)(2,1)S(1)} collective-permute-done((bf16[512,768]{1,0:T(8,128)(2,1)S(1)}, bf16[512,768]{1,0:T(8,128)(2,1)S(1)}, u32[]{:S(2)}, u32[]{:S(2)}) %collective-permute-start) | collective-permute-done | bytes 786464 | tf_op jit(solution)/shard_map/ppermute | solution.py:85
  48.1 0.0 collective-permute-done.1.rest_4_
  48.1 0.0 collective-permute-done.2.rest_5_
  48.1 0.0 collective-permute-done.3.rest_6_
  48.1 0.0 collective-permute-done.4.rest_7_
  48.1 0.0 slice-start.2
  48.1 0.0 slice-start.4
  48.1 1.8 %outer_send.3 = f32[2048,128]{1,0:T(8,128)S(1)} custom-call(s32[192]{0:T(256)S(1)} %bitcast.8, bf16[512,768]{1,0:T(8,128)(2,1)S(1)} %get-tuple-element.36.own_ref, bf16[512,768]{1,0:T(8,128)(2,1)S(1)} %collective-permute-done.got_ref, bf16[1024,512]{1,0:T(8,128)(2,1)S(1)} %get-tuple-element.38.rest_0_, bf16[1024,512]{1,0:T(8,128)(2,1)S(1)} %get-tuple-element.39.rest_1_, ...), custom_call_target="tpu_custom_call" | custom-call | flops 1073741824 | bytes 9962240 | tf_op jit(solution)/shard_map/outer_send/pallas_call | solution.py:94
  49.9 0.0 slice-start.3
  50.0 0.0 slice-start.5
  50.0 1.6 %collective-permute-start.5 = (f32[2048,128]{1,0:T(8,128)S(1)}, f32[2048,128]{1,0:T(8,128)S(1)}, u32[]{:S(2)}, u32[]{:S(2)}) collective-permute-start(f32[2048,128]{1,0:T(8,128)S(1)} %outer_send.3), channel_id=1, source_target_pairs={{0,2},{1,33},{2,0},{3,35},{4,6},{5,37},{6,4},{7,39},{8,10},{9,41},... | collective-permute-start | bytes 3145736 | tf_op jit(solution)/shard_map/ppermute | solution.py:81
  51.5 1.8 %outer_send.4 = f32[2048,128]{1,0:T(8,128)S(1)} custom-call(s32[192]{0:T(256)S(1)} %bitcast.9, bf16[512,768]{1,0:T(8,128)(2,1)S(1)} %get-tuple-element.36.own_ref, bf16[512,768]{1,0:T(8,128)(2,1)S(1)} %collective-permute-done.got_ref, bf16[1024,512]{1,0:T(8,128)(2,1)S(1)} %get-tuple-element.38.rest_0_, bf16[1024,512]{1,0:T(8,128)(2,1)S(1)} %get-tuple-element.39.rest_1_, ...), custom_call_target="tpu_custom_call" | custom-call | flops 1073741824 | bytes 9962240 | tf_op jit(solution)/shard_map/outer_send/pallas_call | solution.py:94
  53.3 0.0 slice-start.1
  53.4 2.2 %collective-permute-start.6 = (f32[2048,128]{1,0:T(8,128)S(1)}, f32[2048,128]{1,0:T(8,128)S(1)}, u32[]{:S(2)}, u32[]{:S(2)}) collective-permute-start(f32[2048,128]{1,0:T(8,128)S(1)} %outer_send.4), channel_id=1, source_target_pairs={{0,6},{1,97},{2,4},{3,99},{4,2},{5,101},{6,0},{7,103},{8,14},{9,10... | collective-permute-start | bytes 3145736 | tf_op jit(solution)/shard_map/ppermute | solution.py:81
  55.6 1.8 %outer_send.5 = f32[2048,128]{1,0:T(8,128)S(1)} custom-call(s32[192]{0:T(256)S(1)} %bitcast.10, bf16[512,768]{1,0:T(8,128)(2,1)S(1)} %get-tuple-element.36.own_ref, bf16[512,768]{1,0:T(8,128)(2,1)S(1)} %collective-permute-done.got_ref, bf16[1024,512]{1,0:T(8,128)(2,1)S(1)} %get-tuple-element.38.rest_0_, bf16[1024,512]{1,0:T(8,128)(2,1)S(1)} %get-tuple-element.39.rest_1_, ...), custom_call_target="tpu_custom_call" | custom-call | flops 1073741824 | bytes 9962240 | tf_op jit(solution)/shard_map/outer_send/pallas_call | solution.py:94
  57.4 3.3 %collective-permute-start.7 = (f32[2048,128]{1,0:T(8,128)S(1)}, f32[2048,128]{1,0:T(8,128)S(1)}, u32[]{:S(2)}, u32[]{:S(2)}) collective-permute-start(f32[2048,128]{1,0:T(8,128)S(1)} %outer_send.5), channel_id=1, source_target_pairs={{0,24},{1,17},{2,26},{3,19},{4,28},{5,21},{6,30},{7,23},{8,16},{9,... | collective-permute-start | bytes 3145736 | tf_op jit(solution)/shard_map/ppermute | solution.py:81
  60.6 0.0 slice-done.2
  60.6 0.0 slice-done
  60.7 0.0 slice-done.1
  60.7 5.7 %back_begin.1.rest_0_ = f32[512,1024]{1,0:T(8,128)S(1)} custom-call(bf16[512,768]{1,0:T(8,128)(2,1)S(1)} %copy-done, bf16[512,768]{1,0:T(8,128)(2,1)S(1)} %copy-done.1, bf16[4096,768]{1,0:T(8,128)(2,1)S(1)} %bitcast.7, bf16[1024,4096]{1,0:T(8,128)(2,1)S(1)} %bitcast.3, f32[8,512,512]{2,1,0:T(8,128)S(1)} %bitcast.5), custom_call_target="tpu_custom_call" | custom-call | flops 5368709120 | bytes 24641536 | tf_op jit(solution)/shard_map/back_begin/pallas_call | solution.py:94
  66.4 4.0 %outer_keep.1 = (f32[2048,128]{1,0:T(8,128)S(1)}, f32[2048,128]{1,0:T(8,128)S(1)}, f32[2048,128]{1,0:T(8,128)S(1)}) custom-call(s32[192]{0:T(256)S(1)} %bitcast.11, bf16[512,768]{1,0:T(8,128)(2,1)S(1)} %get-tuple-element.36.own_ref, bf16[512,768]{1,0:T(8,128)(2,1)S(1)} %collective-permute-done.got_ref, bf16[1024,512]{1,0:T(8,128)(2,1)S(1)} %get-tuple-element.38.rest_0_, ...), custom_call_target="tpu_custom_call" | custom-call | flops 3221225472 | bytes 9962240 | tf_op jit(solution)/shard_map/outer_keep/pallas_call | solution.py:94
  70.4 0.0 collective-permute-done.5
  70.4 0.0 collective-permute-done.6
  70.4 3.1 %collective-permute-done.7 = f32[2048,128]{1,0:T(8,128)S(1)} collective-permute-done((f32[2048,128]{1,0:T(8,128)S(1)}, f32[2048,128]{1,0:T(8,128)S(1)}, u32[]{:S(2)}, u32[]{:S(2)}) %collective-permute-start.7) | collective-permute-done | bytes 1048608 | tf_op jit(solution)/shard_map/ppermute | solution.py:81
  73.4 0.2 slice_add_fusion
  73.6 0.7 collective-permute-start.10
  74.3 0.1 slice_add_fusion.1
  74.4 3.3 %collective-permute-start.9 = (f32[1024,128]{1,0:T(8,128)S(1)}, f32[1024,128]{1,0:T(8,128)S(1)}, u32[]{:S(2)}, u32[]{:S(2)}) collective-permute-start(f32[1024,128]{1,0:T(8,128)S(1)} %get-tuple-element.63), channel_id=1, source_target_pairs={{0,24},{1,17},{2,26},{3,19},{4,28},{5,21},{6,30},{7,23},{8,16},{9,... | collective-permute-start | bytes 1572872 | tf_op jit(solution)/shard_map/ppermute | solution.py:81
  77.7 0.1 slice_add_fusion.4
  77.8 0.9 collective-permute-start.8
  78.7 6.1 %back_end.1.refs_6_ = f32[8,16,128]{2,1,0:T(8,128)S(1)} custom-call(bf16[512,768]{1,0:T(8,128)(2,1)S(1)} %copy-done, bf16[512,768]{1,0:T(8,128)(2,1)S(1)} %copy-done.1, bf16[4096,768]{1,0:T(8,128)(2,1)S(1)} %bitcast.7, bf16[1024,4096]{1,0:T(8,128)(2,1)S(1)} %bitcast.3, f32[8,512,512]{2,1,0:T(8,128)S(1)} %bitcast.5, f32[512,1024]{1,0:T(8,128)S(1)} %back_begin.1.rest_0_, ...), custom_call_target="tpu_custom_call" | custom-call | flops 5368709120 | bytes 28837888 | tf_op jit(solution)/shard_map/back_end/pallas_call | solution.py:94
  84.8 0.0 collective-permute-done.10
  84.8 0.0 collective-permute-done.9
  84.9 3.6 %collective-permute-done.8 = f32[1024,128]{1,0:T(8,128)S(1)} collective-permute-done((f32[1024,128]{1,0:T(8,128)S(1)}, f32[1024,128]{1,0:T(8,128)S(1)}, u32[]{:S(2)}, u32[]{:S(2)}) %collective-permute-start.8) | collective-permute-done | bytes 524320 | tf_op jit(solution)/shard_map/ppermute | solution.py:81
  88.5 0.1 slice_add_fusion.6
  88.5 0.7 collective-permute-start.13
  89.2 0.1 slice_add_fusion.7
  89.3 0.2 collective-permute-start.12
  89.5 0.1 slice_add_fusion.8
  89.6 0.9 collective-permute-start.11
  90.5 0.0 collective-permute-start.14
  90.5 1.3 %collective-permute-done.14.refs_7_ = f32[8,16,128]{2,1,0:T(8,128)S(1)} collective-permute-done((f32[8,16,128]{2,1,0:T(8,128)S(1)}, f32[8,16,128]{2,1,0:T(8,128)S(1)}, u32[]{:S(2)}, u32[]{:S(2)}) %collective-permute-start.14) | collective-permute-done | bytes 65568 | tf_op jit(solution)/shard_map/ppermute | solution.py:85
  91.8 4.4 %collective-permute-done.13.refs_5_ = f32[512,128]{1,0:T(8,128)S(1)} collective-permute-done((f32[512,128]{1,0:T(8,128)S(1)}, f32[512,128]{1,0:T(8,128)S(1)}, u32[]{:S(2)}, u32[]{:S(2)}) %collective-permute-start.13) | collective-permute-done | bytes 262176 | tf_op jit(solution)/shard_map/ppermute | solution.py:81
  96.2 0.0 collective-permute-done.12.refs_4_
  96.2 1.1 collective-permute-done.11.refs_3_
  97.3 0.1 pack.1
  97.4 13.0 %all_to_all.10.got_ref = f32[8,224,128]{2,1,0:T(8,128)S(1)} all-to-all(f32[8,224,128]{2,1,0:T(8,128)S(1)} %pack.1), channel_id=1, replica_groups={{0,16,32,48,64,80,96,112},{8,24,40,56,72,88,104,120},{2,18,34,50,66,82,..., dimensions={0} | all-to-all | bytes 1835008 | tf_op jit(solution)/shard_map/all_to_all | solution.py:439
  110.4 0.1 collective-permute-start.15
  110.5 1.3 %collective-permute-done.15.given_ref = f32[224,128]{1,0:T(8,128)S(1)} collective-permute-done((f32[224,128]{1,0:T(8,128)S(1)}, f32[224,128]{1,0:T(8,128)S(1)}, u32[]{:S(2)}, u32[]{:S(2)}) %collective-permute-start.15) | collective-permute-done | bytes 114720 | tf_op jit(solution)/shard_map/ppermute | solution.py:85
  111.9 0.7 place_blocks.1
  (18 shorter events, 0.1 us)
Async XLA Ops:
  1.4 0.9 copy-start.3
  2.3 0.8 copy-start.4
  3.7 12.4 %all-to-all-start = ((bf16[8,5,16,128]{3,2,1,0:T(8,128)(2,1)}), bf16[8,5,16,128]{3,2,1,0:T(8,128)(2,1)S(1)}, u32[]{:S(2)}, u32[]{:S(2)}) async-start(bf16[8,5,16,128]{3,2,1,0:T(8,128)(2,1)} %gather_in.1), calls=%async_computation | async-start | bytes 327680 | tf_op jit(solution)/shard_map/all_to_all | solution.py:380
  10.3 26.1 %copy-start.5 = (bf16[16,768]{1,0:T(8,128)(2,1)S(1)}, bf16[16,768]{1,0:T(8,128)(2,1)}, u32[]{:S(2)}) copy-start(bf16[16,768]{1,0:T(8,128)(2,1)} %target_ref.1) | copy-start | bytes 73732
  35.2 12.8 %collective-permute-start.1 = (bf16[1024,512]{1,0:T(8,128)(2,1)S(1)}, bf16[1024,512]{1,0:T(8,128)(2,1)S(1)}, u32[]{:S(2)}, u32[]{:S(2)}) collective-permute-start(bf16[1024,512]{1,0:T(8,128)(2,1)S(1)} %get-tuple-element.38.rest_0_), channel_id=1, source_target_pairs={{0,1},{1,0},{2,3},{3,2},{4,5},{5,4},{6,7},{7,6},{8,9},{9,8},{10,11... | collective-permute-start | bytes 3145736 | tf_op jit(solution)/shard_map/ppermute | solution.py:85
  35.3 12.8 %collective-permute-start.2 = (bf16[1024,512]{1,0:T(8,128)(2,1)S(1)}, bf16[1024,512]{1,0:T(8,128)(2,1)S(1)}, u32[]{:S(2)}, u32[]{:S(2)}) collective-permute-start(bf16[1024,512]{1,0:T(8,128)(2,1)S(1)} %get-tuple-element.39.rest_1_), channel_id=1, source_target_pairs={{0,1},{1,0},{2,3},{3,2},{4,5},{5,4},{6,7},{7,6},{8,9},{9,8},{10,11... | collective-permute-start | bytes 3145736 | tf_op jit(solution)/shard_map/ppermute | solution.py:85
  35.8 12.3 %collective-permute-start.3 = (bf16[1024,512]{1,0:T(8,128)(2,1)S(1)}, bf16[1024,512]{1,0:T(8,128)(2,1)S(1)}, u32[]{:S(2)}, u32[]{:S(2)}) collective-permute-start(bf16[1024,512]{1,0:T(8,128)(2,1)S(1)} %get-tuple-element.40.rest_2_), channel_id=1, source_target_pairs={{0,1},{1,0},{2,3},{3,2},{4,5},{5,4},{6,7},{7,6},{8,9},{9,8},{10,11... | collective-permute-start | bytes 3145736 | tf_op jit(solution)/shard_map/ppermute | solution.py:85
  35.9 12.2 %collective-permute-start.4 = (bf16[1024,512]{1,0:T(8,128)(2,1)S(1)}, bf16[1024,512]{1,0:T(8,128)(2,1)S(1)}, u32[]{:S(2)}, u32[]{:S(2)}) collective-permute-start(bf16[1024,512]{1,0:T(8,128)(2,1)S(1)} %get-tuple-element.41.rest_3_), channel_id=1, source_target_pairs={{0,1},{1,0},{2,3},{3,2},{4,5},{5,4},{6,7},{7,6},{8,9},{9,8},{10,11... | collective-permute-start | bytes 3145736 | tf_op jit(solution)/shard_map/ppermute | solution.py:85
  45.7 2.4 %collective-permute-start = (bf16[512,768]{1,0:T(8,128)(2,1)S(1)}, bf16[512,768]{1,0:T(8,128)(2,1)S(1)}, u32[]{:S(2)}, u32[]{:S(2)}) collective-permute-start(bf16[512,768]{1,0:T(8,128)(2,1)S(1)} %get-tuple-element.37), channel_id=1, source_target_pairs={{0,1},{1,0},{2,3},{3,2},{4,5},{5,4},{6,7},{7,6},{8,9},{9,8},{10,11... | collective-permute-start | bytes 2359304 | tf_op jit(solution)/shard_map/ppermute | solution.py:85
  48.1 12.5 %slice-start.2 = ((s8[8388608]{0:T(1024)(128)(4,1)}), s8[4194304]{0:T(1024)(128)(4,1)S(1)}, s32[]{:S(2)}) async-start(s8[8388608]{0:T(1024)(128)(4,1)} %bitcast.4), calls=%async_computation.4 | async-start | bytes 8388608
  48.1 12.5 %slice-start.4 = ((s8[6291456]{0:T(1024)(128)(4,1)}), s8[4194304]{0:T(1024)(128)(4,1)S(1)}, s32[]{:S(2)}) async-start(s8[6291456]{0:T(1024)(128)(4,1)} %bitcast.6), calls=%async_computation.6 | async-start | bytes 8388608
  49.9 10.7 %slice-start.3 = ((s8[8388608]{0:T(1024)(128)(4,1)}), s8[4194304]{0:T(1024)(128)(4,1)S(1)}, s32[]{:S(2)}) async-start(s8[8388608]{0:T(1024)(128)(4,1)} %bitcast.4), calls=%async_computation.5 | async-start | bytes 8388608
  50.0 10.7 %slice-start.5 = ((s8[6291456]{0:T(1024)(128)(4,1)}), s8[2097152]{0:T(1024)(128)(4,1)S(1)}, s32[]{:S(2)}) async-start(s8[6291456]{0:T(1024)(128)(4,1)} %bitcast.6), calls=%async_computation.7 | async-start | bytes 4194304
  50.0 20.4 %collective-permute-start.5 = (f32[2048,128]{1,0:T(8,128)S(1)}, f32[2048,128]{1,0:T(8,128)S(1)}, u32[]{:S(2)}, u32[]{:S(2)}) collective-permute-start(f32[2048,128]{1,0:T(8,128)S(1)} %outer_send.3), channel_id=1, source_target_pairs={{0,2},{1,33},{2,0},{3,35},{4,6},{5,37},{6,4},{7,39},{8,10},{9,41},... | collective-permute-start | bytes 3145736 | tf_op jit(solution)/shard_map/ppermute | solution.py:81
  51.5 9.1 %slice-start = ((s8[8388608]{0:T(1024)(128)(4,1)}), s8[4194304]{0:T(1024)(128)(4,1)S(1)}, s32[]{:S(2)}) async-start(s8[8388608]{0:T(1024)(128)(4,1)} %bitcast.2), calls=%async_computation.2 | async-start | bytes 8388608
  53.3 7.3 %slice-start.1 = ((s8[8388608]{0:T(1024)(128)(4,1)}), s8[4194304]{0:T(1024)(128)(4,1)S(1)}, s32[]{:S(2)}) async-start(s8[8388608]{0:T(1024)(128)(4,1)} %bitcast.2), calls=%async_computation.3 | async-start | bytes 8388608
  53.4 7.3 %copy-start = (bf16[512,768]{1,0:T(8,128)(2,1)S(1)}, bf16[512,768]{1,0:T(8,128)(2,1)}, u32[]{:S(2)}) copy-start(bf16[512,768]{1,0:T(8,128)(2,1)} %get-tuple-element.43.high_ref) | copy-start | bytes 2359300
  53.4 7.3 %copy-start.1 = (bf16[512,768]{1,0:T(8,128)(2,1)S(1)}, bf16[512,768]{1,0:T(8,128)(2,1)}, u32[]{:S(2)}) copy-start(bf16[512,768]{1,0:T(8,128)(2,1)} %get-tuple-element.44.low_ref) | copy-start | bytes 2359300
  53.4 17.0 %collective-permute-start.6 = (f32[2048,128]{1,0:T(8,128)S(1)}, f32[2048,128]{1,0:T(8,128)S(1)}, u32[]{:S(2)}, u32[]{:S(2)}) collective-permute-start(f32[2048,128]{1,0:T(8,128)S(1)} %outer_send.4), channel_id=1, source_target_pairs={{0,6},{1,97},{2,4},{3,99},{4,2},{5,101},{6,0},{7,103},{8,14},{9,10... | collective-permute-start | bytes 3145736 | tf_op jit(solution)/shard_map/ppermute | solution.py:81
  57.4 16.1 %collective-permute-start.7 = (f32[2048,128]{1,0:T(8,128)S(1)}, f32[2048,128]{1,0:T(8,128)S(1)}, u32[]{:S(2)}, u32[]{:S(2)}) collective-permute-start(f32[2048,128]{1,0:T(8,128)S(1)} %outer_send.5), channel_id=1, source_target_pairs={{0,24},{1,17},{2,26},{3,19},{4,28},{5,21},{6,30},{7,23},{8,16},{9,... | collective-permute-start | bytes 3145736 | tf_op jit(solution)/shard_map/ppermute | solution.py:81
  70.4 8.4 %copy-start.2 = (f32[512,1024]{1,0:T(8,128)S(1)}, f32[512,1024]{1,0:T(8,128)}, u32[]{:S(2)}) copy-start(f32[512,1024]{1,0:T(8,128)} %get-tuple-element.52.rest_1_) | copy-start | bytes 6291460
  73.6 11.2 %collective-permute-start.10 = (f32[1024,128]{1,0:T(8,128)S(1)}, f32[1024,128]{1,0:T(8,128)S(1)}, u32[]{:S(2)}, u32[]{:S(2)}) collective-permute-start(f32[1024,128]{1,0:T(8,128)S(1)} %get-tuple-element.61), channel_id=1, source_target_pairs={{0,2},{1,33},{2,0},{3,35},{4,6},{5,37},{6,4},{7,39},{8,10},{9,41},... | collective-permute-start | bytes 1572872 | tf_op jit(solution)/shard_map/ppermute | solution.py:81
  74.4 10.5 %collective-permute-start.9 = (f32[1024,128]{1,0:T(8,128)S(1)}, f32[1024,128]{1,0:T(8,128)S(1)}, u32[]{:S(2)}, u32[]{:S(2)}) collective-permute-start(f32[1024,128]{1,0:T(8,128)S(1)} %get-tuple-element.63), channel_id=1, source_target_pairs={{0,24},{1,17},{2,26},{3,19},{4,28},{5,21},{6,30},{7,23},{8,16},{9,... | collective-permute-start | bytes 1572872 | tf_op jit(solution)/shard_map/ppermute | solution.py:81
  77.8 10.7 %collective-permute-start.8 = (f32[1024,128]{1,0:T(8,128)S(1)}, f32[1024,128]{1,0:T(8,128)S(1)}, u32[]{:S(2)}, u32[]{:S(2)}) collective-permute-start(f32[1024,128]{1,0:T(8,128)S(1)} %get-tuple-element.64), channel_id=1, source_target_pairs={{0,6},{1,97},{2,4},{3,99},{4,2},{5,101},{6,0},{7,103},{8,14},{9,10... | collective-permute-start | bytes 1572872 | tf_op jit(solution)/shard_map/ppermute | solution.py:81
  88.5 7.7 %collective-permute-start.13 = (f32[512,128]{1,0:T(8,128)S(1)}, f32[512,128]{1,0:T(8,128)S(1)}, u32[]{:S(2)}, u32[]{:S(2)}) collective-permute-start(f32[512,128]{1,0:T(8,128)S(1)} %get-tuple-element.66), channel_id=1, source_target_pairs={{0,6},{1,97},{2,4},{3,99},{4,2},{5,101},{6,0},{7,103},{8,14},{9,10... | collective-permute-start | bytes 786440 | tf_op jit(solution)/shard_map/ppermute | solution.py:81
  89.3 6.9 %collective-permute-start.12 = (f32[512,128]{1,0:T(8,128)S(1)}, f32[512,128]{1,0:T(8,128)S(1)}, u32[]{:S(2)}, u32[]{:S(2)}) collective-permute-start(f32[512,128]{1,0:T(8,128)S(1)} %get-tuple-element.68), channel_id=1, source_target_pairs={{0,2},{1,33},{2,0},{3,35},{4,6},{5,37},{6,4},{7,39},{8,10},{9,41},... | collective-permute-start | bytes 786440 | tf_op jit(solution)/shard_map/ppermute | solution.py:81
  89.6 7.7 %collective-permute-start.11 = (f32[512,128]{1,0:T(8,128)S(1)}, f32[512,128]{1,0:T(8,128)S(1)}, u32[]{:S(2)}, u32[]{:S(2)}) collective-permute-start(f32[512,128]{1,0:T(8,128)S(1)} %get-tuple-element.70), channel_id=1, source_target_pairs={{0,24},{1,17},{2,26},{3,19},{4,28},{5,21},{6,30},{7,23},{8,16},{9,... | collective-permute-start | bytes 786440 | tf_op jit(solution)/shard_map/ppermute | solution.py:81
  90.5 1.3 %collective-permute-start.14 = (f32[8,16,128]{2,1,0:T(8,128)S(1)}, f32[8,16,128]{2,1,0:T(8,128)S(1)}, u32[]{:S(2)}, u32[]{:S(2)}) collective-permute-start(f32[8,16,128]{2,1,0:T(8,128)S(1)} %back_end.1.refs_6_), channel_id=1, source_target_pairs={{0,1},{1,0},{2,3},{3,2},{4,5},{5,4},{6,7},{7,6},{8,9},{9,8},{10,11... | collective-permute-start | bytes 196616 | tf_op jit(solution)/shard_map/ppermute | solution.py:85
  110.4 1.4 %collective-permute-start.15 = (f32[224,128]{1,0:T(8,128)S(1)}, f32[224,128]{1,0:T(8,128)S(1)}, u32[]{:S(2)}, u32[]{:S(2)}) collective-permute-start(f32[224,128]{1,0:T(8,128)S(1)} %get-tuple-element.58), channel_id=1, source_target_pairs={{0,1},{1,0},{2,3},{3,2},{4,5},{5,4},{6,7},{7,6},{8,9},{9,8},{10,11... | collective-permute-start | bytes 344072 | tf_op jit(solution)/shard_map/ppermute | solution.py:85

commit v3 on v2

--- a/solution.py
+++ b/solution.py
@@ -27,16 +27,6 @@
     return (place["y"] * 2 + place["z"] % 2) * 16 + (place["z"] // 2) * 8 + place["x"] * 2 + core
 
 
-def chip_bits(chip):
-    place, _ = coords(2 * chip)
-    bits = {}
-    for axis in "xyz":
-        value = place[axis]
-        bits[axis + "0"] = (value & 1) ^ (value >> 1)
-        bits[axis + "1"] = value >> 1
-    return bits
-
-
 def order_of(core, part):
     return FIRST[core][part:] + FIRST[core][:part]
 
@@ -56,18 +46,20 @@
     return [groups[name] for name in sorted(groups)]
 
 
-def chip_table():
-    table = np.zeros((128, 3, 64), np.int32)
-    bits = [chip_bits(chip) for chip in range(64)]
-    for device in range(128):
-        mine, core = bits[device // 2], device % 2
-        for part in range(3):
-            for chip in range(64):
-                place = 0
-                for dim in order_of(core, part):
-                    place = 2 * place + (mine[dim] ^ bits[chip][dim])
-                table[device, part, 8 * place + group_place(2 * chip + core)[1]] = chip
-    return table.reshape(128, 192)
+def shift_of(core, part, group):
+    bits = {dim: group >> (2 - at) & 1 for at, dim in enumerate(order_of(core, part))}
+    if core == 0:
+        return bits["z1"] * 4 + bits["x1"] * 2 + (bits["x0"] ^ bits["x1"])
+    return (bits["y1"] * 2 + (bits["y0"] ^ bits["y1"])) * 16 + bits["z0"] * 8
+
+
+def chip_at(device, part, place):
+    group, at = divmod(place, 8)
+    chip = device // 2
+    low = at * 8 + ((chip & 7) ^ shift_of(0, part, group))
+    lean = (chip >> 3 ^ chip >> 2) & 1
+    line = ((chip & 48) + lean * 8) ^ (shift_of(1, part, group) ^ (at >> 2) * 8)
+    return jnp.where(device % 2 == 0, low, line + at)
 
 
 def partner(index, dim):
@@ -108,7 +100,15 @@
     )(*placed)
 
 
-def gather_kernel(noise_ref, latents_ref, out_ref):
+def gather_kernel(noise_hbm, latents_hbm, out_ref, noise_ref, latents_ref, sems):
+    copies = [
+        pltpu.make_async_copy(noise_hbm, noise_ref, sems.at[0]),
+        pltpu.make_async_copy(latents_hbm, latents_ref, sems.at[1]),
+    ]
+    for copy in copies:
+        copy.start()
+    for copy in copies:
+        copy.wait()
     for j in range(8):
         rows = slice(j * 16, j * 16 + 16)
         for i in range(4):
@@ -127,28 +127,18 @@
     def put(step):
         return pltpu.make_async_copy(slope_ref.at[step], slope_hbm.at[step], out_sems.at[step])
 
-    def fetch_in(half):
-        return [
-            pltpu.make_async_copy(
-                w_in_hbm.at[i * 256 : i * 256 + 256, half * 2048 : half * 2048 + 2048],
-                w_in_ref.at[i * 256 : i * 256 + 256, half * 2048 : half * 2048 + 2048],
-                in_sems.at[half, i],
-            )
-            for i in range(4)
-        ]
+    def fetch_in(i):
+        rows = slice(i * 128, i * 128 + 128)
+        return pltpu.make_async_copy(w_in_hbm.at[rows, :], w_in_ref.at[rows, :], in_sems.at[i])
 
     def fetch_out(step):
         return pltpu.make_async_copy(w_out_hbm.at[columns(step), :], w_out_ref.at[columns(step), :], mid_sems.at[step])
 
     fetch_nw = pltpu.make_async_copy(nw_hbm, nw_ref, nw_sem)
     fetch_nw.start()
-    for copy in fetch_in(0):
-        copy.start()
-    for step in range(STEPS // 2):
-        fetch_out(step).start()
-    for copy in fetch_in(1):
-        copy.start()
-    for step in range(STEPS // 2, STEPS):
+    for i in range(8):
+        fetch_in(i).start()
+    for step in range(STEPS):
         fetch_out(step).start()
     moved = moved_ref[...]
     noise = moved[:, :4].reshape(512, 128)
@@ -164,11 +154,14 @@
     root = np.float32(np.sqrt(2 / np.pi))
     cubic = np.float32(np.sqrt(2 / np.pi) * 0.044715)
     for step in range(STEPS + 1):
-        if step in (0, STEPS // 2):
-            for copy in fetch_in(step // (STEPS // 2)):
-                copy.wait()
+        if step == 0:
+            for i in range(8):
+                fetch_in(i).wait()
         if step < STEPS:
             pre_ref[step % 2] = jnp.dot(normed, w_in_ref[:, columns(step)], preferred_element_type=F32)
+        if step == 1:
+            for i in range(STEPS):
+                fetch_out(i).wait()
         if step > 0:
             done = step - 1
             pre = pre_ref[done % 2]
@@ -182,7 +175,6 @@
             for i in range(4):
                 turned[i][done * 128 : done * 128 + 128, :] = flipped[:, i].reshape(128, 512)
             put(done).start()
-            fetch_out(done).wait()
             term = jnp.dot(hidden, w_out_ref[columns(done), :], preferred_element_type=F32)
             if done == 0:
                 total_ref[...] = term
@@ -199,29 +191,16 @@
     pred_ref[...] = pred_in_ref[...].astype(F32).reshape(32, 16, 768)
     grad_ref[...] = jnp.zeros_like(grad_ref)
 
-    def pair(own, other, total):
-        diff = own - pred_ref[other]
-        inverse = lax.rsqrt(jnp.mean(diff * diff, axis=-1, keepdims=True) + 1e-06)
-        push = diff * inverse
-        grad_ref[other] -= push
-        return total + push
-
-    def ring(member, carry):
+    for member in range(32):
         own = pred_ref[member]
         total = jnp.zeros((16, 768), F32)
-        for offset in range(1, 16):
-            total = pair(own, lax.rem(member + offset, 32), total)
+        for offset in range(1, 17 if member < 16 else 16):
+            other = (member + offset) % 32
+            diff = own - pred_ref[other]
+            push = diff * lax.rsqrt(jnp.mean(diff * diff, axis=-1, keepdims=True) + 1e-06)
+            grad_ref[other] -= push
+            total = total + push
         grad_ref[member] += total
-        return carry
-
-    def opposite(step, carry):
-        for i in range(4):
-            member = step * 4 + i
-            grad_ref[member] += pair(pred_ref[member], member + 16, jnp.zeros((16, 768), F32))
-        return carry
-
-    lax.fori_loop(0, 32, ring, 0)
-    lax.fori_loop(0, 4, opposite, 0)
     err = pred_ref[...] - target_ref[...].astype(F32)[None]
     inverse = lax.rsqrt(jnp.mean(err * err, axis=-1, keepdims=True) + 1e-06)
     grad = (err * inverse - grad_ref[...] * (1.0 / 32)).reshape(512, 768)
@@ -256,7 +235,7 @@
         copy.wait()
 
 
-def outer_kernel(parts, side, chips_ref, own_ref, got_ref, *rest):
+def outer_kernel(parts, side, device_ref, own_ref, got_ref, *rest):
     mine, theirs, rest = rest[:4], rest[4:8], rest[8:]
     outs, (a_ref, b_ref) = rest[: len(parts)], rest[len(parts) :]
     for slot, part in enumerate(parts):
@@ -264,7 +243,7 @@
         for quarter in range(4):
             at = slice(quarter * 512, quarter * 512 + 512)
             for block in range(8):
-                chip = chips_ref[part * 64 + side * 32 + quarter * 8 + block]
+                chip = chip_at(device_ref[0], part, side * 32 + quarter * 8 + block)
                 rows = pl.ds(pl.multiple_of(chip * 16, 16), 16)
                 for i in range(4):
                     first = quarter * 512 + block * 64 + i * 16
@@ -275,13 +254,13 @@
             outs[slot][at, :] = both[:, :128] + both[:, 128:]
 
 
-def make_outer(parts, side, chips, mine, theirs, own, got):
+def make_outer(parts, side, device, mine, theirs, own, got):
     n = len(parts)
     return call(
         functools.partial(outer_kernel, parts, side),
         "outer_send" if side else "outer_keep",
         [((2048, 128), F32)] * n,
-        (chips, own, got, *mine, *theirs),
+        (device, own, got, *mine, *theirs),
         "smm" + "m" * 8,
         "m" * n,
         [pltpu.VMEM((2048, 512), BF16)] * 2,
@@ -371,12 +350,12 @@
 
 def per_device(latents, noise, noise_weight, gain, w_in, w_out, observed):
     device = lax.axis_index(AXES)
-    chips = lax.dynamic_index_in_dim(jnp.asarray(chip_table()), device, 0, keepdims=False)
     core = (device % 2).reshape(1)
+    device = device.reshape(1)
     gain = gain.reshape(1, 1024)
 
-    noise, latents, chips, core = lax.optimization_barrier((noise, latents, chips, core))
-    (moved,) = call(gather_kernel, "gather_in", [((8, 5, 16, 128), BF16)], (noise, latents), "mm", "m")
+    noise, latents, device, core = lax.optimization_barrier((noise, latents, device, core))
+    (moved,) = call(gather_kernel, "gather_in", [((8, 5, 16, 128), BF16)], (noise, latents), "aa", "m", [pltpu.VMEM((4, 128, 128), BF16), pltpu.VMEM((128, 128), BF16), pltpu.SemaphoreType.DMA((2,))])
     moved = lax.all_to_all(moved, "member", split_axis=0, concat_axis=0, tiled=True)
     cond, slope, pred, *turned = call(
         forward_kernel,
@@ -395,7 +374,7 @@
             pltpu.VMEM((1024, 4096), BF16),
             pltpu.VMEM((4096, 768), BF16),
             pltpu.VMEM((128, 1024), BF16),
-            pltpu.SemaphoreType.DMA((2, 4)),
+            pltpu.SemaphoreType.DMA((8,)),
             pltpu.SemaphoreType.DMA((STEPS,)),
             pltpu.SemaphoreType.DMA,
         ],
@@ -417,9 +396,9 @@
     got = swap_core(other)
     came = []
     for part in range(3):
-        (send,) = make_outer((part,), 1, chips, turned, theirs, own, got)
+        (send,) = make_outer((part,), 1, device, turned, theirs, own, got)
         came.append(swap_stage(send, part, 0))
-    keep = make_outer((0, 1, 2), 0, chips, turned, theirs, own, got)
+    keep = make_outer((0, 1, 2), 0, device, turned, theirs, own, got)
     begun = make_back(0, high, low, w_out, w_in, slope)
     *came, begun = lax.optimization_barrier((*came, begun))
 

time: 114 us -> 106 us (0.930)
  Pallas kernels: 51.1 us -> 45.2 us
  local copies, waits for them, and re-layouts: 3.11 us -> 0.74 us
    pallas_call x12, Pallas kernels: 51.1 us -> 45.2 us  [call(): pl.pallas_call(body, in_specs=[pl.BlockSpec(memory_space=kinds[space]) fo...]
    unnamed x24 -> x20, local copies, waits for them, and re-layouts: 1.71 us -> 0.05 us
  transfers between devices with their start and end apart: 17 -> 17, of which waited for: 8 -> 9; matrix products, arithmetic and copies ran while one was open for 1% -> 1% of each run, Pallas kernels for 25% -> 24%
where the time goes in v3:
time: 106 us; the launch traced here: 105 us
  Pallas kernels  45.2 us (43%)
  waiting for transfers between devices  23.2 us (22%)
  starting transfers between devices  21.2 us (20%)
  blocking collectives  13 us (12%)
    pallas_call x12, Pallas kernels, call(): pl.pallas_call(body, in_specs=[pl.BlockSpec(memory_space=kinds[space]) fo...  45.2 us
    ppermute x9, starting transfers between devices, swap_stage(): return lax.ppermute(values, AXES, pairs)  13.9 us
    all_to_all x1, blocking collectives, per_device(): lax.all_to_all(packed, AXES, split_axis=0, concat_axis=0, tiled=True, axi...  13 us
    ppermute x9, waiting for transfers between devices, swap_stage(): return lax.ppermute(values, AXES, pairs)  12.6 us
    all_to_all x1, starting transfers between devices, per_device(): lax.all_to_all(moved, 'member', split_axis=0, concat_axis=0, tiled=True)  5.92 us
    all_to_all x1, waiting for transfers between devices, per_device(): lax.all_to_all(moved, 'member', split_axis=0, concat_axis=0, tiled=True)  5.85 us
    ppermute x7, waiting for transfers between devices, swap_core(): return lax.ppermute(values, AXES, [(i, i ^ 1) for i in range(128)])  4.77 us
  transfers between devices with their start and end apart: 17, of which 9 were waited for; matrix products, arithmetic and copies ran while one was open for 1% of the time, Pallas kernels for 24%

profile of v3, /device:TPU:0, one launch (start us, length us, event | category | flops | bytes accessed | tf_op | source)
XLA Modules:
  0.0 104.9 jit_solution(18052393709162941827)
XLA Ops:
  0.6 1.6 %gather_in.1 = bf16[8,5,16,128]{3,2,1,0:T(8,128)(2,1)} custom-call(bf16[4,128,128]{2,1,0:T(8,128)(2,1)} %noise_hbm, bf16[128,128]{1,0:T(8,128)(2,1)} %latents_hbm), custom_call_target="tpu_custom_call" | custom-call | bytes 163840 | tf_op jit(solution)/shard_map/gather_in/pallas_call | solution.py:86
  2.2 5.9 %all-to-all-start = ((bf16[8,5,16,128]{3,2,1,0:T(8,128)(2,1)}), bf16[8,5,16,128]{3,2,1,0:T(8,128)(2,1)S(1)}, u32[]{:S(2)}, u32[]{:S(2)}) async-start(bf16[8,5,16,128]{3,2,1,0:T(8,128)(2,1)} %gather_in.1), calls=%async_computation | async-start | bytes 327680 | tf_op jit(solution)/shard_map/all_to_all | solution.py:359
  8.2 0.7 reshape.15.gain_ref.rest_2_
  8.8 5.8 %all-to-all-done.moved_ref = bf16[8,5,16,128]{3,2,1,0:T(8,128)(2,1)S(1)} async-done(((bf16[8,5,16,128]{3,2,1,0:T(8,128)(2,1)}), bf16[8,5,16,128]{3,2,1,0:T(8,128)(2,1)S(1)}, u32[]{:S(2)}, u32[]{:S(2)}) %all-to-all-start) | async-done | bytes 163872 | tf_op jit(solution)/shard_map/all_to_all | solution.py:359
  14.7 16.6 %forward_rows.1 = (f32[512,1024]{1,0:T(8,128)}, f32[8,512,512]{2,1,0:T(8,128)}, bf16[512,768]{1,0:T(8,128)(2,1)S(1)}, bf16[1024,512]{1,0:T(8,128)(2,1)S(1)}, bf1...) custom-call(bf16[8,5,16,128]{3,2,1,0:T(8,128)(2,1)S(1)} %all-to-all-done.moved_ref, ...), custom_call_target="tpu_custom_call" | custom-call | flops 7516192768 | bytes 15108096 | tf_op jit(solution)/shard_map/forward_rows/pallas_call | solution.py:86
  31.3 0.1 collective-permute-start.1
  31.4 0.5 collective-permute-start.2
  31.9 0.1 collective-permute-start.3
  32.0 0.4 collective-permute-start.4
  32.4 0.0 copy-done.3
  32.4 7.3 %score_rows.1 = (bf16[512,768]{1,0:T(8,128)(2,1)}, bf16[512,768]{1,0:T(8,128)(2,1)}, bf16[512,768]{1,0:T(8,128)(2,1)S(1)}, bf16[512,768]{1,0:T(8,128)(2,1)S(1)}) custom-call(s32[1]{0:T(128)} %bitcast.1.core_ref, bf16[512,768]{1,0:T(8,128)(2,1)S(1)} %get-tuple-element.35.pred_in_ref, bf16[16,768]{1,0:T(8,128)(2,1)S(1)} %copy-done.3), custom_call_target="tpu_custom_call" | custom-call | flops 4294967296 | bytes 811012 | tf_op jit(solution)/shard_map/score_rows/pallas_call | solution.py:86
  39.7 0.2 collective-permute-start
  39.9 2.2 %collective-permute-done.got_ref = bf16[512,768]{1,0:T(8,128)(2,1)S(1)} collective-permute-done((bf16[512,768]{1,0:T(8,128)(2,1)S(1)}, bf16[512,768]{1,0:T(8,128)(2,1)S(1)}, u32[]{:S(2)}, u32[]{:S(2)}) %collective-permute-start) | collective-permute-done | bytes 786464 | tf_op jit(solution)/shard_map/ppermute | solution.py:77
  42.1 0.0 collective-permute-done.1.rest_4_
  42.1 0.0 collective-permute-done.2.rest_5_
  42.1 0.0 collective-permute-done.3.rest_6_
  42.1 0.0 collective-permute-done.4.rest_7_
  42.1 0.0 slice-start.2
  42.1 0.0 slice-start.4
  42.1 1.3 %outer_send.3 = f32[2048,128]{1,0:T(8,128)S(1)} custom-call(s32[1]{0:T(128)} %bitcast.device_ref, bf16[512,768]{1,0:T(8,128)(2,1)S(1)} %get-tuple-element.36.own_ref, bf16[512,768]{1,0:T(8,128)(2,1)S(1)} %collective-permute-done.got_ref, bf16[1024,512]{1,0:T(8,128)(2,1)S(1)} %get-tuple-element.38.rest_0_, bf16[1024,512]{1,0:T(8,128)(2,1)S(1)} %get-tuple-element.39.rest_1_, ...), custom_call_target="tpu_custom_call" | custom-call | flops 1073741824 | bytes 9961476 | tf_op jit(solution)/shard_map/outer_send/pallas_call | solution.py:86
  43.4 0.0 slice-start.3
  43.4 0.0 slice-start.5
  43.4 1.6 %collective-permute-start.5 = (f32[2048,128]{1,0:T(8,128)S(1)}, f32[2048,128]{1,0:T(8,128)S(1)}, u32[]{:S(2)}, u32[]{:S(2)}) collective-permute-start(f32[2048,128]{1,0:T(8,128)S(1)} %outer_send.3), channel_id=1, source_target_pairs={{0,2},{1,33},{2,0},{3,35},{4,6},{5,37},{6,4},{7,39},{8,10},{9,41},... | collective-permute-start | bytes 3145736 | tf_op jit(solution)/shard_map/ppermute | solution.py:73
  45.0 1.3 %outer_send.4 = f32[2048,128]{1,0:T(8,128)S(1)} custom-call(s32[1]{0:T(128)} %bitcast.device_ref, bf16[512,768]{1,0:T(8,128)(2,1)S(1)} %get-tuple-element.36.own_ref, bf16[512,768]{1,0:T(8,128)(2,1)S(1)} %collective-permute-done.got_ref, bf16[1024,512]{1,0:T(8,128)(2,1)S(1)} %get-tuple-element.38.rest_0_, bf16[1024,512]{1,0:T(8,128)(2,1)S(1)} %get-tuple-element.39.rest_1_, ...), custom_call_target="tpu_custom_call" | custom-call | flops 1073741824 | bytes 9961476 | tf_op jit(solution)/shard_map/outer_send/pallas_call | solution.py:86
  46.3 0.0 slice-start.1
  46.3 0.0 copy-start
  46.3 0.0 copy-start.1
  46.3 2.2 %collective-permute-start.6 = (f32[2048,128]{1,0:T(8,128)S(1)}, f32[2048,128]{1,0:T(8,128)S(1)}, u32[]{:S(2)}, u32[]{:S(2)}) collective-permute-start(f32[2048,128]{1,0:T(8,128)S(1)} %outer_send.4), channel_id=1, source_target_pairs={{0,6},{1,97},{2,4},{3,99},{4,2},{5,101},{6,0},{7,103},{8,14},{9,10... | collective-permute-start | bytes 3145736 | tf_op jit(solution)/shard_map/ppermute | solution.py:73
  48.4 1.3 %outer_send.5 = f32[2048,128]{1,0:T(8,128)S(1)} custom-call(s32[1]{0:T(128)} %bitcast.device_ref, bf16[512,768]{1,0:T(8,128)(2,1)S(1)} %get-tuple-element.36.own_ref, bf16[512,768]{1,0:T(8,128)(2,1)S(1)} %collective-permute-done.got_ref, bf16[1024,512]{1,0:T(8,128)(2,1)S(1)} %get-tuple-element.38.rest_0_, bf16[1024,512]{1,0:T(8,128)(2,1)S(1)} %get-tuple-element.39.rest_1_, ...), custom_call_target="tpu_custom_call" | custom-call | flops 1073741824 | bytes 9961476 | tf_op jit(solution)/shard_map/outer_send/pallas_call | solution.py:86
  49.7 3.5 %collective-permute-start.7 = (f32[2048,128]{1,0:T(8,128)S(1)}, f32[2048,128]{1,0:T(8,128)S(1)}, u32[]{:S(2)}, u32[]{:S(2)}) collective-permute-start(f32[2048,128]{1,0:T(8,128)S(1)} %outer_send.5), channel_id=1, source_target_pairs={{0,24},{1,17},{2,26},{3,19},{4,28},{5,21},{6,30},{7,23},{8,16},{9,... | collective-permute-start | bytes 3145736 | tf_op jit(solution)/shard_map/ppermute | solution.py:73
  53.2 0.0 slice-done.2
  53.2 0.0 slice-done.4
  53.2 0.0 slice-done.3
  53.3 5.7 %back_begin.1.rest_0_ = f32[512,1024]{1,0:T(8,128)S(1)} custom-call(bf16[512,768]{1,0:T(8,128)(2,1)S(1)} %copy-done, bf16[512,768]{1,0:T(8,128)(2,1)S(1)} %copy-done.1, bf16[4096,768]{1,0:T(8,128)(2,1)S(1)} %bitcast.7, bf16[1024,4096]{1,0:T(8,128)(2,1)S(1)} %bitcast.3, f32[8,512,512]{2,1,0:T(8,128)S(1)} %bitcast.5), custom_call_target="tpu_custom_call" | custom-call | flops 5368709120 | bytes 24641536 | tf_op jit(solution)/shard_map/back_begin/pallas_call | solution.py:86
  59.0 3.4 %outer_keep.1 = (f32[2048,128]{1,0:T(8,128)S(1)}, f32[2048,128]{1,0:T(8,128)S(1)}, f32[2048,128]{1,0:T(8,128)S(1)}) custom-call(s32[1]{0:T(128)} %bitcast.device_ref, bf16[512,768]{1,0:T(8,128)(2,1)S(1)} %get-tuple-element.36.own_ref, bf16[512,768]{1,0:T(8,128)(2,1)S(1)} %collective-permute-done.got_ref, bf16[1024,512]{1,0:T(8,128)(2,1)S(1)} %get-tuple-element.38.rest_0_, ...), custom_call_target="tpu_custom_call" | custom-call | flops 3221225472 | bytes 9961476 | tf_op jit(solution)/shard_map/outer_keep/pallas_call | solution.py:86
  62.4 0.0 collective-permute-done.5
  62.4 0.0 collective-permute-done.6
  62.4 3.6 %collective-permute-done.7 = f32[2048,128]{1,0:T(8,128)S(1)} collective-permute-done((f32[2048,128]{1,0:T(8,128)S(1)}, f32[2048,128]{1,0:T(8,128)S(1)}, u32[]{:S(2)}, u32[]{:S(2)}) %collective-permute-start.7) | collective-permute-done | bytes 1048608 | tf_op jit(solution)/shard_map/ppermute | solution.py:73
  66.0 0.2 slice_add_fusion
  66.2 0.7 collective-permute-start.10
  66.9 0.1 slice_add_fusion.1
  67.0 3.3 %collective-permute-start.9 = (f32[1024,128]{1,0:T(8,128)S(1)}, f32[1024,128]{1,0:T(8,128)S(1)}, u32[]{:S(2)}, u32[]{:S(2)}) collective-permute-start(f32[1024,128]{1,0:T(8,128)S(1)} %get-tuple-element.63), channel_id=1, source_target_pairs={{0,24},{1,17},{2,26},{3,19},{4,28},{5,21},{6,30},{7,23},{8,16},{9,... | collective-permute-start | bytes 1572872 | tf_op jit(solution)/shard_map/ppermute | solution.py:73
  70.2 0.1 slice_add_fusion.4
  70.4 0.7 collective-permute-start.8
  71.1 6.1 %back_end.1.refs_6_ = f32[8,16,128]{2,1,0:T(8,128)S(1)} custom-call(bf16[512,768]{1,0:T(8,128)(2,1)S(1)} %copy-done, bf16[512,768]{1,0:T(8,128)(2,1)S(1)} %copy-done.1, bf16[4096,768]{1,0:T(8,128)(2,1)S(1)} %bitcast.7, bf16[1024,4096]{1,0:T(8,128)(2,1)S(1)} %bitcast.3, f32[8,512,512]{2,1,0:T(8,128)S(1)} %bitcast.5, f32[512,1024]{1,0:T(8,128)S(1)} %back_begin.1.rest_0_, ...), custom_call_target="tpu_custom_call" | custom-call | flops 5368709120 | bytes 28837888 | tf_op jit(solution)/shard_map/back_end/pallas_call | solution.py:86
  77.2 0.0 collective-permute-done.10
  77.2 0.3 collective-permute-done.9
  77.4 3.4 %collective-permute-done.8 = f32[1024,128]{1,0:T(8,128)S(1)} collective-permute-done((f32[1024,128]{1,0:T(8,128)S(1)}, f32[1024,128]{1,0:T(8,128)S(1)}, u32[]{:S(2)}, u32[]{:S(2)}) %collective-permute-start.8) | collective-permute-done | bytes 524320 | tf_op jit(solution)/shard_map/ppermute | solution.py:73
  80.8 0.1 slice_add_fusion.6
  80.9 0.7 collective-permute-start.13
  81.6 0.1 slice_add_fusion.7
  81.7 0.2 collective-permute-start.12
  81.9 0.1 slice_add_fusion.8
  82.0 1.1 %collective-permute-start.11 = (f32[512,128]{1,0:T(8,128)S(1)}, f32[512,128]{1,0:T(8,128)S(1)}, u32[]{:S(2)}, u32[]{:S(2)}) collective-permute-start(f32[512,128]{1,0:T(8,128)S(1)} %get-tuple-element.70), channel_id=1, source_target_pairs={{0,24},{1,17},{2,26},{3,19},{4,28},{5,21},{6,30},{7,23},{8,16},{9,... | collective-permute-start | bytes 786440 | tf_op jit(solution)/shard_map/ppermute | solution.py:73
  83.1 0.0 collective-permute-start.14
  83.1 1.3 %collective-permute-done.14.refs_7_ = f32[8,16,128]{2,1,0:T(8,128)S(1)} collective-permute-done((f32[8,16,128]{2,1,0:T(8,128)S(1)}, f32[8,16,128]{2,1,0:T(8,128)S(1)}, u32[]{:S(2)}, u32[]{:S(2)}) %collective-permute-start.14) | collective-permute-done | bytes 65568 | tf_op jit(solution)/shard_map/ppermute | solution.py:77
  84.3 4.2 %collective-permute-done.13.refs_5_ = f32[512,128]{1,0:T(8,128)S(1)} collective-permute-done((f32[512,128]{1,0:T(8,128)S(1)}, f32[512,128]{1,0:T(8,128)S(1)}, u32[]{:S(2)}, u32[]{:S(2)}) %collective-permute-start.13) | collective-permute-done | bytes 262176 | tf_op jit(solution)/shard_map/ppermute | solution.py:73
  88.5 0.0 collective-permute-done.12.refs_4_
  88.6 1.1 %collective-permute-done.11.refs_3_ = f32[512,128]{1,0:T(8,128)S(1)} collective-permute-done((f32[512,128]{1,0:T(8,128)S(1)}, f32[512,128]{1,0:T(8,128)S(1)}, u32[]{:S(2)}, u32[]{:S(2)}) %collective-permute-start.11) | collective-permute-done | bytes 262176 | tf_op jit(solution)/shard_map/ppermute | solution.py:73
  89.6 0.1 pack.1
  89.7 13.0 %all_to_all.10.got_ref = f32[8,224,128]{2,1,0:T(8,128)S(1)} all-to-all(f32[8,224,128]{2,1,0:T(8,128)S(1)} %pack.1), channel_id=1, replica_groups={{0,16,32,48,64,80,96,112},{8,24,40,56,72,88,104,120},{2,18,34,50,66,82,..., dimensions={0} | all-to-all | bytes 1835008 | tf_op jit(solution)/shard_map/all_to_all | solution.py:418
  102.8 0.1 collective-permute-start.15
  102.9 1.3 %collective-permute-done.15.given_ref = f32[224,128]{1,0:T(8,128)S(1)} collective-permute-done((f32[224,128]{1,0:T(8,128)S(1)}, f32[224,128]{1,0:T(8,128)S(1)}, u32[]{:S(2)}, u32[]{:S(2)}) %collective-permute-start.15) | collective-permute-done | bytes 114720 | tf_op jit(solution)/shard_map/ppermute | solution.py:77
  104.2 0.7 place_blocks.1
  (13 shorter events, 0.1 us)
Async XLA Ops:
  2.2 12.5 %all-to-all-start = ((bf16[8,5,16,128]{3,2,1,0:T(8,128)(2,1)}), bf16[8,5,16,128]{3,2,1,0:T(8,128)(2,1)S(1)}, u32[]{:S(2)}, u32[]{:S(2)}) async-start(bf16[8,5,16,128]{3,2,1,0:T(8,128)(2,1)} %gather_in.1), calls=%async_computation | async-start | bytes 327680 | tf_op jit(solution)/shard_map/all_to_all | solution.py:359
  8.8 23.6 %copy-start.3 = (bf16[16,768]{1,0:T(8,128)(2,1)S(1)}, bf16[16,768]{1,0:T(8,128)(2,1)}, u32[]{:S(2)}) copy-start(bf16[16,768]{1,0:T(8,128)(2,1)} %target_ref.1) | copy-start | bytes 73732
  31.3 10.8 %collective-permute-start.1 = (bf16[1024,512]{1,0:T(8,128)(2,1)S(1)}, bf16[1024,512]{1,0:T(8,128)(2,1)S(1)}, u32[]{:S(2)}, u32[]{:S(2)}) collective-permute-start(bf16[1024,512]{1,0:T(8,128)(2,1)S(1)} %get-tuple-element.38.rest_0_), channel_id=1, source_target_pairs={{0,1},{1,0},{2,3},{3,2},{4,5},{5,4},{6,7},{7,6},{8,9},{9,8},{10,11... | collective-permute-start | bytes 3145736 | tf_op jit(solution)/shard_map/ppermute | solution.py:77
  31.4 10.7 %collective-permute-start.2 = (bf16[1024,512]{1,0:T(8,128)(2,1)S(1)}, bf16[1024,512]{1,0:T(8,128)(2,1)S(1)}, u32[]{:S(2)}, u32[]{:S(2)}) collective-permute-start(bf16[1024,512]{1,0:T(8,128)(2,1)S(1)} %get-tuple-element.39.rest_1_), channel_id=1, source_target_pairs={{0,1},{1,0},{2,3},{3,2},{4,5},{5,4},{6,7},{7,6},{8,9},{9,8},{10,11... | collective-permute-start | bytes 3145736 | tf_op jit(solution)/shard_map/ppermute | solution.py:77
  31.9 10.2 %collective-permute-start.3 = (bf16[1024,512]{1,0:T(8,128)(2,1)S(1)}, bf16[1024,512]{1,0:T(8,128)(2,1)S(1)}, u32[]{:S(2)}, u32[]{:S(2)}) collective-permute-start(bf16[1024,512]{1,0:T(8,128)(2,1)S(1)} %get-tuple-element.40.rest_2_), channel_id=1, source_target_pairs={{0,1},{1,0},{2,3},{3,2},{4,5},{5,4},{6,7},{7,6},{8,9},{9,8},{10,11... | collective-permute-start | bytes 3145736 | tf_op jit(solution)/shard_map/ppermute | solution.py:77
  32.0 10.1 %collective-permute-start.4 = (bf16[1024,512]{1,0:T(8,128)(2,1)S(1)}, bf16[1024,512]{1,0:T(8,128)(2,1)S(1)}, u32[]{:S(2)}, u32[]{:S(2)}) collective-permute-start(bf16[1024,512]{1,0:T(8,128)(2,1)S(1)} %get-tuple-element.41.rest_3_), channel_id=1, source_target_pairs={{0,1},{1,0},{2,3},{3,2},{4,5},{5,4},{6,7},{7,6},{8,9},{9,8},{10,11... | collective-permute-start | bytes 3145736 | tf_op jit(solution)/shard_map/ppermute | solution.py:77
  39.7 2.4 %collective-permute-start = (bf16[512,768]{1,0:T(8,128)(2,1)S(1)}, bf16[512,768]{1,0:T(8,128)(2,1)S(1)}, u32[]{:S(2)}, u32[]{:S(2)}) collective-permute-start(bf16[512,768]{1,0:T(8,128)(2,1)S(1)} %get-tuple-element.37), channel_id=1, source_target_pairs={{0,1},{1,0},{2,3},{3,2},{4,5},{5,4},{6,7},{7,6},{8,9},{9,8},{10,11... | collective-permute-start | bytes 2359304 | tf_op jit(solution)/shard_map/ppermute | solution.py:77
  42.1 11.1 %slice-start.2 = ((s8[8388608]{0:T(1024)(128)(4,1)}), s8[4194304]{0:T(1024)(128)(4,1)S(1)}, s32[]{:S(2)}) async-start(s8[8388608]{0:T(1024)(128)(4,1)} %bitcast.4), calls=%async_computation.4 | async-start | bytes 8388608
  42.1 11.1 %slice-start.4 = ((s8[6291456]{0:T(1024)(128)(4,1)}), s8[4194304]{0:T(1024)(128)(4,1)S(1)}, s32[]{:S(2)}) async-start(s8[6291456]{0:T(1024)(128)(4,1)} %bitcast.6), calls=%async_computation.6 | async-start | bytes 8388608
  43.4 9.9 %slice-start.3 = ((s8[8388608]{0:T(1024)(128)(4,1)}), s8[4194304]{0:T(1024)(128)(4,1)S(1)}, s32[]{:S(2)}) async-start(s8[8388608]{0:T(1024)(128)(4,1)} %bitcast.4), calls=%async_computation.5 | async-start | bytes 8388608
  43.4 9.8 %slice-start.5 = ((s8[6291456]{0:T(1024)(128)(4,1)}), s8[2097152]{0:T(1024)(128)(4,1)S(1)}, s32[]{:S(2)}) async-start(s8[6291456]{0:T(1024)(128)(4,1)} %bitcast.6), calls=%async_computation.7 | async-start | bytes 4194304
  43.4 19.0 %collective-permute-start.5 = (f32[2048,128]{1,0:T(8,128)S(1)}, f32[2048,128]{1,0:T(8,128)S(1)}, u32[]{:S(2)}, u32[]{:S(2)}) collective-permute-start(f32[2048,128]{1,0:T(8,128)S(1)} %outer_send.3), channel_id=1, source_target_pairs={{0,2},{1,33},{2,0},{3,35},{4,6},{5,37},{6,4},{7,39},{8,10},{9,41},... | collective-permute-start | bytes 3145736 | tf_op jit(solution)/shard_map/ppermute | solution.py:73
  45.0 8.2 %slice-start = ((s8[8388608]{0:T(1024)(128)(4,1)}), s8[4194304]{0:T(1024)(128)(4,1)S(1)}, s32[]{:S(2)}) async-start(s8[8388608]{0:T(1024)(128)(4,1)} %bitcast.2), calls=%async_computation.2 | async-start | bytes 8388608
  46.3 7.0 %slice-start.1 = ((s8[8388608]{0:T(1024)(128)(4,1)}), s8[4194304]{0:T(1024)(128)(4,1)S(1)}, s32[]{:S(2)}) async-start(s8[8388608]{0:T(1024)(128)(4,1)} %bitcast.2), calls=%async_computation.3 | async-start | bytes 8388608
  46.3 7.0 %copy-start = (bf16[512,768]{1,0:T(8,128)(2,1)S(1)}, bf16[512,768]{1,0:T(8,128)(2,1)}, u32[]{:S(2)}) copy-start(bf16[512,768]{1,0:T(8,128)(2,1)} %get-tuple-element.43.high_ref) | copy-start | bytes 2359300
  46.3 7.0 %copy-start.1 = (bf16[512,768]{1,0:T(8,128)(2,1)S(1)}, bf16[512,768]{1,0:T(8,128)(2,1)}, u32[]{:S(2)}) copy-start(bf16[512,768]{1,0:T(8,128)(2,1)} %get-tuple-element.44.low_ref) | copy-start | bytes 2359300
  46.3 16.1 %collective-permute-start.6 = (f32[2048,128]{1,0:T(8,128)S(1)}, f32[2048,128]{1,0:T(8,128)S(1)}, u32[]{:S(2)}, u32[]{:S(2)}) collective-permute-start(f32[2048,128]{1,0:T(8,128)S(1)} %outer_send.4), channel_id=1, source_target_pairs={{0,6},{1,97},{2,4},{3,99},{4,2},{5,101},{6,0},{7,103},{8,14},{9,10... | collective-permute-start | bytes 3145736 | tf_op jit(solution)/shard_map/ppermute | solution.py:73
  49.7 16.3 %collective-permute-start.7 = (f32[2048,128]{1,0:T(8,128)S(1)}, f32[2048,128]{1,0:T(8,128)S(1)}, u32[]{:S(2)}, u32[]{:S(2)}) collective-permute-start(f32[2048,128]{1,0:T(8,128)S(1)} %outer_send.5), channel_id=1, source_target_pairs={{0,24},{1,17},{2,26},{3,19},{4,28},{5,21},{6,30},{7,23},{8,16},{9,... | collective-permute-start | bytes 3145736 | tf_op jit(solution)/shard_map/ppermute | solution.py:73
  62.4 8.7 %copy-start.2 = (f32[512,1024]{1,0:T(8,128)S(1)}, f32[512,1024]{1,0:T(8,128)}, u32[]{:S(2)}) copy-start(f32[512,1024]{1,0:T(8,128)} %get-tuple-element.52.rest_1_) | copy-start | bytes 6291460
  66.2 11.0 %collective-permute-start.10 = (f32[1024,128]{1,0:T(8,128)S(1)}, f32[1024,128]{1,0:T(8,128)S(1)}, u32[]{:S(2)}, u32[]{:S(2)}) collective-permute-start(f32[1024,128]{1,0:T(8,128)S(1)} %get-tuple-element.61), channel_id=1, source_target_pairs={{0,2},{1,33},{2,0},{3,35},{4,6},{5,37},{6,4},{7,39},{8,10},{9,41},... | collective-permute-start | bytes 1572872 | tf_op jit(solution)/shard_map/ppermute | solution.py:73
  67.0 10.5 %collective-permute-start.9 = (f32[1024,128]{1,0:T(8,128)S(1)}, f32[1024,128]{1,0:T(8,128)S(1)}, u32[]{:S(2)}, u32[]{:S(2)}) collective-permute-start(f32[1024,128]{1,0:T(8,128)S(1)} %get-tuple-element.63), channel_id=1, source_target_pairs={{0,24},{1,17},{2,26},{3,19},{4,28},{5,21},{6,30},{7,23},{8,16},{9,... | collective-permute-start | bytes 1572872 | tf_op jit(solution)/shard_map/ppermute | solution.py:73
  70.4 10.5 %collective-permute-start.8 = (f32[1024,128]{1,0:T(8,128)S(1)}, f32[1024,128]{1,0:T(8,128)S(1)}, u32[]{:S(2)}, u32[]{:S(2)}) collective-permute-start(f32[1024,128]{1,0:T(8,128)S(1)} %get-tuple-element.64), channel_id=1, source_target_pairs={{0,6},{1,97},{2,4},{3,99},{4,2},{5,101},{6,0},{7,103},{8,14},{9,10... | collective-permute-start | bytes 1572872 | tf_op jit(solution)/shard_map/ppermute | solution.py:73
  80.9 7.7 %collective-permute-start.13 = (f32[512,128]{1,0:T(8,128)S(1)}, f32[512,128]{1,0:T(8,128)S(1)}, u32[]{:S(2)}, u32[]{:S(2)}) collective-permute-start(f32[512,128]{1,0:T(8,128)S(1)} %get-tuple-element.66), channel_id=1, source_target_pairs={{0,6},{1,97},{2,4},{3,99},{4,2},{5,101},{6,0},{7,103},{8,14},{9,10... | collective-permute-start | bytes 786440 | tf_op jit(solution)/shard_map/ppermute | solution.py:73
  81.7 6.9 %collective-permute-start.12 = (f32[512,128]{1,0:T(8,128)S(1)}, f32[512,128]{1,0:T(8,128)S(1)}, u32[]{:S(2)}, u32[]{:S(2)}) collective-permute-start(f32[512,128]{1,0:T(8,128)S(1)} %get-tuple-element.68), channel_id=1, source_target_pairs={{0,2},{1,33},{2,0},{3,35},{4,6},{5,37},{6,4},{7,39},{8,10},{9,41},... | collective-permute-start | bytes 786440 | tf_op jit(solution)/shard_map/ppermute | solution.py:73
  82.0 7.7 %collective-permute-start.11 = (f32[512,128]{1,0:T(8,128)S(1)}, f32[512,128]{1,0:T(8,128)S(1)}, u32[]{:S(2)}, u32[]{:S(2)}) collective-permute-start(f32[512,128]{1,0:T(8,128)S(1)} %get-tuple-element.70), channel_id=1, source_target_pairs={{0,24},{1,17},{2,26},{3,19},{4,28},{5,21},{6,30},{7,23},{8,16},{9,... | collective-permute-start | bytes 786440 | tf_op jit(solution)/shard_map/ppermute | solution.py:73
  83.1 1.3 %collective-permute-start.14 = (f32[8,16,128]{2,1,0:T(8,128)S(1)}, f32[8,16,128]{2,1,0:T(8,128)S(1)}, u32[]{:S(2)}, u32[]{:S(2)}) collective-permute-start(f32[8,16,128]{2,1,0:T(8,128)S(1)} %back_end.1.refs_6_), channel_id=1, source_target_pairs={{0,1},{1,0},{2,3},{3,2},{4,5},{5,4},{6,7},{7,6},{8,9},{9,8},{10,11... | collective-permute-start | bytes 196616 | tf_op jit(solution)/shard_map/ppermute | solution.py:77
  102.8 1.4 %collective-permute-start.15 = (f32[224,128]{1,0:T(8,128)S(1)}, f32[224,128]{1,0:T(8,128)S(1)}, u32[]{:S(2)}, u32[]{:S(2)}) collective-permute-start(f32[224,128]{1,0:T(8,128)S(1)} %get-tuple-element.58), channel_id=1, source_target_pairs={{0,1},{1,0},{2,3},{3,2},{4,5},{5,4},{6,7},{7,6},{8,9},{9,8},{10,11... | collective-permute-start | bytes 344072 | tf_op jit(solution)/shard_map/ppermute | solution.py:77

commit v4 on v3

--- a/solution.py
+++ b/solution.py
@@ -235,10 +235,12 @@
         copy.wait()
 
 
-def outer_kernel(parts, side, device_ref, own_ref, got_ref, *rest):
-    mine, theirs, rest = rest[:4], rest[4:8], rest[8:]
-    outs, (a_ref, b_ref) = rest[: len(parts)], rest[len(parts) :]
-    for slot, part in enumerate(parts):
+def outer_kernel(side, sources, added, device_ref, *refs):
+    grads, refs = refs[:sources], refs[sources:]
+    turned, refs = [refs[4 * i : 4 * i + 4] for i in range(sources)], refs[4 * sources :]
+    before, refs = refs[: 3 * added], refs[3 * added :]
+    outs, rows_refs = refs[:3], refs[3:]
+    for part in range(3):
         fields = slice(part * 256, part * 256 + 256)
         for quarter in range(4):
             at = slice(quarter * 512, quarter * 512 + 512)
@@ -247,24 +249,27 @@
                 rows = pl.ds(pl.multiple_of(chip * 16, 16), 16)
                 for i in range(4):
                     first = quarter * 512 + block * 64 + i * 16
-                    a_ref[first : first + 16, :] = mine[i][rows, :]
-                    b_ref[first : first + 16, :] = theirs[i][rows, :]
-            both = jnp.dot(a_ref[at, :], own_ref[:, fields], preferred_element_type=F32)
-            both += jnp.dot(b_ref[at, :], got_ref[:, fields], preferred_element_type=F32)
-            outs[slot][at, :] = both[:, :128] + both[:, 128:]
-
-
-def make_outer(parts, side, device, mine, theirs, own, got):
-    n = len(parts)
+                    for source in range(sources):
+                        rows_refs[source][first : first + 16, :] = turned[source][i][rows, :]
+            both = jnp.dot(rows_refs[0][at, :], grads[0][:, fields], preferred_element_type=F32)
+            for source in range(1, sources):
+                both += jnp.dot(rows_refs[source][at, :], grads[source][:, fields], preferred_element_type=F32)
+            total = both[:, :128] + both[:, 128:]
+            outs[part][at, :] = total + before[part][at, :] if added else total
+
+
+def make_outer(name, side, device, grads, turned, before=()):
+    n = len(grads)
+    pieces = [piece for pieces in turned for piece in pieces]
     return call(
-        functools.partial(outer_kernel, parts, side),
-        "outer_send" if side else "outer_keep",
-        [((2048, 128), F32)] * n,
-        (device, own, got, *mine, *theirs),
-        "smm" + "m" * 8,
-        "m" * n,
-        [pltpu.VMEM((2048, 512), BF16)] * 2,
-        flops=2 * 1024 * 256 * 2048 * n,
+        functools.partial(outer_kernel, side, n, len(before) // 3),
+        name,
+        [((2048, 128), F32)] * 3,
+        (device, *grads, *pieces, *before),
+        "s" + "m" * (5 * n + len(before)),
+        "mmm",
+        [pltpu.VMEM((2048, 512), BF16)] * n,
+        flops=2 * 512 * n * 256 * 2048 * 3,
         limit=8,
     )
 
@@ -394,11 +399,10 @@
         limit=16,
     )
     got = swap_core(other)
-    came = []
-    for part in range(3):
-        (send,) = make_outer((part,), 1, device, turned, theirs, own, got)
-        came.append(swap_stage(send, part, 0))
-    keep = make_outer((0, 1, 2), 0, device, turned, theirs, own, got)
+    begun = make_outer("outer_own", 1, device, (own,), (turned,))
+    send = make_outer("outer_send", 1, device, (got,), (theirs,), begun)
+    came = [swap_stage(send[part], part, 0) for part in range(3)]
+    keep = make_outer("outer_keep", 0, device, (own, got), (turned, theirs))
     begun = make_back(0, high, low, w_out, w_in, slope)
     *came, begun = lax.optimization_barrier((*came, begun))
 

time: 106 us -> 104 us (0.981)
  waiting for transfers between devices: 23.2 us -> 21.3 us
    ppermute x7, waiting for transfers between devices: 4.77 us -> 2.94 us  [swap_core(): return lax.ppermute(values, AXES, [(i, i ^ 1) for i in range(128)])]
    pallas_call x12 -> x11, Pallas kernels: 45.2 us -> 45.2 us  [call(): pl.pallas_call(body, in_specs=[pl.BlockSpec(memory_space=kinds[space]) fo...]
  transfers between devices with their start and end apart: 17 -> 17, of which waited for: 9 -> 10; matrix products, arithmetic and copies ran while one was open for 1% -> 1% of each run, Pallas kernels for 24% -> 24%
where the time goes in v4:
time: 104 us; the launch traced here: 102 us
  Pallas kernels  45.2 us (43%)
  waiting for transfers between devices  21.3 us (20%)
  starting transfers between devices  20.8 us (20%)
  blocking collectives  13 us (12%)
    pallas_call x11, Pallas kernels, call(): pl.pallas_call(body, in_specs=[pl.BlockSpec(memory_space=kinds[space]) fo...  45.2 us
    ppermute x9, starting transfers between devices, swap_stage(): return lax.ppermute(values, AXES, pairs)  13.5 us
    all_to_all x1, blocking collectives, per_device(): lax.all_to_all(packed, AXES, split_axis=0, concat_axis=0, tiled=True, axi...  13 us
    ppermute x9, waiting for transfers between devices, swap_stage(): return lax.ppermute(values, AXES, pairs)  12.5 us
    all_to_all x1, starting transfers between devices, per_device(): lax.all_to_all(moved, 'member', split_axis=0, concat_axis=0, tiled=True)  5.92 us
    all_to_all x1, waiting for transfers between devices, per_device(): lax.all_to_all(moved, 'member', split_axis=0, concat_axis=0, tiled=True)  5.85 us
    ppermute x7, waiting for transfers between devices, swap_core(): return lax.ppermute(values, AXES, [(i, i ^ 1) for i in range(128)])  2.94 us
  transfers between devices with their start and end apart: 17, of which 10 were waited for; matrix products, arithmetic and copies ran while one was open for 1% of the time, Pallas kernels for 24%

profile of v4, /device:TPU:0, one launch (start us, length us, event | category | flops | bytes accessed | tf_op | source)
XLA Modules:
  0.0 102.5 jit_solution(8972675119987967981)
XLA Ops:
  0.6 1.6 %gather_in.1 = bf16[8,5,16,128]{3,2,1,0:T(8,128)(2,1)} custom-call(bf16[4,128,128]{2,1,0:T(8,128)(2,1)} %noise_hbm, bf16[128,128]{1,0:T(8,128)(2,1)} %latents_hbm), custom_call_target="tpu_custom_call" | custom-call | bytes 163840 | tf_op jit(solution)/shard_map/gather_in/pallas_call | solution.py:86
  2.3 5.9 %all-to-all-start = ((bf16[8,5,16,128]{3,2,1,0:T(8,128)(2,1)}), bf16[8,5,16,128]{3,2,1,0:T(8,128)(2,1)S(1)}, u32[]{:S(2)}, u32[]{:S(2)}) async-start(bf16[8,5,16,128]{3,2,1,0:T(8,128)(2,1)} %gather_in.1), calls=%async_computation | async-start | bytes 327680 | tf_op jit(solution)/shard_map/all_to_all | solution.py:364
  8.2 0.7 reshape.15.gain_ref.rest_2_
  8.9 5.8 %all-to-all-done.moved_ref = bf16[8,5,16,128]{3,2,1,0:T(8,128)(2,1)S(1)} async-done(((bf16[8,5,16,128]{3,2,1,0:T(8,128)(2,1)}), bf16[8,5,16,128]{3,2,1,0:T(8,128)(2,1)S(1)}, u32[]{:S(2)}, u32[]{:S(2)}) %all-to-all-start) | async-done | bytes 163872 | tf_op jit(solution)/shard_map/all_to_all | solution.py:364
  14.7 16.6 %forward_rows.1 = (f32[512,1024]{1,0:T(8,128)}, f32[8,512,512]{2,1,0:T(8,128)}, bf16[512,768]{1,0:T(8,128)(2,1)S(1)}, bf16[1024,512]{1,0:T(8,128)(2,1)S(1)}, bf1...) custom-call(bf16[8,5,16,128]{3,2,1,0:T(8,128)(2,1)S(1)} %all-to-all-done.moved_ref, ...), custom_call_target="tpu_custom_call" | custom-call | flops 7516192768 | bytes 15108096 | tf_op jit(solution)/shard_map/forward_rows/pallas_call | solution.py:86
  31.3 0.0 copy-start.3
  31.3 0.1 collective-permute-start.1
  31.4 0.5 collective-permute-start.2
  31.9 0.1 collective-permute-start.3
  32.0 0.4 collective-permute-start.4
  32.4 0.0 copy-done.5
  32.4 0.0 slice-start.3
  32.4 7.4 %score_rows.1 = (bf16[512,768]{1,0:T(8,128)(2,1)}, bf16[512,768]{1,0:T(8,128)(2,1)}, bf16[512,768]{1,0:T(8,128)(2,1)S(1)}, bf16[512,768]{1,0:T(8,128)(2,1)S(1)}) custom-call(s32[1]{0:T(128)} %bitcast.1.core_ref, bf16[512,768]{1,0:T(8,128)(2,1)S(1)} %get-tuple-element.41.pred_in_ref, bf16[16,768]{1,0:T(8,128)(2,1)S(1)} %copy-done.5), custom_call_target="tpu_custom_call" | custom-call | flops 4294967296 | bytes 811012 | tf_op jit(solution)/shard_map/score_rows/pallas_call | solution.py:86
  39.8 0.2 collective-permute-start
  40.0 0.0 copy-done.3
  40.0 1.8 %outer_own.1 = (f32[2048,128]{1,0:T(8,128)S(1)}, f32[2048,128]{1,0:T(8,128)S(1)}, f32[2048,128]{1,0:T(8,128)S(1)}) custom-call(s32[1]{0:T(128)} %bitcast.device_ref, bf16[512,768]{1,0:T(8,128)(2,1)S(1)} %get-tuple-element.42.refs_0_, bf16[1024,512]{1,0:T(8,128)(2,1)S(1)} %get-tuple-element.44.refs_2_.refs_1_, ...), custom_call_target="tpu_custom_call" | custom-call | flops 1610612736 | bytes 4980740 | tf_op jit(solution)/shard_map/outer_own/pallas_call | solution.py:86
  41.8 0.4 collective-permute-done.refs_1_.refs_0_
  42.2 0.0 collective-permute-done.1.refs_6_.refs_1_
  42.2 0.0 collective-permute-done.2.refs_7_.refs_2_
  42.2 0.0 collective-permute-done.3.refs_8_.refs_3_
  42.2 0.0 collective-permute-done.4.refs_9_.refs_4_
  42.2 0.0 slice-start.5
  42.2 1.8 %outer_send.1 = (f32[2048,128]{1,0:T(8,128)S(1)}, f32[2048,128]{1,0:T(8,128)S(1)}, f32[2048,128]{1,0:T(8,128)S(1)}) custom-call(s32[1]{0:T(128)} %bitcast.device_ref, bf16[512,768]{1,0:T(8,128)(2,1)S(1)} %collective-permute-done.refs_1_.refs_0_, bf16[1024,512]{1,0:T(8,128)(2,1)S(1)} %collective-permute-done.1.refs_6_.refs_1_, ...), custom_call_target="tpu_custom_call" | custom-call | flops 1610612736 | bytes 8126468 | tf_op jit(solution)/shard_map/outer_send/pallas_call | solution.py:86
  44.0 1.6 %collective-permute-start.5 = (f32[2048,128]{1,0:T(8,128)S(1)}, f32[2048,128]{1,0:T(8,128)S(1)}, u32[]{:S(2)}, u32[]{:S(2)}) collective-permute-start(f32[2048,128]{1,0:T(8,128)S(1)} %get-tuple-element.52), channel_id=1, source_target_pairs={{0,2},{1,33},{2,0},{3,35},{4,6},{5,37},{6,4},{7,39},{8,10},{9,41},... | collective-permute-start | bytes 3145736 | tf_op jit(solution)/shard_map/ppermute | solution.py:73
  45.6 2.1 %collective-permute-start.6 = (f32[2048,128]{1,0:T(8,128)S(1)}, f32[2048,128]{1,0:T(8,128)S(1)}, u32[]{:S(2)}, u32[]{:S(2)}) collective-permute-start(f32[2048,128]{1,0:T(8,128)S(1)} %get-tuple-element.53), channel_id=1, source_target_pairs={{0,6},{1,97},{2,4},{3,99},{4,2},{5,101},{6,0},{7,103},{8,14},{9,10... | collective-permute-start | bytes 3145736 | tf_op jit(solution)/shard_map/ppermute | solution.py:73
  47.7 3.2 %collective-permute-start.7 = (f32[2048,128]{1,0:T(8,128)S(1)}, f32[2048,128]{1,0:T(8,128)S(1)}, u32[]{:S(2)}, u32[]{:S(2)}) collective-permute-start(f32[2048,128]{1,0:T(8,128)S(1)} %get-tuple-element.54), channel_id=1, source_target_pairs={{0,24},{1,17},{2,26},{3,19},{4,28},{5,21},{6,30},{7,23},{8,16},{9,... | collective-permute-start | bytes 3145736 | tf_op jit(solution)/shard_map/ppermute | solution.py:73
  50.9 0.0 slice-done
  50.9 0.0 slice-done.2
  50.9 0.0 slice-done.1
  50.9 0.0 slice-done.3
  50.9 0.0 slice-done.4
  51.0 5.7 %back_begin.1.rest_0_ = f32[512,1024]{1,0:T(8,128)S(1)} custom-call(bf16[512,768]{1,0:T(8,128)(2,1)S(1)} %copy-done, bf16[512,768]{1,0:T(8,128)(2,1)S(1)} %copy-done.1, bf16[4096,768]{1,0:T(8,128)(2,1)S(1)} %bitcast.7, bf16[1024,4096]{1,0:T(8,128)(2,1)S(1)} %bitcast.3, f32[8,512,512]{2,1,0:T(8,128)S(1)} %bitcast.5), custom_call_target="tpu_custom_call" | custom-call | flops 5368709120 | bytes 24641536 | tf_op jit(solution)/shard_map/back_begin/pallas_call | solution.py:86
  56.7 0.0 copy-done.4
  56.7 3.4 %outer_keep.1 = (f32[2048,128]{1,0:T(8,128)S(1)}, f32[2048,128]{1,0:T(8,128)S(1)}, f32[2048,128]{1,0:T(8,128)S(1)}) custom-call(s32[1]{0:T(128)} %bitcast.device_ref, bf16[512,768]{1,0:T(8,128)(2,1)S(1)} %get-tuple-element.42.refs_0_, bf16[512,768]{1,0:T(8,128)(2,1)S(1)} %collective-permute-done.refs_1_.refs_0_, ...), custom_call_target="tpu_custom_call" | custom-call | flops 3221225472 | bytes 9961476 | tf_op jit(solution)/shard_map/outer_keep/pallas_call | solution.py:86
  60.1 0.0 copy-start.2
  60.1 0.0 collective-permute-done.5
  60.1 1.5 %collective-permute-done.6 = f32[2048,128]{1,0:T(8,128)S(1)} collective-permute-done((f32[2048,128]{1,0:T(8,128)S(1)}, f32[2048,128]{1,0:T(8,128)S(1)}, u32[]{:S(2)}, u32[]{:S(2)}) %collective-permute-start.6) | collective-permute-done | bytes 1048608 | tf_op jit(solution)/shard_map/ppermute | solution.py:73
  61.6 2.1 %collective-permute-done.7 = f32[2048,128]{1,0:T(8,128)S(1)} collective-permute-done((f32[2048,128]{1,0:T(8,128)S(1)}, f32[2048,128]{1,0:T(8,128)S(1)}, u32[]{:S(2)}, u32[]{:S(2)}) %collective-permute-start.7) | collective-permute-done | bytes 1048608 | tf_op jit(solution)/shard_map/ppermute | solution.py:73
  63.7 0.1 slice_add_fusion
  63.8 0.7 collective-permute-start.10
  64.5 0.1 slice_add_fusion.1
  64.6 3.3 %collective-permute-start.9 = (f32[1024,128]{1,0:T(8,128)S(1)}, f32[1024,128]{1,0:T(8,128)S(1)}, u32[]{:S(2)}, u32[]{:S(2)}) collective-permute-start(f32[1024,128]{1,0:T(8,128)S(1)} %get-tuple-element.75), channel_id=1, source_target_pairs={{0,24},{1,17},{2,26},{3,19},{4,28},{5,21},{6,30},{7,23},{8,16},{9,... | collective-permute-start | bytes 1572872 | tf_op jit(solution)/shard_map/ppermute | solution.py:73
  67.9 0.1 slice_add_fusion.4
  68.0 0.7 collective-permute-start.8
  68.7 6.1 %back_end.1.refs_6_ = f32[8,16,128]{2,1,0:T(8,128)S(1)} custom-call(bf16[512,768]{1,0:T(8,128)(2,1)S(1)} %copy-done, bf16[512,768]{1,0:T(8,128)(2,1)S(1)} %copy-done.1, bf16[4096,768]{1,0:T(8,128)(2,1)S(1)} %bitcast.7, bf16[1024,4096]{1,0:T(8,128)(2,1)S(1)} %bitcast.3, f32[8,512,512]{2,1,0:T(8,128)S(1)} %bitcast.5, f32[512,1024]{1,0:T(8,128)S(1)} %back_begin.1.rest_0_, ...), custom_call_target="tpu_custom_call" | custom-call | flops 5368709120 | bytes 28837888 | tf_op jit(solution)/shard_map/back_end/pallas_call | solution.py:86
  74.8 0.0 collective-permute-done.10
  74.8 0.3 collective-permute-done.9
  75.1 3.4 %collective-permute-done.8 = f32[1024,128]{1,0:T(8,128)S(1)} collective-permute-done((f32[1024,128]{1,0:T(8,128)S(1)}, f32[1024,128]{1,0:T(8,128)S(1)}, u32[]{:S(2)}, u32[]{:S(2)}) %collective-permute-start.8) | collective-permute-done | bytes 524320 | tf_op jit(solution)/shard_map/ppermute | solution.py:73
  78.4 0.1 slice_add_fusion.6
  78.5 0.7 collective-permute-start.13
  79.2 0.1 slice_add_fusion.7
  79.2 0.2 collective-permute-start.12
  79.5 0.1 slice_add_fusion.8
  79.6 1.1 %collective-permute-start.11 = (f32[512,128]{1,0:T(8,128)S(1)}, f32[512,128]{1,0:T(8,128)S(1)}, u32[]{:S(2)}, u32[]{:S(2)}) collective-permute-start(f32[512,128]{1,0:T(8,128)S(1)} %get-tuple-element.82), channel_id=1, source_target_pairs={{0,24},{1,17},{2,26},{3,19},{4,28},{5,21},{6,30},{7,23},{8,16},{9,... | collective-permute-start | bytes 786440 | tf_op jit(solution)/shard_map/ppermute | solution.py:73
  80.7 0.0 collective-permute-start.14
  80.7 1.3 %collective-permute-done.14.refs_7_ = f32[8,16,128]{2,1,0:T(8,128)S(1)} collective-permute-done((f32[8,16,128]{2,1,0:T(8,128)S(1)}, f32[8,16,128]{2,1,0:T(8,128)S(1)}, u32[]{:S(2)}, u32[]{:S(2)}) %collective-permute-start.14) | collective-permute-done | bytes 65568 | tf_op jit(solution)/shard_map/ppermute | solution.py:77
  81.9 4.2 %collective-permute-done.13.refs_5_ = f32[512,128]{1,0:T(8,128)S(1)} collective-permute-done((f32[512,128]{1,0:T(8,128)S(1)}, f32[512,128]{1,0:T(8,128)S(1)}, u32[]{:S(2)}, u32[]{:S(2)}) %collective-permute-start.13) | collective-permute-done | bytes 262176 | tf_op jit(solution)/shard_map/ppermute | solution.py:73
  86.2 0.0 collective-permute-done.12.refs_4_
  86.2 1.1 %collective-permute-done.11.refs_3_ = f32[512,128]{1,0:T(8,128)S(1)} collective-permute-done((f32[512,128]{1,0:T(8,128)S(1)}, f32[512,128]{1,0:T(8,128)S(1)}, u32[]{:S(2)}, u32[]{:S(2)}) %collective-permute-start.11) | collective-permute-done | bytes 262176 | tf_op jit(solution)/shard_map/ppermute | solution.py:73
  87.2 0.1 pack.1
  87.3 13.0 %all_to_all.10.got_ref = f32[8,224,128]{2,1,0:T(8,128)S(1)} all-to-all(f32[8,224,128]{2,1,0:T(8,128)S(1)} %pack.1), channel_id=1, replica_groups={{0,16,32,48,64,80,96,112},{8,24,40,56,72,88,104,120},{2,18,34,50,66,82,..., dimensions={0} | all-to-all | bytes 1835008 | tf_op jit(solution)/shard_map/all_to_all | solution.py:422
  100.4 0.1 collective-permute-start.15
  100.5 1.3 %collective-permute-done.15.given_ref = f32[224,128]{1,0:T(8,128)S(1)} collective-permute-done((f32[224,128]{1,0:T(8,128)S(1)}, f32[224,128]{1,0:T(8,128)S(1)}, u32[]{:S(2)}, u32[]{:S(2)}) %collective-permute-start.15) | collective-permute-done | bytes 114720 | tf_op jit(solution)/shard_map/ppermute | solution.py:77
  101.8 0.7 place_blocks.1
  (16 shorter events, 0.1 us)
Async XLA Ops:
  2.3 12.5 %all-to-all-start = ((bf16[8,5,16,128]{3,2,1,0:T(8,128)(2,1)}), bf16[8,5,16,128]{3,2,1,0:T(8,128)(2,1)S(1)}, u32[]{:S(2)}, u32[]{:S(2)}) async-start(bf16[8,5,16,128]{3,2,1,0:T(8,128)(2,1)} %gather_in.1), calls=%async_computation | async-start | bytes 327680 | tf_op jit(solution)/shard_map/all_to_all | solution.py:364
  8.9 23.6 %copy-start.5 = (bf16[16,768]{1,0:T(8,128)(2,1)S(1)}, bf16[16,768]{1,0:T(8,128)(2,1)}, u32[]{:S(2)}) copy-start(bf16[16,768]{1,0:T(8,128)(2,1)} %target_ref.1) | copy-start | bytes 73732
  31.3 8.7 %copy-start.3 = (bf16[1024,512]{1,0:T(8,128)(2,1)}, bf16[1024,512]{1,0:T(8,128)(2,1)S(1)}, u32[]{:S(2)}) copy-start(bf16[1024,512]{1,0:T(8,128)(2,1)S(1)} %get-tuple-element.47.refs_5_.refs_4_) | copy-start | bytes 3145732
  31.3 10.9 %collective-permute-start.1 = (bf16[1024,512]{1,0:T(8,128)(2,1)S(1)}, bf16[1024,512]{1,0:T(8,128)(2,1)S(1)}, u32[]{:S(2)}, u32[]{:S(2)}) collective-permute-start(bf16[1024,512]{1,0:T(8,128)(2,1)S(1)} %get-tuple-element.44.refs_2_.refs_1_), channel_id=1, source_target_pairs={{0,1},{1,0},{2,3},{3,2},{4,5},{5,4},{6,7},{7,6},{8,9},{9,8},{10,11... | collective-permute-start | bytes 3145736 | tf_op jit(solution)/shard_map/ppermute | solution.py:77
  31.4 10.8 %collective-permute-start.2 = (bf16[1024,512]{1,0:T(8,128)(2,1)S(1)}, bf16[1024,512]{1,0:T(8,128)(2,1)S(1)}, u32[]{:S(2)}, u32[]{:S(2)}) collective-permute-start(bf16[1024,512]{1,0:T(8,128)(2,1)S(1)} %get-tuple-element.45.refs_3_.refs_2_), channel_id=1, source_target_pairs={{0,1},{1,0},{2,3},{3,2},{4,5},{5,4},{6,7},{7,6},{8,9},{9,8},{10,11... | collective-permute-start | bytes 3145736 | tf_op jit(solution)/shard_map/ppermute | solution.py:77
  31.9 10.3 %collective-permute-start.3 = (bf16[1024,512]{1,0:T(8,128)(2,1)S(1)}, bf16[1024,512]{1,0:T(8,128)(2,1)S(1)}, u32[]{:S(2)}, u32[]{:S(2)}) collective-permute-start(bf16[1024,512]{1,0:T(8,128)(2,1)S(1)} %get-tuple-element.46.refs_4_.refs_3_), channel_id=1, source_target_pairs={{0,1},{1,0},{2,3},{3,2},{4,5},{5,4},{6,7},{7,6},{8,9},{9,8},{10,11... | collective-permute-start | bytes 3145736 | tf_op jit(solution)/shard_map/ppermute | solution.py:77
  32.0 10.2 %collective-permute-start.4 = (bf16[1024,512]{1,0:T(8,128)(2,1)S(1)}, bf16[1024,512]{1,0:T(8,128)(2,1)S(1)}, u32[]{:S(2)}, u32[]{:S(2)}) collective-permute-start(bf16[1024,512]{1,0:T(8,128)(2,1)S(1)} %get-tuple-element.47.refs_5_.refs_4_), channel_id=1, source_target_pairs={{0,1},{1,0},{2,3},{3,2},{4,5},{5,4},{6,7},{7,6},{8,9},{9,8},{10,11... | collective-permute-start | bytes 3145736 | tf_op jit(solution)/shard_map/ppermute | solution.py:77
  32.4 18.5 %slice-start = ((s8[8388608]{0:T(1024)(128)(4,1)}), s8[4194304]{0:T(1024)(128)(4,1)S(1)}, s32[]{:S(2)}) async-start(s8[8388608]{0:T(1024)(128)(4,1)} %bitcast.2), calls=%async_computation.2 | async-start | bytes 8388608
  32.4 18.5 %slice-start.2 = ((s8[8388608]{0:T(1024)(128)(4,1)}), s8[4194304]{0:T(1024)(128)(4,1)S(1)}, s32[]{:S(2)}) async-start(s8[8388608]{0:T(1024)(128)(4,1)} %bitcast.4), calls=%async_computation.4 | async-start | bytes 8388608
  32.4 18.5 %slice-start.1 = ((s8[8388608]{0:T(1024)(128)(4,1)}), s8[4194304]{0:T(1024)(128)(4,1)S(1)}, s32[]{:S(2)}) async-start(s8[8388608]{0:T(1024)(128)(4,1)} %bitcast.2), calls=%async_computation.3 | async-start | bytes 8388608
  32.4 18.5 %slice-start.3 = ((s8[8388608]{0:T(1024)(128)(4,1)}), s8[4194304]{0:T(1024)(128)(4,1)S(1)}, s32[]{:S(2)}) async-start(s8[8388608]{0:T(1024)(128)(4,1)} %bitcast.4), calls=%async_computation.5 | async-start | bytes 8388608
  39.8 2.4 %collective-permute-start = (bf16[512,768]{1,0:T(8,128)(2,1)S(1)}, bf16[512,768]{1,0:T(8,128)(2,1)S(1)}, u32[]{:S(2)}, u32[]{:S(2)}) collective-permute-start(bf16[512,768]{1,0:T(8,128)(2,1)S(1)} %get-tuple-element.43), channel_id=1, source_target_pairs={{0,1},{1,0},{2,3},{3,2},{4,5},{5,4},{6,7},{7,6},{8,9},{9,8},{10,11... | collective-permute-start | bytes 2359304 | tf_op jit(solution)/shard_map/ppermute | solution.py:77
  40.0 10.9 %slice-start.4 = ((s8[6291456]{0:T(1024)(128)(4,1)}), s8[4194304]{0:T(1024)(128)(4,1)S(1)}, s32[]{:S(2)}) async-start(s8[6291456]{0:T(1024)(128)(4,1)} %bitcast.6), calls=%async_computation.6 | async-start | bytes 8388608
  40.0 10.9 %copy-start = (bf16[512,768]{1,0:T(8,128)(2,1)S(1)}, bf16[512,768]{1,0:T(8,128)(2,1)}, u32[]{:S(2)}) copy-start(bf16[512,768]{1,0:T(8,128)(2,1)} %get-tuple-element.55.high_ref) | copy-start | bytes 2359300
  40.0 10.9 %copy-start.1 = (bf16[512,768]{1,0:T(8,128)(2,1)S(1)}, bf16[512,768]{1,0:T(8,128)(2,1)}, u32[]{:S(2)}) copy-start(bf16[512,768]{1,0:T(8,128)(2,1)} %get-tuple-element.56.low_ref) | copy-start | bytes 2359300
  42.2 8.7 %slice-start.5 = ((s8[6291456]{0:T(1024)(128)(4,1)}), s8[2097152]{0:T(1024)(128)(4,1)S(1)}, s32[]{:S(2)}) async-start(s8[6291456]{0:T(1024)(128)(4,1)} %bitcast.6), calls=%async_computation.7 | async-start | bytes 4194304
  44.0 16.1 %collective-permute-start.5 = (f32[2048,128]{1,0:T(8,128)S(1)}, f32[2048,128]{1,0:T(8,128)S(1)}, u32[]{:S(2)}, u32[]{:S(2)}) collective-permute-start(f32[2048,128]{1,0:T(8,128)S(1)} %get-tuple-element.52), channel_id=1, source_target_pairs={{0,2},{1,33},{2,0},{3,35},{4,6},{5,37},{6,4},{7,39},{8,10},{9,41},... | collective-permute-start | bytes 3145736 | tf_op jit(solution)/shard_map/ppermute | solution.py:73
  45.6 16.0 %collective-permute-start.6 = (f32[2048,128]{1,0:T(8,128)S(1)}, f32[2048,128]{1,0:T(8,128)S(1)}, u32[]{:S(2)}, u32[]{:S(2)}) collective-permute-start(f32[2048,128]{1,0:T(8,128)S(1)} %get-tuple-element.53), channel_id=1, source_target_pairs={{0,6},{1,97},{2,4},{3,99},{4,2},{5,101},{6,0},{7,103},{8,14},{9,10... | collective-permute-start | bytes 3145736 | tf_op jit(solution)/shard_map/ppermute | solution.py:73
  47.7 16.0 %collective-permute-start.7 = (f32[2048,128]{1,0:T(8,128)S(1)}, f32[2048,128]{1,0:T(8,128)S(1)}, u32[]{:S(2)}, u32[]{:S(2)}) collective-permute-start(f32[2048,128]{1,0:T(8,128)S(1)} %get-tuple-element.54), channel_id=1, source_target_pairs={{0,24},{1,17},{2,26},{3,19},{4,28},{5,21},{6,30},{7,23},{8,16},{9,... | collective-permute-start | bytes 3145736 | tf_op jit(solution)/shard_map/ppermute | solution.py:73
  51.0 5.7 %copy-start.4 = (bf16[1024,512]{1,0:T(8,128)(2,1)S(1)}, bf16[1024,512]{1,0:T(8,128)(2,1)}, u32[]{:S(2)}) copy-start(bf16[1024,512]{1,0:T(8,128)(2,1)} %copy-done.3) | copy-start | bytes 3145732
  60.1 8.6 %copy-start.2 = (f32[512,1024]{1,0:T(8,128)S(1)}, f32[512,1024]{1,0:T(8,128)}, u32[]{:S(2)}) copy-start(f32[512,1024]{1,0:T(8,128)} %get-tuple-element.64.rest_1_) | copy-start | bytes 6291460
  63.8 11.0 %collective-permute-start.10 = (f32[1024,128]{1,0:T(8,128)S(1)}, f32[1024,128]{1,0:T(8,128)S(1)}, u32[]{:S(2)}, u32[]{:S(2)}) collective-permute-start(f32[1024,128]{1,0:T(8,128)S(1)} %get-tuple-element.73), channel_id=1, source_target_pairs={{0,2},{1,33},{2,0},{3,35},{4,6},{5,37},{6,4},{7,39},{8,10},{9,41},... | collective-permute-start | bytes 1572872 | tf_op jit(solution)/shard_map/ppermute | solution.py:73
  64.6 10.5 %collective-permute-start.9 = (f32[1024,128]{1,0:T(8,128)S(1)}, f32[1024,128]{1,0:T(8,128)S(1)}, u32[]{:S(2)}, u32[]{:S(2)}) collective-permute-start(f32[1024,128]{1,0:T(8,128)S(1)} %get-tuple-element.75), channel_id=1, source_target_pairs={{0,24},{1,17},{2,26},{3,19},{4,28},{5,21},{6,30},{7,23},{8,16},{9,... | collective-permute-start | bytes 1572872 | tf_op jit(solution)/shard_map/ppermute | solution.py:73
  68.0 10.5 %collective-permute-start.8 = (f32[1024,128]{1,0:T(8,128)S(1)}, f32[1024,128]{1,0:T(8,128)S(1)}, u32[]{:S(2)}, u32[]{:S(2)}) collective-permute-start(f32[1024,128]{1,0:T(8,128)S(1)} %get-tuple-element.76), channel_id=1, source_target_pairs={{0,6},{1,97},{2,4},{3,99},{4,2},{5,101},{6,0},{7,103},{8,14},{9,10... | collective-permute-start | bytes 1572872 | tf_op jit(solution)/shard_map/ppermute | solution.py:73
  78.5 7.7 %collective-permute-start.13 = (f32[512,128]{1,0:T(8,128)S(1)}, f32[512,128]{1,0:T(8,128)S(1)}, u32[]{:S(2)}, u32[]{:S(2)}) collective-permute-start(f32[512,128]{1,0:T(8,128)S(1)} %get-tuple-element.78), channel_id=1, source_target_pairs={{0,6},{1,97},{2,4},{3,99},{4,2},{5,101},{6,0},{7,103},{8,14},{9,10... | collective-permute-start | bytes 786440 | tf_op jit(solution)/shard_map/ppermute | solution.py:73
  79.2 6.9 %collective-permute-start.12 = (f32[512,128]{1,0:T(8,128)S(1)}, f32[512,128]{1,0:T(8,128)S(1)}, u32[]{:S(2)}, u32[]{:S(2)}) collective-permute-start(f32[512,128]{1,0:T(8,128)S(1)} %get-tuple-element.80), channel_id=1, source_target_pairs={{0,2},{1,33},{2,0},{3,35},{4,6},{5,37},{6,4},{7,39},{8,10},{9,41},... | collective-permute-start | bytes 786440 | tf_op jit(solution)/shard_map/ppermute | solution.py:73
  79.6 7.7 %collective-permute-start.11 = (f32[512,128]{1,0:T(8,128)S(1)}, f32[512,128]{1,0:T(8,128)S(1)}, u32[]{:S(2)}, u32[]{:S(2)}) collective-permute-start(f32[512,128]{1,0:T(8,128)S(1)} %get-tuple-element.82), channel_id=1, source_target_pairs={{0,24},{1,17},{2,26},{3,19},{4,28},{5,21},{6,30},{7,23},{8,16},{9,... | collective-permute-start | bytes 786440 | tf_op jit(solution)/shard_map/ppermute | solution.py:73
  80.7 1.3 %collective-permute-start.14 = (f32[8,16,128]{2,1,0:T(8,128)S(1)}, f32[8,16,128]{2,1,0:T(8,128)S(1)}, u32[]{:S(2)}, u32[]{:S(2)}) collective-permute-start(f32[8,16,128]{2,1,0:T(8,128)S(1)} %back_end.1.refs_6_), channel_id=1, source_target_pairs={{0,1},{1,0},{2,3},{3,2},{4,5},{5,4},{6,7},{7,6},{8,9},{9,8},{10,11... | collective-permute-start | bytes 196616 | tf_op jit(solution)/shard_map/ppermute | solution.py:77
  100.4 1.4 %collective-permute-start.15 = (f32[224,128]{1,0:T(8,128)S(1)}, f32[224,128]{1,0:T(8,128)S(1)}, u32[]{:S(2)}, u32[]{:S(2)}) collective-permute-start(f32[224,128]{1,0:T(8,128)S(1)} %get-tuple-element.70), channel_id=1, source_target_pairs={{0,1},{1,0},{2,3},{3,2},{4,5},{5,4},{6,7},{7,6},{8,9},{9,8},{10,11... | collective-permute-start | bytes 344072 | tf_op jit(solution)/shard_map/ppermute | solution.py:77

commit v5 on v4

--- a/solution.py
+++ b/solution.py
@@ -11,6 +11,7 @@
 AXES = ("member", "token")
 FIRST = (("x0", "x1", "z1"), ("y0", "y1", "z0"))
 CHUNK = 512
+NEAR = 1024
 STEPS = 4096 // CHUNK
 F32, BF16 = jnp.float32, jnp.bfloat16
 LAST = (((1,), (1,)), ((), ()))
@@ -116,10 +117,16 @@
         out_ref[j, 4] = latents_ref[rows, :]
 
 
-def forward_kernel(moved_ref, nw_hbm, gain_ref, w_in_hbm, w_out_hbm, cond_hbm, slope_hbm, pred_ref, *rest):
+def fetch_kernel(w_in_hbm, near_ref, sem):
+    copy = pltpu.make_async_copy(w_in_hbm.at[:, 0:NEAR], near_ref, sem)
+    copy.start()
+    copy.wait()
+
+
+def forward_kernel(moved_ref, near_ref, nw_hbm, gain_ref, w_in_hbm, w_out_hbm, cond_hbm, slope_hbm, pred_ref, *rest):
     turned = rest[:4]
     cond_ref, slope_ref, pre_ref, total_ref, out_sems, cond_sem = rest[4:10]
-    w_in_ref, w_out_ref, nw_ref, in_sems, mid_sems, nw_sem = rest[10:]
+    w_in_ref, w_out_ref, nw_ref, in_sem, mid_sems, nw_sem = rest[10:]
 
     def columns(step):
         return slice(step * CHUNK, (step + 1) * CHUNK)
@@ -127,19 +134,16 @@
     def put(step):
         return pltpu.make_async_copy(slope_ref.at[step], slope_hbm.at[step], out_sems.at[step])
 
-    def fetch_in(i):
-        rows = slice(i * 128, i * 128 + 128)
-        return pltpu.make_async_copy(w_in_hbm.at[rows, :], w_in_ref.at[rows, :], in_sems.at[i])
-
-    def fetch_out(step):
-        return pltpu.make_async_copy(w_out_hbm.at[columns(step), :], w_out_ref.at[columns(step), :], mid_sems.at[step])
-
+    fetch_in = pltpu.make_async_copy(w_in_hbm.at[:, NEAR:], w_in_ref, in_sem)
+    fetch_out = [
+        pltpu.make_async_copy(w_out_hbm.at[rows, :], w_out_ref.at[rows, :], mid_sems.at[i])
+        for i, rows in enumerate((slice(0, NEAR), slice(NEAR, 4096)))
+    ]
     fetch_nw = pltpu.make_async_copy(nw_hbm, nw_ref, nw_sem)
     fetch_nw.start()
-    for i in range(8):
-        fetch_in(i).start()
-    for step in range(STEPS):
-        fetch_out(step).start()
+    fetch_out[0].start()
+    fetch_in.start()
+    fetch_out[1].start()
     moved = moved_ref[...]
     noise = moved[:, :4].reshape(512, 128)
     latents = jnp.concatenate([moved[j, 4] for j in range(8)], axis=1).astype(F32)
@@ -154,14 +158,17 @@
     root = np.float32(np.sqrt(2 / np.pi))
     cubic = np.float32(np.sqrt(2 / np.pi) * 0.044715)
     for step in range(STEPS + 1):
-        if step == 0:
-            for i in range(8):
-                fetch_in(i).wait()
-        if step < STEPS:
-            pre_ref[step % 2] = jnp.dot(normed, w_in_ref[:, columns(step)], preferred_element_type=F32)
+        if step == NEAR // CHUNK:
+            fetch_in.wait()
+        if step < NEAR // CHUNK:
+            pre_ref[step % 2] = jnp.dot(normed, near_ref[:, columns(step)], preferred_element_type=F32)
+        elif step < STEPS:
+            at = slice(step * CHUNK - NEAR, (step + 1) * CHUNK - NEAR)
+            pre_ref[step % 2] = jnp.dot(normed, w_in_ref[:, at], preferred_element_type=F32)
         if step == 1:
-            for i in range(STEPS):
-                fetch_out(i).wait()
+            fetch_out[0].wait()
+        if step == NEAR // CHUNK + 1:
+            fetch_out[1].wait()
         if step > 0:
             done = step - 1
             pre = pre_ref[done % 2]
@@ -362,12 +369,15 @@
     noise, latents, device, core = lax.optimization_barrier((noise, latents, device, core))
     (moved,) = call(gather_kernel, "gather_in", [((8, 5, 16, 128), BF16)], (noise, latents), "aa", "m", [pltpu.VMEM((4, 128, 128), BF16), pltpu.VMEM((128, 128), BF16), pltpu.SemaphoreType.DMA((2,))])
     moved = lax.all_to_all(moved, "member", split_axis=0, concat_axis=0, tiled=True)
+    (near,) = call(
+        fetch_kernel, "fetch_near", [((1024, NEAR), BF16)], (w_in,), "a", "m", [pltpu.SemaphoreType.DMA], limit=1
+    )
     cond, slope, pred, *turned = call(
         forward_kernel,
         "forward_rows",
         [((512, 1024), F32), ((STEPS, 512, CHUNK), F32), ((512, 768), BF16)] + [((1024, 512), BF16)] * 4,
-        (moved, noise_weight, gain, w_in, w_out),
-        "mamaa",
+        (moved, near, noise_weight, gain, w_in, w_out),
+        "mmamaa",
         "hhmmmmm",
         [
             pltpu.VMEM((512, 1024), F32),
@@ -376,15 +386,15 @@
             pltpu.VMEM((512, 768), F32),
             pltpu.SemaphoreType.DMA((STEPS,)),
             pltpu.SemaphoreType.DMA,
-            pltpu.VMEM((1024, 4096), BF16),
+            pltpu.VMEM((1024, 4096 - NEAR), BF16),
             pltpu.VMEM((4096, 768), BF16),
             pltpu.VMEM((128, 1024), BF16),
-            pltpu.SemaphoreType.DMA((8,)),
-            pltpu.SemaphoreType.DMA((STEPS,)),
+            pltpu.SemaphoreType.DMA,
+            pltpu.SemaphoreType.DMA((2,)),
             pltpu.SemaphoreType.DMA,
         ],
         flops=2 * 512 * 4096 * (1024 + 768),
-        limit=40,
+        limit=32,
     )
     theirs = [swap_core(piece) for piece in turned]
     high, low, own, other = call(
@@ -396,7 +406,7 @@
         "hhmm",
         [pltpu.VMEM((32, 16, 768), F32)] * 2 + [pltpu.VMEM((512, 768), BF16)] * 2 + [pltpu.SemaphoreType.DMA((2,))],
         flops=2 * 512 * 4096 * 1024,
-        limit=16,
+        limit=10,
     )
     got = swap_core(other)
     begun = make_outer("outer_own", 1, device, (own,), (turned,))

time: 104 us -> 101 us (0.971)
  waiting for transfers between devices: 21.3 us -> 19.6 us
    all_to_all x1, waiting for transfers between devices: 5.85 us -> 4.23 us  [per_device(): lax.all_to_all(moved, 'member', split_axis=0, concat_axis=0, tiled=True)]
    pallas_call x11 -> x12, Pallas kernels: 45.2 us -> 44.3 us  [call(): pl.pallas_call(body, in_specs=[pl.BlockSpec(memory_space=kinds[space]) fo...]
  transfers between devices with their start and end apart: 17 -> 17, of which waited for: 10 -> 10; matrix products, arithmetic and copies ran while one was open for 1% -> 1% of each run, Pallas kernels for 24% -> 26%
where the time goes in v5:
time: 101 us; the launch traced here: 100 us
  Pallas kernels  44.3 us (44%)
  starting transfers between devices  20.8 us (21%)
  waiting for transfers between devices  19.6 us (19%)
  blocking collectives  13 us (13%)
    pallas_call x12, Pallas kernels, call(): pl.pallas_call(body, in_specs=[pl.BlockSpec(memory_space=kinds[space]) fo...  44.3 us
    ppermute x9, starting transfers between devices, swap_stage(): return lax.ppermute(values, AXES, pairs)  13.5 us
    all_to_all x1, blocking collectives, per_device(): lax.all_to_all(packed, AXES, split_axis=0, concat_axis=0, tiled=True, axi...  13 us
    ppermute x9, waiting for transfers between devices, swap_stage(): return lax.ppermute(values, AXES, pairs)  12.5 us
    all_to_all x1, starting transfers between devices, per_device(): lax.all_to_all(moved, 'member', split_axis=0, concat_axis=0, tiled=True)  5.92 us
    all_to_all x1, waiting for transfers between devices, per_device(): lax.all_to_all(moved, 'member', split_axis=0, concat_axis=0, tiled=True)  4.23 us
    ppermute x7, waiting for transfers between devices, swap_core(): return lax.ppermute(values, AXES, [(i, i ^ 1) for i in range(128)])  2.94 us
  transfers between devices with their start and end apart: 17, of which 10 were waited for; matrix products, arithmetic and copies ran while one was open for 1% of the time, Pallas kernels for 26%

profile of v5, /device:TPU:0, one launch (start us, length us, event | category | flops | bytes accessed | tf_op | source)
XLA Modules:
  0.0 100.0 jit_solution(16727207866819120594)
XLA Ops:
  0.6 1.6 %gather_in.1 = bf16[8,5,16,128]{3,2,1,0:T(8,128)(2,1)} custom-call(bf16[4,128,128]{2,1,0:T(8,128)(2,1)} %noise_hbm, bf16[128,128]{1,0:T(8,128)(2,1)} %latents_hbm), custom_call_target="tpu_custom_call" | custom-call | bytes 163840 | tf_op jit(solution)/shard_map/gather_in/pallas_call | solution.py:87
  2.3 5.9 %all-to-all-start = ((bf16[8,5,16,128]{3,2,1,0:T(8,128)(2,1)}), bf16[8,5,16,128]{3,2,1,0:T(8,128)(2,1)S(1)}, u32[]{:S(2)}, u32[]{:S(2)}) async-start(bf16[8,5,16,128]{3,2,1,0:T(8,128)(2,1)} %gather_in.1), calls=%async_computation | async-start | bytes 327680 | tf_op jit(solution)/shard_map/all_to_all | solution.py:371
  8.2 0.7 reshape.15.gain_ref.rest_2_
  8.9 1.6 %fetch_near.1.near_ref = bf16[1024,1024]{1,0:T(8,128)(2,1)S(1)} custom-call(bf16[1024,4096]{1,0:T(8,128)(2,1)} %w_in_ref.3), custom_call_target="tpu_custom_call" | custom-call | bytes 8388608 | tf_op jit(solution)/shard_map/fetch_near/pallas_call | solution.py:87
  10.5 0.0 copy-start.5
  10.5 4.2 %all-to-all-done.moved_ref = bf16[8,5,16,128]{3,2,1,0:T(8,128)(2,1)S(1)} async-done(((bf16[8,5,16,128]{3,2,1,0:T(8,128)(2,1)}), bf16[8,5,16,128]{3,2,1,0:T(8,128)(2,1)S(1)}, u32[]{:S(2)}, u32[]{:S(2)}) %all-to-all-start) | async-done | bytes 163872 | tf_op jit(solution)/shard_map/all_to_all | solution.py:371
  14.7 14.1 %forward_rows.1 = (f32[512,1024]{1,0:T(8,128)}, f32[8,512,512]{2,1,0:T(8,128)}, bf16[512,768]{1,0:T(8,128)(2,1)S(1)}, bf16[1024,512]{1,0:T(8,128)(2,1)S(1)}, bf1...) custom-call(bf16[8,5,16,128]{3,2,1,0:T(8,128)(2,1)S(1)} %all-to-all-done.moved_ref, ...), custom_call_target="tpu_custom_call" | custom-call | flops 7516192768 | bytes 17205248 | tf_op jit(solution)/shard_map/forward_rows/pallas_call | solution.py:87
  28.8 0.0 copy-start.3
  28.8 0.1 collective-permute-start.1
  28.9 0.5 collective-permute-start.2
  29.4 0.1 collective-permute-start.3
  29.5 0.4 collective-permute-start.4
  29.9 0.0 copy-done.5
  29.9 0.0 slice-start.3
  29.9 7.4 %score_rows.1 = (bf16[512,768]{1,0:T(8,128)(2,1)}, bf16[512,768]{1,0:T(8,128)(2,1)}, bf16[512,768]{1,0:T(8,128)(2,1)S(1)}, bf16[512,768]{1,0:T(8,128)(2,1)S(1)}) custom-call(s32[1]{0:T(128)} %bitcast.1.core_ref, bf16[512,768]{1,0:T(8,128)(2,1)S(1)} %get-tuple-element.41.pred_in_ref, bf16[16,768]{1,0:T(8,128)(2,1)S(1)} %copy-done.5), custom_call_target="tpu_custom_call" | custom-call | flops 4294967296 | bytes 811012 | tf_op jit(solution)/shard_map/score_rows/pallas_call | solution.py:87
  37.3 0.2 collective-permute-start
  37.5 0.0 copy-done.3
  37.5 1.8 %outer_own.1 = (f32[2048,128]{1,0:T(8,128)S(1)}, f32[2048,128]{1,0:T(8,128)S(1)}, f32[2048,128]{1,0:T(8,128)S(1)}) custom-call(s32[1]{0:T(128)} %bitcast.device_ref, bf16[512,768]{1,0:T(8,128)(2,1)S(1)} %get-tuple-element.42.refs_0_, bf16[1024,512]{1,0:T(8,128)(2,1)S(1)} %get-tuple-element.44.refs_2_.refs_1_, ...), custom_call_target="tpu_custom_call" | custom-call | flops 1610612736 | bytes 4980740 | tf_op jit(solution)/shard_map/outer_own/pallas_call | solution.py:87
  39.3 0.4 collective-permute-done.refs_1_.refs_0_
  39.6 0.0 collective-permute-done.1.refs_6_.refs_1_
  39.6 0.0 collective-permute-done.2.refs_7_.refs_2_
  39.7 0.0 collective-permute-done.3.refs_8_.refs_3_
  39.7 0.0 collective-permute-done.4.refs_9_.refs_4_
  39.7 0.0 slice-start.5
  39.7 1.8 %outer_send.1 = (f32[2048,128]{1,0:T(8,128)S(1)}, f32[2048,128]{1,0:T(8,128)S(1)}, f32[2048,128]{1,0:T(8,128)S(1)}) custom-call(s32[1]{0:T(128)} %bitcast.device_ref, bf16[512,768]{1,0:T(8,128)(2,1)S(1)} %collective-permute-done.refs_1_.refs_0_, bf16[1024,512]{1,0:T(8,128)(2,1)S(1)} %collective-permute-done.1.refs_6_.refs_1_, ...), custom_call_target="tpu_custom_call" | custom-call | flops 1610612736 | bytes 8126468 | tf_op jit(solution)/shard_map/outer_send/pallas_call | solution.py:87
  41.5 1.6 %collective-permute-start.5 = (f32[2048,128]{1,0:T(8,128)S(1)}, f32[2048,128]{1,0:T(8,128)S(1)}, u32[]{:S(2)}, u32[]{:S(2)}) collective-permute-start(f32[2048,128]{1,0:T(8,128)S(1)} %get-tuple-element.52), channel_id=1, source_target_pairs={{0,2},{1,33},{2,0},{3,35},{4,6},{5,37},{6,4},{7,39},{8,10},{9,41},... | collective-permute-start | bytes 3145736 | tf_op jit(solution)/shard_map/ppermute | solution.py:74
  43.1 2.1 %collective-permute-start.6 = (f32[2048,128]{1,0:T(8,128)S(1)}, f32[2048,128]{1,0:T(8,128)S(1)}, u32[]{:S(2)}, u32[]{:S(2)}) collective-permute-start(f32[2048,128]{1,0:T(8,128)S(1)} %get-tuple-element.53), channel_id=1, source_target_pairs={{0,6},{1,97},{2,4},{3,99},{4,2},{5,101},{6,0},{7,103},{8,14},{9,10... | collective-permute-start | bytes 3145736 | tf_op jit(solution)/shard_map/ppermute | solution.py:74
  45.2 3.2 %collective-permute-start.7 = (f32[2048,128]{1,0:T(8,128)S(1)}, f32[2048,128]{1,0:T(8,128)S(1)}, u32[]{:S(2)}, u32[]{:S(2)}) collective-permute-start(f32[2048,128]{1,0:T(8,128)S(1)} %get-tuple-element.54), channel_id=1, source_target_pairs={{0,24},{1,17},{2,26},{3,19},{4,28},{5,21},{6,30},{7,23},{8,16},{9,... | collective-permute-start | bytes 3145736 | tf_op jit(solution)/shard_map/ppermute | solution.py:74
  48.3 0.0 slice-done
  48.4 0.0 slice-done.2
  48.4 0.0 slice-done.1
  48.4 0.0 slice-done.3
  48.4 0.0 slice-done.4
  48.4 5.7 %back_begin.1.rest_0_ = f32[512,1024]{1,0:T(8,128)S(1)} custom-call(bf16[512,768]{1,0:T(8,128)(2,1)S(1)} %copy-done, bf16[512,768]{1,0:T(8,128)(2,1)S(1)} %copy-done.1, bf16[4096,768]{1,0:T(8,128)(2,1)S(1)} %bitcast.7, bf16[1024,4096]{1,0:T(8,128)(2,1)S(1)} %bitcast.3, f32[8,512,512]{2,1,0:T(8,128)S(1)} %bitcast.5), custom_call_target="tpu_custom_call" | custom-call | flops 5368709120 | bytes 24641536 | tf_op jit(solution)/shard_map/back_begin/pallas_call | solution.py:87
  54.1 3.4 %outer_keep.1 = (f32[2048,128]{1,0:T(8,128)S(1)}, f32[2048,128]{1,0:T(8,128)S(1)}, f32[2048,128]{1,0:T(8,128)S(1)}) custom-call(s32[1]{0:T(128)} %bitcast.device_ref, bf16[512,768]{1,0:T(8,128)(2,1)S(1)} %get-tuple-element.42.refs_0_, bf16[512,768]{1,0:T(8,128)(2,1)S(1)} %collective-permute-done.refs_1_.refs_0_, ...), custom_call_target="tpu_custom_call" | custom-call | flops 3221225472 | bytes 9961476 | tf_op jit(solution)/shard_map/outer_keep/pallas_call | solution.py:87
  57.6 0.0 collective-permute-done.5
  57.6 1.5 %collective-permute-done.6 = f32[2048,128]{1,0:T(8,128)S(1)} collective-permute-done((f32[2048,128]{1,0:T(8,128)S(1)}, f32[2048,128]{1,0:T(8,128)S(1)}, u32[]{:S(2)}, u32[]{:S(2)}) %collective-permute-start.6) | collective-permute-done | bytes 1048608 | tf_op jit(solution)/shard_map/ppermute | solution.py:74
  59.1 2.1 %collective-permute-done.7 = f32[2048,128]{1,0:T(8,128)S(1)} collective-permute-done((f32[2048,128]{1,0:T(8,128)S(1)}, f32[2048,128]{1,0:T(8,128)S(1)}, u32[]{:S(2)}, u32[]{:S(2)}) %collective-permute-start.7) | collective-permute-done | bytes 1048608 | tf_op jit(solution)/shard_map/ppermute | solution.py:74
  61.2 0.1 slice_add_fusion
  61.3 0.7 collective-permute-start.10
  62.0 0.1 slice_add_fusion.1
  62.1 3.3 %collective-permute-start.9 = (f32[1024,128]{1,0:T(8,128)S(1)}, f32[1024,128]{1,0:T(8,128)S(1)}, u32[]{:S(2)}, u32[]{:S(2)}) collective-permute-start(f32[1024,128]{1,0:T(8,128)S(1)} %get-tuple-element.75), channel_id=1, source_target_pairs={{0,24},{1,17},{2,26},{3,19},{4,28},{5,21},{6,30},{7,23},{8,16},{9,... | collective-permute-start | bytes 1572872 | tf_op jit(solution)/shard_map/ppermute | solution.py:74
  65.3 0.1 slice_add_fusion.4
  65.5 0.7 collective-permute-start.8
  66.1 6.2 %back_end.1.refs_6_ = f32[8,16,128]{2,1,0:T(8,128)S(1)} custom-call(bf16[512,768]{1,0:T(8,128)(2,1)S(1)} %copy-done, bf16[512,768]{1,0:T(8,128)(2,1)S(1)} %copy-done.1, bf16[4096,768]{1,0:T(8,128)(2,1)S(1)} %bitcast.7, bf16[1024,4096]{1,0:T(8,128)(2,1)S(1)} %bitcast.3, f32[8,512,512]{2,1,0:T(8,128)S(1)} %bitcast.5, f32[512,1024]{1,0:T(8,128)S(1)} %back_begin.1.rest_0_, ...), custom_call_target="tpu_custom_call" | custom-call | flops 5368709120 | bytes 28837888 | tf_op jit(solution)/shard_map/back_end/pallas_call | solution.py:87
  72.3 0.0 collective-permute-done.10
  72.3 0.2 collective-permute-done.9
  72.5 3.4 %collective-permute-done.8 = f32[1024,128]{1,0:T(8,128)S(1)} collective-permute-done((f32[1024,128]{1,0:T(8,128)S(1)}, f32[1024,128]{1,0:T(8,128)S(1)}, u32[]{:S(2)}, u32[]{:S(2)}) %collective-permute-start.8) | collective-permute-done | bytes 524320 | tf_op jit(solution)/shard_map/ppermute | solution.py:74
  75.9 0.1 slice_add_fusion.6
  76.0 0.7 collective-permute-start.13
  76.7 0.1 slice_add_fusion.7
  76.7 0.2 collective-permute-start.12
  77.0 0.1 slice_add_fusion.8
  77.0 1.1 %collective-permute-start.11 = (f32[512,128]{1,0:T(8,128)S(1)}, f32[512,128]{1,0:T(8,128)S(1)}, u32[]{:S(2)}, u32[]{:S(2)}) collective-permute-start(f32[512,128]{1,0:T(8,128)S(1)} %get-tuple-element.82), channel_id=1, source_target_pairs={{0,24},{1,17},{2,26},{3,19},{4,28},{5,21},{6,30},{7,23},{8,16},{9,... | collective-permute-start | bytes 786440 | tf_op jit(solution)/shard_map/ppermute | solution.py:74
  78.1 0.0 collective-permute-start.14
  78.2 1.3 %collective-permute-done.14.refs_7_ = f32[8,16,128]{2,1,0:T(8,128)S(1)} collective-permute-done((f32[8,16,128]{2,1,0:T(8,128)S(1)}, f32[8,16,128]{2,1,0:T(8,128)S(1)}, u32[]{:S(2)}, u32[]{:S(2)}) %collective-permute-start.14) | collective-permute-done | bytes 65568 | tf_op jit(solution)/shard_map/ppermute | solution.py:78
  79.4 4.2 %collective-permute-done.13.refs_5_ = f32[512,128]{1,0:T(8,128)S(1)} collective-permute-done((f32[512,128]{1,0:T(8,128)S(1)}, f32[512,128]{1,0:T(8,128)S(1)}, u32[]{:S(2)}, u32[]{:S(2)}) %collective-permute-start.13) | collective-permute-done | bytes 262176 | tf_op jit(solution)/shard_map/ppermute | solution.py:74
  83.6 0.0 collective-permute-done.12.refs_4_
  83.6 1.1 %collective-permute-done.11.refs_3_ = f32[512,128]{1,0:T(8,128)S(1)} collective-permute-done((f32[512,128]{1,0:T(8,128)S(1)}, f32[512,128]{1,0:T(8,128)S(1)}, u32[]{:S(2)}, u32[]{:S(2)}) %collective-permute-start.11) | collective-permute-done | bytes 262176 | tf_op jit(solution)/shard_map/ppermute | solution.py:74
  84.7 0.1 pack.1
  84.8 13.0 %all_to_all.10.got_ref = f32[8,224,128]{2,1,0:T(8,128)S(1)} all-to-all(f32[8,224,128]{2,1,0:T(8,128)S(1)} %pack.1), channel_id=1, replica_groups={{0,16,32,48,64,80,96,112},{8,24,40,56,72,88,104,120},{2,18,34,50,66,82,..., dimensions={0} | all-to-all | bytes 1835008 | tf_op jit(solution)/shard_map/all_to_all | solution.py:432
  97.9 0.1 collective-permute-start.15
  98.0 1.3 %collective-permute-done.15.given_ref = f32[224,128]{1,0:T(8,128)S(1)} collective-permute-done((f32[224,128]{1,0:T(8,128)S(1)}, f32[224,128]{1,0:T(8,128)S(1)}, u32[]{:S(2)}, u32[]{:S(2)}) %collective-permute-start.15) | collective-permute-done | bytes 114720 | tf_op jit(solution)/shard_map/ppermute | solution.py:78
  99.3 0.7 place_blocks.1
  (17 shorter events, 0.1 us)
Async XLA Ops:
  2.3 12.5 %all-to-all-start = ((bf16[8,5,16,128]{3,2,1,0:T(8,128)(2,1)}), bf16[8,5,16,128]{3,2,1,0:T(8,128)(2,1)S(1)}, u32[]{:S(2)}, u32[]{:S(2)}) async-start(bf16[8,5,16,128]{3,2,1,0:T(8,128)(2,1)} %gather_in.1), calls=%async_computation | async-start | bytes 327680 | tf_op jit(solution)/shard_map/all_to_all | solution.py:371
  10.5 19.4 %copy-start.5 = (bf16[16,768]{1,0:T(8,128)(2,1)S(1)}, bf16[16,768]{1,0:T(8,128)(2,1)}, u32[]{:S(2)}) copy-start(bf16[16,768]{1,0:T(8,128)(2,1)} %target_ref.1) | copy-start | bytes 73732
  28.8 8.7 %copy-start.3 = (bf16[1024,512]{1,0:T(8,128)(2,1)}, bf16[1024,512]{1,0:T(8,128)(2,1)S(1)}, u32[]{:S(2)}) copy-start(bf16[1024,512]{1,0:T(8,128)(2,1)S(1)} %get-tuple-element.47.refs_5_.refs_4_) | copy-start | bytes 3145732
  28.8 10.9 %collective-permute-start.1 = (bf16[1024,512]{1,0:T(8,128)(2,1)S(1)}, bf16[1024,512]{1,0:T(8,128)(2,1)S(1)}, u32[]{:S(2)}, u32[]{:S(2)}) collective-permute-start(bf16[1024,512]{1,0:T(8,128)(2,1)S(1)} %get-tuple-element.44.refs_2_.refs_1_), channel_id=1, source_target_pairs={{0,1},{1,0},{2,3},{3,2},{4,5},{5,4},{6,7},{7,6},{8,9},{9,8},{10,11... | collective-permute-start | bytes 3145736 | tf_op jit(solution)/shard_map/ppermute | solution.py:78
  28.9 10.8 %collective-permute-start.2 = (bf16[1024,512]{1,0:T(8,128)(2,1)S(1)}, bf16[1024,512]{1,0:T(8,128)(2,1)S(1)}, u32[]{:S(2)}, u32[]{:S(2)}) collective-permute-start(bf16[1024,512]{1,0:T(8,128)(2,1)S(1)} %get-tuple-element.45.refs_3_.refs_2_), channel_id=1, source_target_pairs={{0,1},{1,0},{2,3},{3,2},{4,5},{5,4},{6,7},{7,6},{8,9},{9,8},{10,11... | collective-permute-start | bytes 3145736 | tf_op jit(solution)/shard_map/ppermute | solution.py:78
  29.4 10.3 %collective-permute-start.3 = (bf16[1024,512]{1,0:T(8,128)(2,1)S(1)}, bf16[1024,512]{1,0:T(8,128)(2,1)S(1)}, u32[]{:S(2)}, u32[]{:S(2)}) collective-permute-start(bf16[1024,512]{1,0:T(8,128)(2,1)S(1)} %get-tuple-element.46.refs_4_.refs_3_), channel_id=1, source_target_pairs={{0,1},{1,0},{2,3},{3,2},{4,5},{5,4},{6,7},{7,6},{8,9},{9,8},{10,11... | collective-permute-start | bytes 3145736 | tf_op jit(solution)/shard_map/ppermute | solution.py:78
  29.5 10.2 %collective-permute-start.4 = (bf16[1024,512]{1,0:T(8,128)(2,1)S(1)}, bf16[1024,512]{1,0:T(8,128)(2,1)S(1)}, u32[]{:S(2)}, u32[]{:S(2)}) collective-permute-start(bf16[1024,512]{1,0:T(8,128)(2,1)S(1)} %get-tuple-element.47.refs_5_.refs_4_), channel_id=1, source_target_pairs={{0,1},{1,0},{2,3},{3,2},{4,5},{5,4},{6,7},{7,6},{8,9},{9,8},{10,11... | collective-permute-start | bytes 3145736 | tf_op jit(solution)/shard_map/ppermute | solution.py:78
  29.9 18.5 %slice-start = ((s8[8388608]{0:T(1024)(128)(4,1)}), s8[4194304]{0:T(1024)(128)(4,1)S(1)}, s32[]{:S(2)}) async-start(s8[8388608]{0:T(1024)(128)(4,1)} %bitcast.2), calls=%async_computation.2 | async-start | bytes 8388608
  29.9 18.5 %slice-start.2 = ((s8[8388608]{0:T(1024)(128)(4,1)}), s8[4194304]{0:T(1024)(128)(4,1)S(1)}, s32[]{:S(2)}) async-start(s8[8388608]{0:T(1024)(128)(4,1)} %bitcast.4), calls=%async_computation.4 | async-start | bytes 8388608
  29.9 18.5 %slice-start.1 = ((s8[8388608]{0:T(1024)(128)(4,1)}), s8[4194304]{0:T(1024)(128)(4,1)S(1)}, s32[]{:S(2)}) async-start(s8[8388608]{0:T(1024)(128)(4,1)} %bitcast.2), calls=%async_computation.3 | async-start | bytes 8388608
  29.9 18.5 %slice-start.3 = ((s8[8388608]{0:T(1024)(128)(4,1)}), s8[4194304]{0:T(1024)(128)(4,1)S(1)}, s32[]{:S(2)}) async-start(s8[8388608]{0:T(1024)(128)(4,1)} %bitcast.4), calls=%async_computation.5 | async-start | bytes 8388608
  37.3 2.4 %collective-permute-start = (bf16[512,768]{1,0:T(8,128)(2,1)S(1)}, bf16[512,768]{1,0:T(8,128)(2,1)S(1)}, u32[]{:S(2)}, u32[]{:S(2)}) collective-permute-start(bf16[512,768]{1,0:T(8,128)(2,1)S(1)} %get-tuple-element.43), channel_id=1, source_target_pairs={{0,1},{1,0},{2,3},{3,2},{4,5},{5,4},{6,7},{7,6},{8,9},{9,8},{10,11... | collective-permute-start | bytes 2359304 | tf_op jit(solution)/shard_map/ppermute | solution.py:78
  37.5 10.9 %slice-start.4 = ((s8[6291456]{0:T(1024)(128)(4,1)}), s8[4194304]{0:T(1024)(128)(4,1)S(1)}, s32[]{:S(2)}) async-start(s8[6291456]{0:T(1024)(128)(4,1)} %bitcast.6), calls=%async_computation.6 | async-start | bytes 8388608
  37.5 10.9 %copy-start = (bf16[512,768]{1,0:T(8,128)(2,1)S(1)}, bf16[512,768]{1,0:T(8,128)(2,1)}, u32[]{:S(2)}) copy-start(bf16[512,768]{1,0:T(8,128)(2,1)} %get-tuple-element.55.high_ref) | copy-start | bytes 2359300
  37.5 10.9 %copy-start.1 = (bf16[512,768]{1,0:T(8,128)(2,1)S(1)}, bf16[512,768]{1,0:T(8,128)(2,1)}, u32[]{:S(2)}) copy-start(bf16[512,768]{1,0:T(8,128)(2,1)} %get-tuple-element.56.low_ref) | copy-start | bytes 2359300
  39.7 8.7 %slice-start.5 = ((s8[6291456]{0:T(1024)(128)(4,1)}), s8[2097152]{0:T(1024)(128)(4,1)S(1)}, s32[]{:S(2)}) async-start(s8[6291456]{0:T(1024)(128)(4,1)} %bitcast.6), calls=%async_computation.7 | async-start | bytes 4194304
  41.5 16.1 %collective-permute-start.5 = (f32[2048,128]{1,0:T(8,128)S(1)}, f32[2048,128]{1,0:T(8,128)S(1)}, u32[]{:S(2)}, u32[]{:S(2)}) collective-permute-start(f32[2048,128]{1,0:T(8,128)S(1)} %get-tuple-element.52), channel_id=1, source_target_pairs={{0,2},{1,33},{2,0},{3,35},{4,6},{5,37},{6,4},{7,39},{8,10},{9,41},... | collective-permute-start | bytes 3145736 | tf_op jit(solution)/shard_map/ppermute | solution.py:74
  43.1 16.0 %collective-permute-start.6 = (f32[2048,128]{1,0:T(8,128)S(1)}, f32[2048,128]{1,0:T(8,128)S(1)}, u32[]{:S(2)}, u32[]{:S(2)}) collective-permute-start(f32[2048,128]{1,0:T(8,128)S(1)} %get-tuple-element.53), channel_id=1, source_target_pairs={{0,6},{1,97},{2,4},{3,99},{4,2},{5,101},{6,0},{7,103},{8,14},{9,10... | collective-permute-start | bytes 3145736 | tf_op jit(solution)/shard_map/ppermute | solution.py:74
  45.2 16.0 %collective-permute-start.7 = (f32[2048,128]{1,0:T(8,128)S(1)}, f32[2048,128]{1,0:T(8,128)S(1)}, u32[]{:S(2)}, u32[]{:S(2)}) collective-permute-start(f32[2048,128]{1,0:T(8,128)S(1)} %get-tuple-element.54), channel_id=1, source_target_pairs={{0,24},{1,17},{2,26},{3,19},{4,28},{5,21},{6,30},{7,23},{8,16},{9,... | collective-permute-start | bytes 3145736 | tf_op jit(solution)/shard_map/ppermute | solution.py:74
  48.4 5.7 %copy-start.4 = (bf16[1024,512]{1,0:T(8,128)(2,1)S(1)}, bf16[1024,512]{1,0:T(8,128)(2,1)}, u32[]{:S(2)}) copy-start(bf16[1024,512]{1,0:T(8,128)(2,1)} %copy-done.3) | copy-start | bytes 3145732
  57.6 8.6 %copy-start.2 = (f32[512,1024]{1,0:T(8,128)S(1)}, f32[512,1024]{1,0:T(8,128)}, u32[]{:S(2)}) copy-start(f32[512,1024]{1,0:T(8,128)} %get-tuple-element.64.rest_1_) | copy-start | bytes 6291460
  61.3 11.1 %collective-permute-start.10 = (f32[1024,128]{1,0:T(8,128)S(1)}, f32[1024,128]{1,0:T(8,128)S(1)}, u32[]{:S(2)}, u32[]{:S(2)}) collective-permute-start(f32[1024,128]{1,0:T(8,128)S(1)} %get-tuple-element.73), channel_id=1, source_target_pairs={{0,2},{1,33},{2,0},{3,35},{4,6},{5,37},{6,4},{7,39},{8,10},{9,41},... | collective-permute-start | bytes 1572872 | tf_op jit(solution)/shard_map/ppermute | solution.py:74
  62.1 10.5 %collective-permute-start.9 = (f32[1024,128]{1,0:T(8,128)S(1)}, f32[1024,128]{1,0:T(8,128)S(1)}, u32[]{:S(2)}, u32[]{:S(2)}) collective-permute-start(f32[1024,128]{1,0:T(8,128)S(1)} %get-tuple-element.75), channel_id=1, source_target_pairs={{0,24},{1,17},{2,26},{3,19},{4,28},{5,21},{6,30},{7,23},{8,16},{9,... | collective-permute-start | bytes 1572872 | tf_op jit(solution)/shard_map/ppermute | solution.py:74
  65.5 10.5 %collective-permute-start.8 = (f32[1024,128]{1,0:T(8,128)S(1)}, f32[1024,128]{1,0:T(8,128)S(1)}, u32[]{:S(2)}, u32[]{:S(2)}) collective-permute-start(f32[1024,128]{1,0:T(8,128)S(1)} %get-tuple-element.76), channel_id=1, source_target_pairs={{0,6},{1,97},{2,4},{3,99},{4,2},{5,101},{6,0},{7,103},{8,14},{9,10... | collective-permute-start | bytes 1572872 | tf_op jit(solution)/shard_map/ppermute | solution.py:74
  76.0 7.7 %collective-permute-start.13 = (f32[512,128]{1,0:T(8,128)S(1)}, f32[512,128]{1,0:T(8,128)S(1)}, u32[]{:S(2)}, u32[]{:S(2)}) collective-permute-start(f32[512,128]{1,0:T(8,128)S(1)} %get-tuple-element.78), channel_id=1, source_target_pairs={{0,6},{1,97},{2,4},{3,99},{4,2},{5,101},{6,0},{7,103},{8,14},{9,10... | collective-permute-start | bytes 786440 | tf_op jit(solution)/shard_map/ppermute | solution.py:74
  76.7 6.9 %collective-permute-start.12 = (f32[512,128]{1,0:T(8,128)S(1)}, f32[512,128]{1,0:T(8,128)S(1)}, u32[]{:S(2)}, u32[]{:S(2)}) collective-permute-start(f32[512,128]{1,0:T(8,128)S(1)} %get-tuple-element.80), channel_id=1, source_target_pairs={{0,2},{1,33},{2,0},{3,35},{4,6},{5,37},{6,4},{7,39},{8,10},{9,41},... | collective-permute-start | bytes 786440 | tf_op jit(solution)/shard_map/ppermute | solution.py:74
  77.0 7.7 %collective-permute-start.11 = (f32[512,128]{1,0:T(8,128)S(1)}, f32[512,128]{1,0:T(8,128)S(1)}, u32[]{:S(2)}, u32[]{:S(2)}) collective-permute-start(f32[512,128]{1,0:T(8,128)S(1)} %get-tuple-element.82), channel_id=1, source_target_pairs={{0,24},{1,17},{2,26},{3,19},{4,28},{5,21},{6,30},{7,23},{8,16},{9,... | collective-permute-start | bytes 786440 | tf_op jit(solution)/shard_map/ppermute | solution.py:74
  78.1 1.3 %collective-permute-start.14 = (f32[8,16,128]{2,1,0:T(8,128)S(1)}, f32[8,16,128]{2,1,0:T(8,128)S(1)}, u32[]{:S(2)}, u32[]{:S(2)}) collective-permute-start(f32[8,16,128]{2,1,0:T(8,128)S(1)} %back_end.1.refs_6_), channel_id=1, source_target_pairs={{0,1},{1,0},{2,3},{3,2},{4,5},{5,4},{6,7},{7,6},{8,9},{9,8},{10,11... | collective-permute-start | bytes 196616 | tf_op jit(solution)/shard_map/ppermute | solution.py:78
  97.9 1.4 %collective-permute-start.15 = (f32[224,128]{1,0:T(8,128)S(1)}, f32[224,128]{1,0:T(8,128)S(1)}, u32[]{:S(2)}, u32[]{:S(2)}) collective-permute-start(f32[224,128]{1,0:T(8,128)S(1)} %get-tuple-element.70), channel_id=1, source_target_pairs={{0,1},{1,0},{2,3},{3,2},{4,5},{5,4},{6,7},{7,6},{8,9},{9,8},{10,11... | collective-permute-start | bytes 344072 | tf_op jit(solution)/shard_map/ppermute | solution.py:78

commit v6 on v5

--- a/solution.py
+++ b/solution.py
@@ -414,13 +414,14 @@
     came = [swap_stage(send[part], part, 0) for part in range(3)]
     keep = make_outer("outer_keep", 0, device, (own, got), (turned, theirs))
     begun = make_back(0, high, low, w_out, w_in, slope)
-    *came, begun = lax.optimization_barrier((*came, begun))
+    came[2], begun = lax.optimization_barrier((came[2], begun))
 
     send = [keep[part][1024:] + came[part][1024:] for part in range(3)]
     after = [swap_stage(send[part], part, 1) for part in range(3)]
     keep = [keep[part][:1024] + came[part][:1024] for part in range(3)]
     latent = make_back(STEPS // 2, high, low, w_out, w_in, slope, begun, cond, gain)
-    *came, latent = lax.optimization_barrier((*after, latent))
+    came = after
+    came[2], latent = lax.optimization_barrier((came[2], latent))
 
     send = [keep[part][512:] + came[part][512:] for part in range(3)]
     after = [swap_stage(send[part], part, 2) for part in range(3)]

time: 101 us -> 99 us (0.980)
  waiting for transfers between devices: 19.6 us -> 15.4 us
  starting transfers between devices: 20.8 us -> 23.3 us
    ppermute x9, waiting for transfers between devices: 12.5 us -> 7.57 us  [swap_stage(): return lax.ppermute(values, AXES, pairs)]
    ppermute x9, starting transfers between devices: 13.5 us -> 16.1 us  [swap_stage(): return lax.ppermute(values, AXES, pairs)]
  transfers between devices with their start and end apart: 17 -> 17, of which waited for: 10 -> 8; matrix products, arithmetic and copies ran while one was open for 1% -> 1% of each run, Pallas kernels for 26% -> 27%
where the time goes in v6:
time: 99 us; the launch traced here: 97.6 us
  Pallas kernels  44.3 us (45%)
  starting transfers between devices  23.3 us (24%)
  waiting for transfers between devices  15.4 us (16%)
  blocking collectives  13 us (13%)
    pallas_call x12, Pallas kernels, call(): pl.pallas_call(body, in_specs=[pl.BlockSpec(memory_space=kinds[space]) fo...  44.3 us
    ppermute x9, starting transfers between devices, swap_stage(): return lax.ppermute(values, AXES, pairs)  16.1 us
    all_to_all x1, blocking collectives, per_device(): lax.all_to_all(packed, AXES, split_axis=0, concat_axis=0, tiled=True, axi...  13 us
    ppermute x9, waiting for transfers between devices, swap_stage(): return lax.ppermute(values, AXES, pairs)  7.57 us
    all_to_all x1, starting transfers between devices, per_device(): lax.all_to_all(moved, 'member', split_axis=0, concat_axis=0, tiled=True)  5.92 us
    all_to_all x1, waiting for transfers between devices, per_device(): lax.all_to_all(moved, 'member', split_axis=0, concat_axis=0, tiled=True)  4.9 us
    ppermute x7, waiting for transfers between devices, swap_core(): return lax.ppermute(values, AXES, [(i, i ^ 1) for i in range(128)])  2.94 us
  transfers between devices with their start and end apart: 17, of which 8 were waited for; matrix products, arithmetic and copies ran while one was open for 1% of the time, Pallas kernels for 27%

profile of v6, /device:TPU:0, one launch (start us, length us, event | category | flops | bytes accessed | tf_op | source)
XLA Modules:
  0.0 97.6 jit_solution(3704525307953441209)
XLA Ops:
  0.6 0.0 copy-start.6
  0.7 1.6 %gather_in.1 = bf16[8,5,16,128]{3,2,1,0:T(8,128)(2,1)} custom-call(bf16[4,128,128]{2,1,0:T(8,128)(2,1)} %noise_hbm, bf16[128,128]{1,0:T(8,128)(2,1)} %latents_hbm), custom_call_target="tpu_custom_call" | custom-call | bytes 163840 | tf_op jit(solution)/shard_map/gather_in/pallas_call | solution.py:87
  2.3 5.9 %all-to-all-start = ((bf16[8,5,16,128]{3,2,1,0:T(8,128)(2,1)}), bf16[8,5,16,128]{3,2,1,0:T(8,128)(2,1)S(1)}, u32[]{:S(2)}, u32[]{:S(2)}) async-start(bf16[8,5,16,128]{3,2,1,0:T(8,128)(2,1)} %gather_in.1), calls=%async_computation | async-start | bytes 327680 | tf_op jit(solution)/shard_map/all_to_all | solution.py:371
  8.2 1.6 %fetch_near.1.near_ref = bf16[1024,1024]{1,0:T(8,128)(2,1)S(1)} custom-call(bf16[1024,4096]{1,0:T(8,128)(2,1)} %w_in_ref.3), custom_call_target="tpu_custom_call" | custom-call | bytes 8388608 | tf_op jit(solution)/shard_map/fetch_near/pallas_call | solution.py:87
  9.8 0.0 copy-done.6
  9.8 0.0 copy-start.5
  9.8 4.9 %all-to-all-done.moved_ref = bf16[8,5,16,128]{3,2,1,0:T(8,128)(2,1)S(1)} async-done(((bf16[8,5,16,128]{3,2,1,0:T(8,128)(2,1)}), bf16[8,5,16,128]{3,2,1,0:T(8,128)(2,1)S(1)}, u32[]{:S(2)}, u32[]{:S(2)}) %all-to-all-start) | async-done | bytes 163872 | tf_op jit(solution)/shard_map/all_to_all | solution.py:371
  14.7 14.0 %forward_rows.1 = (f32[512,1024]{1,0:T(8,128)}, f32[8,512,512]{2,1,0:T(8,128)}, bf16[512,768]{1,0:T(8,128)(2,1)S(1)}, bf16[1024,512]{1,0:T(8,128)(2,1)S(1)}, bf1...) custom-call(bf16[8,5,16,128]{3,2,1,0:T(8,128)(2,1)S(1)} %all-to-all-done.moved_ref, ...), custom_call_target="tpu_custom_call" | custom-call | flops 7516192768 | bytes 17205248 | tf_op jit(solution)/shard_map/forward_rows/pallas_call | solution.py:87
  28.8 0.0 copy-start.3
  28.8 0.1 collective-permute-start.1
  28.9 0.5 collective-permute-start.2
  29.4 0.1 collective-permute-start.3
  29.5 0.4 collective-permute-start.4
  29.9 0.0 copy-done.5
  29.9 0.0 slice-start.3
  29.9 7.4 %score_rows.1 = (bf16[512,768]{1,0:T(8,128)(2,1)}, bf16[512,768]{1,0:T(8,128)(2,1)}, bf16[512,768]{1,0:T(8,128)(2,1)S(1)}, bf16[512,768]{1,0:T(8,128)(2,1)S(1)}) custom-call(s32[1]{0:T(128)} %bitcast.1.core_ref, bf16[512,768]{1,0:T(8,128)(2,1)S(1)} %get-tuple-element.37.pred_in_ref, bf16[16,768]{1,0:T(8,128)(2,1)S(1)} %copy-done.5), custom_call_target="tpu_custom_call" | custom-call | flops 4294967296 | bytes 811012 | tf_op jit(solution)/shard_map/score_rows/pallas_call | solution.py:87
  37.3 0.2 collective-permute-start
  37.5 0.0 copy-done.3
  37.5 1.8 %outer_own.1 = (f32[2048,128]{1,0:T(8,128)S(1)}, f32[2048,128]{1,0:T(8,128)S(1)}, f32[2048,128]{1,0:T(8,128)S(1)}) custom-call(s32[1]{0:T(128)} %bitcast.device_ref, bf16[512,768]{1,0:T(8,128)(2,1)S(1)} %get-tuple-element.38.refs_0_, bf16[1024,512]{1,0:T(8,128)(2,1)S(1)} %get-tuple-element.40.refs_2_.refs_1_, ...), custom_call_target="tpu_custom_call" | custom-call | flops 1610612736 | bytes 4980740 | tf_op jit(solution)/shard_map/outer_own/pallas_call | solution.py:87
  39.3 0.4 collective-permute-done.refs_1_.refs_0_
  39.6 0.0 collective-permute-done.1.refs_6_.refs_1_
  39.6 0.0 collective-permute-done.2.refs_7_.refs_2_
  39.7 0.0 collective-permute-done.3.refs_8_.refs_3_
  39.7 0.0 collective-permute-done.4.refs_9_.refs_4_
  39.7 0.0 slice-start.5
  39.7 1.8 %outer_send.1 = (f32[2048,128]{1,0:T(8,128)S(1)}, f32[2048,128]{1,0:T(8,128)S(1)}, f32[2048,128]{1,0:T(8,128)S(1)}) custom-call(s32[1]{0:T(128)} %bitcast.device_ref, bf16[512,768]{1,0:T(8,128)(2,1)S(1)} %collective-permute-done.refs_1_.refs_0_, bf16[1024,512]{1,0:T(8,128)(2,1)S(1)} %collective-permute-done.1.refs_6_.refs_1_, ...), custom_call_target="tpu_custom_call" | custom-call | flops 1610612736 | bytes 8126468 | tf_op jit(solution)/shard_map/outer_send/pallas_call | solution.py:87
  41.5 1.6 %collective-permute-start.5 = (f32[2048,128]{1,0:T(8,128)S(1)}, f32[2048,128]{1,0:T(8,128)S(1)}, u32[]{:S(2)}, u32[]{:S(2)}) collective-permute-start(f32[2048,128]{1,0:T(8,128)S(1)} %get-tuple-element.48), channel_id=1, source_target_pairs={{0,2},{1,33},{2,0},{3,35},{4,6},{5,37},{6,4},{7,39},{8,10},{9,41},... | collective-permute-start | bytes 3145736 | tf_op jit(solution)/shard_map/ppermute | solution.py:74
  43.1 2.1 %collective-permute-start.7 = (f32[2048,128]{1,0:T(8,128)S(1)}, f32[2048,128]{1,0:T(8,128)S(1)}, u32[]{:S(2)}, u32[]{:S(2)}) collective-permute-start(f32[2048,128]{1,0:T(8,128)S(1)} %get-tuple-element.50), channel_id=1, source_target_pairs={{0,6},{1,97},{2,4},{3,99},{4,2},{5,101},{6,0},{7,103},{8,14},{9,10... | collective-permute-start | bytes 3145736 | tf_op jit(solution)/shard_map/ppermute | solution.py:74
  45.2 3.2 %collective-permute-start.9 = (f32[2048,128]{1,0:T(8,128)S(1)}, f32[2048,128]{1,0:T(8,128)S(1)}, u32[]{:S(2)}, u32[]{:S(2)}) collective-permute-start(f32[2048,128]{1,0:T(8,128)S(1)} %get-tuple-element.52), channel_id=1, source_target_pairs={{0,24},{1,17},{2,26},{3,19},{4,28},{5,21},{6,30},{7,23},{8,16},{9,... | collective-permute-start | bytes 3145736 | tf_op jit(solution)/shard_map/ppermute | solution.py:74
  48.3 0.0 slice-done
  48.4 0.0 slice-done.2
  48.4 0.0 slice-done.1
  48.4 5.7 %back_begin.1.rest_0_ = f32[512,1024]{1,0:T(8,128)S(1)} custom-call(bf16[512,768]{1,0:T(8,128)(2,1)S(1)} %copy-done, bf16[512,768]{1,0:T(8,128)(2,1)S(1)} %copy-done.1, bf16[4096,768]{1,0:T(8,128)(2,1)S(1)} %bitcast.7, bf16[1024,4096]{1,0:T(8,128)(2,1)S(1)} %bitcast.3, f32[8,512,512]{2,1,0:T(8,128)S(1)} %bitcast.5), custom_call_target="tpu_custom_call" | custom-call | flops 5368709120 | bytes 24641536 | tf_op jit(solution)/shard_map/back_begin/pallas_call | solution.py:87
  54.1 3.4 %outer_keep.1 = (f32[2048,128]{1,0:T(8,128)S(1)}, f32[2048,128]{1,0:T(8,128)S(1)}, f32[2048,128]{1,0:T(8,128)S(1)}) custom-call(s32[1]{0:T(128)} %bitcast.device_ref, bf16[512,768]{1,0:T(8,128)(2,1)S(1)} %get-tuple-element.38.refs_0_, bf16[512,768]{1,0:T(8,128)(2,1)S(1)} %collective-permute-done.refs_1_.refs_0_, ...), custom_call_target="tpu_custom_call" | custom-call | flops 3221225472 | bytes 9961476 | tf_op jit(solution)/shard_map/outer_keep/pallas_call | solution.py:87
  57.6 0.0 copy-start.2
  57.6 0.0 collective-permute-done.5
  57.6 0.1 slice_add_fusion.3
  57.7 1.6 %collective-permute-start.6 = (f32[1024,128]{1,0:T(8,128)S(1)}, f32[1024,128]{1,0:T(8,128)S(1)}, u32[]{:S(2)}, u32[]{:S(2)}) collective-permute-start(f32[1024,128]{1,0:T(8,128)S(1)} %get-tuple-element.69), channel_id=1, source_target_pairs={{0,6},{1,97},{2,4},{3,99},{4,2},{5,101},{6,0},{7,103},{8,14},{9,10... | collective-permute-start | bytes 1572872 | tf_op jit(solution)/shard_map/ppermute | solution.py:74
  59.3 1.8 %collective-permute-done.9 = f32[2048,128]{1,0:T(8,128)S(1)} collective-permute-done((f32[2048,128]{1,0:T(8,128)S(1)}, f32[2048,128]{1,0:T(8,128)S(1)}, u32[]{:S(2)}, u32[]{:S(2)}) %collective-permute-start.9) | collective-permute-done | bytes 1048608 | tf_op jit(solution)/shard_map/ppermute | solution.py:74
  61.2 0.1 slice_add_fusion.4
  61.3 0.7 collective-permute-start.10
  62.0 0.0 collective-permute-done.7
  62.0 0.1 slice_add_fusion.1
  62.1 3.3 %collective-permute-start.8 = (f32[1024,128]{1,0:T(8,128)S(1)}, f32[1024,128]{1,0:T(8,128)S(1)}, u32[]{:S(2)}, u32[]{:S(2)}) collective-permute-start(f32[1024,128]{1,0:T(8,128)S(1)} %get-tuple-element.67), channel_id=1, source_target_pairs={{0,24},{1,17},{2,26},{3,19},{4,28},{5,21},{6,30},{7,23},{8,16},{9,... | collective-permute-start | bytes 1572872 | tf_op jit(solution)/shard_map/ppermute | solution.py:74
  65.3 6.2 %back_end.1.refs_6_ = f32[8,16,128]{2,1,0:T(8,128)S(1)} custom-call(bf16[512,768]{1,0:T(8,128)(2,1)S(1)} %copy-done, bf16[512,768]{1,0:T(8,128)(2,1)S(1)} %copy-done.1, bf16[4096,768]{1,0:T(8,128)(2,1)S(1)} %bitcast.7, bf16[1024,4096]{1,0:T(8,128)(2,1)S(1)} %bitcast.3, f32[8,512,512]{2,1,0:T(8,128)S(1)} %bitcast.5, f32[512,1024]{1,0:T(8,128)S(1)} %back_begin.1.rest_0_, ...), custom_call_target="tpu_custom_call" | custom-call | flops 5368709120 | bytes 28837888 | tf_op jit(solution)/shard_map/back_end/pallas_call | solution.py:87
  71.5 0.0 collective-permute-done.10
  71.5 0.0 collective-permute-done.6
  71.6 0.1 slice_add_fusion.8
  71.6 2.3 %collective-permute-start.11 = (f32[512,128]{1,0:T(8,128)S(1)}, f32[512,128]{1,0:T(8,128)S(1)}, u32[]{:S(2)}, u32[]{:S(2)}) collective-permute-start(f32[512,128]{1,0:T(8,128)S(1)} %get-tuple-element.74), channel_id=1, source_target_pairs={{0,24},{1,17},{2,26},{3,19},{4,28},{5,21},{6,30},{7,23},{8,16},{9,... | collective-permute-start | bytes 786440 | tf_op jit(solution)/shard_map/ppermute | solution.py:74
  73.9 0.0 collective-permute-done.8
  73.9 0.1 slice_add_fusion.7
  74.0 0.7 collective-permute-start.12
  74.6 0.1 slice_add_fusion.6
  74.7 0.7 collective-permute-start.13
  75.4 0.0 collective-permute-start.14
  75.4 1.3 %collective-permute-done.14.refs_7_ = f32[8,16,128]{2,1,0:T(8,128)S(1)} collective-permute-done((f32[8,16,128]{2,1,0:T(8,128)S(1)}, f32[8,16,128]{2,1,0:T(8,128)S(1)}, u32[]{:S(2)}, u32[]{:S(2)}) %collective-permute-start.14) | collective-permute-done | bytes 65568 | tf_op jit(solution)/shard_map/ppermute | solution.py:78
  76.6 2.7 %collective-permute-done.11.refs_3_ = f32[512,128]{1,0:T(8,128)S(1)} collective-permute-done((f32[512,128]{1,0:T(8,128)S(1)}, f32[512,128]{1,0:T(8,128)S(1)}, u32[]{:S(2)}, u32[]{:S(2)}) %collective-permute-start.11) | collective-permute-done | bytes 262176 | tf_op jit(solution)/shard_map/ppermute | solution.py:74
  79.3 1.1 %collective-permute-done.12.refs_4_ = f32[512,128]{1,0:T(8,128)S(1)} collective-permute-done((f32[512,128]{1,0:T(8,128)S(1)}, f32[512,128]{1,0:T(8,128)S(1)}, u32[]{:S(2)}, u32[]{:S(2)}) %collective-permute-start.12) | collective-permute-done | bytes 262176 | tf_op jit(solution)/shard_map/ppermute | solution.py:74
  80.4 2.0 %collective-permute-done.13.refs_5_ = f32[512,128]{1,0:T(8,128)S(1)} collective-permute-done((f32[512,128]{1,0:T(8,128)S(1)}, f32[512,128]{1,0:T(8,128)S(1)}, u32[]{:S(2)}, u32[]{:S(2)}) %collective-permute-start.13) | collective-permute-done | bytes 262176 | tf_op jit(solution)/shard_map/ppermute | solution.py:74
  82.4 0.1 pack.1
  82.5 13.0 %all_to_all.10.got_ref = f32[8,224,128]{2,1,0:T(8,128)S(1)} all-to-all(f32[8,224,128]{2,1,0:T(8,128)S(1)} %pack.1), channel_id=1, replica_groups={{0,16,32,48,64,80,96,112},{8,24,40,56,72,88,104,120},{2,18,34,50,66,82,..., dimensions={0} | all-to-all | bytes 1835008 | tf_op jit(solution)/shard_map/all_to_all | solution.py:433
  95.5 0.1 collective-permute-start.15
  95.6 1.3 %collective-permute-done.15.given_ref = f32[224,128]{1,0:T(8,128)S(1)} collective-permute-done((f32[224,128]{1,0:T(8,128)S(1)}, f32[224,128]{1,0:T(8,128)S(1)}, u32[]{:S(2)}, u32[]{:S(2)}) %collective-permute-start.15) | collective-permute-done | bytes 114720 | tf_op jit(solution)/shard_map/ppermute | solution.py:78
  96.9 0.7 place_blocks.1
  (19 shorter events, 0.1 us)
Async XLA Ops:
  0.6 9.2 %copy-start.6 = (bf16[1024]{0:T(1024)(128)(2,1)S(1)}, bf16[1024]{0:T(1024)(128)(2,1)}, u32[]{:S(2)}) copy-start(bf16[1024]{0:T(1024)(128)(2,1)} %param.10) | copy-start | bytes 6148
  2.3 12.5 %all-to-all-start = ((bf16[8,5,16,128]{3,2,1,0:T(8,128)(2,1)}), bf16[8,5,16,128]{3,2,1,0:T(8,128)(2,1)S(1)}, u32[]{:S(2)}, u32[]{:S(2)}) async-start(bf16[8,5,16,128]{3,2,1,0:T(8,128)(2,1)} %gather_in.1), calls=%async_computation | async-start | bytes 327680 | tf_op jit(solution)/shard_map/all_to_all | solution.py:371
  9.8 20.1 %copy-start.5 = (bf16[16,768]{1,0:T(8,128)(2,1)S(1)}, bf16[16,768]{1,0:T(8,128)(2,1)}, u32[]{:S(2)}) copy-start(bf16[16,768]{1,0:T(8,128)(2,1)} %target_ref.1) | copy-start | bytes 73732
  28.8 8.7 %copy-start.3 = (bf16[1024,512]{1,0:T(8,128)(2,1)}, bf16[1024,512]{1,0:T(8,128)(2,1)S(1)}, u32[]{:S(2)}) copy-start(bf16[1024,512]{1,0:T(8,128)(2,1)S(1)} %get-tuple-element.43.refs_5_.refs_4_) | copy-start | bytes 3145732
  28.8 10.9 %collective-permute-start.1 = (bf16[1024,512]{1,0:T(8,128)(2,1)S(1)}, bf16[1024,512]{1,0:T(8,128)(2,1)S(1)}, u32[]{:S(2)}, u32[]{:S(2)}) collective-permute-start(bf16[1024,512]{1,0:T(8,128)(2,1)S(1)} %get-tuple-element.40.refs_2_.refs_1_), channel_id=1, source_target_pairs={{0,1},{1,0},{2,3},{3,2},{4,5},{5,4},{6,7},{7,6},{8,9},{9,8},{10,11... | collective-permute-start | bytes 3145736 | tf_op jit(solution)/shard_map/ppermute | solution.py:78
  28.9 10.8 %collective-permute-start.2 = (bf16[1024,512]{1,0:T(8,128)(2,1)S(1)}, bf16[1024,512]{1,0:T(8,128)(2,1)S(1)}, u32[]{:S(2)}, u32[]{:S(2)}) collective-permute-start(bf16[1024,512]{1,0:T(8,128)(2,1)S(1)} %get-tuple-element.41.refs_3_.refs_2_), channel_id=1, source_target_pairs={{0,1},{1,0},{2,3},{3,2},{4,5},{5,4},{6,7},{7,6},{8,9},{9,8},{10,11... | collective-permute-start | bytes 3145736 | tf_op jit(solution)/shard_map/ppermute | solution.py:78
  29.4 10.3 %collective-permute-start.3 = (bf16[1024,512]{1,0:T(8,128)(2,1)S(1)}, bf16[1024,512]{1,0:T(8,128)(2,1)S(1)}, u32[]{:S(2)}, u32[]{:S(2)}) collective-permute-start(bf16[1024,512]{1,0:T(8,128)(2,1)S(1)} %get-tuple-element.42.refs_4_.refs_3_), channel_id=1, source_target_pairs={{0,1},{1,0},{2,3},{3,2},{4,5},{5,4},{6,7},{7,6},{8,9},{9,8},{10,11... | collective-permute-start | bytes 3145736 | tf_op jit(solution)/shard_map/ppermute | solution.py:78
  29.5 10.2 %collective-permute-start.4 = (bf16[1024,512]{1,0:T(8,128)(2,1)S(1)}, bf16[1024,512]{1,0:T(8,128)(2,1)S(1)}, u32[]{:S(2)}, u32[]{:S(2)}) collective-permute-start(bf16[1024,512]{1,0:T(8,128)(2,1)S(1)} %get-tuple-element.43.refs_5_.refs_4_), channel_id=1, source_target_pairs={{0,1},{1,0},{2,3},{3,2},{4,5},{5,4},{6,7},{7,6},{8,9},{9,8},{10,11... | collective-permute-start | bytes 3145736 | tf_op jit(solution)/shard_map/ppermute | solution.py:78
  29.9 18.5 %slice-start = ((s8[8388608]{0:T(1024)(128)(4,1)}), s8[4194304]{0:T(1024)(128)(4,1)S(1)}, s32[]{:S(2)}) async-start(s8[8388608]{0:T(1024)(128)(4,1)} %bitcast.2), calls=%async_computation.2 | async-start | bytes 8388608
  29.9 18.5 %slice-start.2 = ((s8[8388608]{0:T(1024)(128)(4,1)}), s8[4194304]{0:T(1024)(128)(4,1)S(1)}, s32[]{:S(2)}) async-start(s8[8388608]{0:T(1024)(128)(4,1)} %bitcast.4), calls=%async_computation.4 | async-start | bytes 8388608
  29.9 18.5 %slice-start.1 = ((s8[8388608]{0:T(1024)(128)(4,1)}), s8[4194304]{0:T(1024)(128)(4,1)S(1)}, s32[]{:S(2)}) async-start(s8[8388608]{0:T(1024)(128)(4,1)} %bitcast.2), calls=%async_computation.3 | async-start | bytes 8388608
  29.9 18.5 %slice-start.3 = ((s8[8388608]{0:T(1024)(128)(4,1)}), s8[4194304]{0:T(1024)(128)(4,1)S(1)}, s32[]{:S(2)}) async-start(s8[8388608]{0:T(1024)(128)(4,1)} %bitcast.4), calls=%async_computation.5 | async-start | bytes 8388608
  37.3 2.4 %collective-permute-start = (bf16[512,768]{1,0:T(8,128)(2,1)S(1)}, bf16[512,768]{1,0:T(8,128)(2,1)S(1)}, u32[]{:S(2)}, u32[]{:S(2)}) collective-permute-start(bf16[512,768]{1,0:T(8,128)(2,1)S(1)} %get-tuple-element.39), channel_id=1, source_target_pairs={{0,1},{1,0},{2,3},{3,2},{4,5},{5,4},{6,7},{7,6},{8,9},{9,8},{10,11... | collective-permute-start | bytes 2359304 | tf_op jit(solution)/shard_map/ppermute | solution.py:78
  37.5 10.9 %slice-start.4 = ((s8[6291456]{0:T(1024)(128)(4,1)}), s8[4194304]{0:T(1024)(128)(4,1)S(1)}, s32[]{:S(2)}) async-start(s8[6291456]{0:T(1024)(128)(4,1)} %bitcast.6), calls=%async_computation.6 | async-start | bytes 8388608
  37.5 10.9 %copy-start = (bf16[512,768]{1,0:T(8,128)(2,1)S(1)}, bf16[512,768]{1,0:T(8,128)(2,1)}, u32[]{:S(2)}) copy-start(bf16[512,768]{1,0:T(8,128)(2,1)} %get-tuple-element.53.high_ref) | copy-start | bytes 2359300
  37.5 10.9 %copy-start.1 = (bf16[512,768]{1,0:T(8,128)(2,1)S(1)}, bf16[512,768]{1,0:T(8,128)(2,1)}, u32[]{:S(2)}) copy-start(bf16[512,768]{1,0:T(8,128)(2,1)} %get-tuple-element.54.low_ref) | copy-start | bytes 2359300
  39.7 8.7 %slice-start.5 = ((s8[6291456]{0:T(1024)(128)(4,1)}), s8[2097152]{0:T(1024)(128)(4,1)S(1)}, s32[]{:S(2)}) async-start(s8[6291456]{0:T(1024)(128)(4,1)} %bitcast.6), calls=%async_computation.7 | async-start | bytes 4194304
  41.5 16.1 %collective-permute-start.5 = (f32[2048,128]{1,0:T(8,128)S(1)}, f32[2048,128]{1,0:T(8,128)S(1)}, u32[]{:S(2)}, u32[]{:S(2)}) collective-permute-start(f32[2048,128]{1,0:T(8,128)S(1)} %get-tuple-element.48), channel_id=1, source_target_pairs={{0,2},{1,33},{2,0},{3,35},{4,6},{5,37},{6,4},{7,39},{8,10},{9,41},... | collective-permute-start | bytes 3145736 | tf_op jit(solution)/shard_map/ppermute | solution.py:74
  43.1 18.9 %collective-permute-start.7 = (f32[2048,128]{1,0:T(8,128)S(1)}, f32[2048,128]{1,0:T(8,128)S(1)}, u32[]{:S(2)}, u32[]{:S(2)}) collective-permute-start(f32[2048,128]{1,0:T(8,128)S(1)} %get-tuple-element.50), channel_id=1, source_target_pairs={{0,6},{1,97},{2,4},{3,99},{4,2},{5,101},{6,0},{7,103},{8,14},{9,10... | collective-permute-start | bytes 3145736 | tf_op jit(solution)/shard_map/ppermute | solution.py:74
  45.2 16.0 %collective-permute-start.9 = (f32[2048,128]{1,0:T(8,128)S(1)}, f32[2048,128]{1,0:T(8,128)S(1)}, u32[]{:S(2)}, u32[]{:S(2)}) collective-permute-start(f32[2048,128]{1,0:T(8,128)S(1)} %get-tuple-element.52), channel_id=1, source_target_pairs={{0,24},{1,17},{2,26},{3,19},{4,28},{5,21},{6,30},{7,23},{8,16},{9,... | collective-permute-start | bytes 3145736 | tf_op jit(solution)/shard_map/ppermute | solution.py:74
  48.4 5.7 %copy-start.4 = (bf16[1024,512]{1,0:T(8,128)(2,1)S(1)}, bf16[1024,512]{1,0:T(8,128)(2,1)}, u32[]{:S(2)}) copy-start(bf16[1024,512]{1,0:T(8,128)(2,1)} %copy-done.3) | copy-start | bytes 3145732
  57.6 7.8 %copy-start.2 = (f32[512,1024]{1,0:T(8,128)S(1)}, f32[512,1024]{1,0:T(8,128)}, u32[]{:S(2)}) copy-start(f32[512,1024]{1,0:T(8,128)} %get-tuple-element.58.rest_1_) | copy-start | bytes 6291460
  57.7 13.9 %collective-permute-start.6 = (f32[1024,128]{1,0:T(8,128)S(1)}, f32[1024,128]{1,0:T(8,128)S(1)}, u32[]{:S(2)}, u32[]{:S(2)}) collective-permute-start(f32[1024,128]{1,0:T(8,128)S(1)} %get-tuple-element.69), channel_id=1, source_target_pairs={{0,6},{1,97},{2,4},{3,99},{4,2},{5,101},{6,0},{7,103},{8,14},{9,10... | collective-permute-start | bytes 1572872 | tf_op jit(solution)/shard_map/ppermute | solution.py:74
  61.3 10.3 %collective-permute-start.10 = (f32[1024,128]{1,0:T(8,128)S(1)}, f32[1024,128]{1,0:T(8,128)S(1)}, u32[]{:S(2)}, u32[]{:S(2)}) collective-permute-start(f32[1024,128]{1,0:T(8,128)S(1)} %get-tuple-element.64), channel_id=1, source_target_pairs={{0,2},{1,33},{2,0},{3,35},{4,6},{5,37},{6,4},{7,39},{8,10},{9,41},... | collective-permute-start | bytes 1572872 | tf_op jit(solution)/shard_map/ppermute | solution.py:74
  62.1 11.8 %collective-permute-start.8 = (f32[1024,128]{1,0:T(8,128)S(1)}, f32[1024,128]{1,0:T(8,128)S(1)}, u32[]{:S(2)}, u32[]{:S(2)}) collective-permute-start(f32[1024,128]{1,0:T(8,128)S(1)} %get-tuple-element.67), channel_id=1, source_target_pairs={{0,24},{1,17},{2,26},{3,19},{4,28},{5,21},{6,30},{7,23},{8,16},{9,... | collective-permute-start | bytes 1572872 | tf_op jit(solution)/shard_map/ppermute | solution.py:74
  71.6 7.7 %collective-permute-start.11 = (f32[512,128]{1,0:T(8,128)S(1)}, f32[512,128]{1,0:T(8,128)S(1)}, u32[]{:S(2)}, u32[]{:S(2)}) collective-permute-start(f32[512,128]{1,0:T(8,128)S(1)} %get-tuple-element.74), channel_id=1, source_target_pairs={{0,24},{1,17},{2,26},{3,19},{4,28},{5,21},{6,30},{7,23},{8,16},{9,... | collective-permute-start | bytes 786440 | tf_op jit(solution)/shard_map/ppermute | solution.py:74
  74.0 6.5 %collective-permute-start.12 = (f32[512,128]{1,0:T(8,128)S(1)}, f32[512,128]{1,0:T(8,128)S(1)}, u32[]{:S(2)}, u32[]{:S(2)}) collective-permute-start(f32[512,128]{1,0:T(8,128)S(1)} %get-tuple-element.72), channel_id=1, source_target_pairs={{0,2},{1,33},{2,0},{3,35},{4,6},{5,37},{6,4},{7,39},{8,10},{9,41},... | collective-permute-start | bytes 786440 | tf_op jit(solution)/shard_map/ppermute | solution.py:74
  74.7 7.7 %collective-permute-start.13 = (f32[512,128]{1,0:T(8,128)S(1)}, f32[512,128]{1,0:T(8,128)S(1)}, u32[]{:S(2)}, u32[]{:S(2)}) collective-permute-start(f32[512,128]{1,0:T(8,128)S(1)} %get-tuple-element.70), channel_id=1, source_target_pairs={{0,6},{1,97},{2,4},{3,99},{4,2},{5,101},{6,0},{7,103},{8,14},{9,10... | collective-permute-start | bytes 786440 | tf_op jit(solution)/shard_map/ppermute | solution.py:74
  75.4 1.3 %collective-permute-start.14 = (f32[8,16,128]{2,1,0:T(8,128)S(1)}, f32[8,16,128]{2,1,0:T(8,128)S(1)}, u32[]{:S(2)}, u32[]{:S(2)}) collective-permute-start(f32[8,16,128]{2,1,0:T(8,128)S(1)} %back_end.1.refs_6_), channel_id=1, source_target_pairs={{0,1},{1,0},{2,3},{3,2},{4,5},{5,4},{6,7},{7,6},{8,9},{9,8},{10,11... | collective-permute-start | bytes 196616 | tf_op jit(solution)/shard_map/ppermute | solution.py:78
  95.5 1.4 %collective-permute-start.15 = (f32[224,128]{1,0:T(8,128)S(1)}, f32[224,128]{1,0:T(8,128)S(1)}, u32[]{:S(2)}, u32[]{:S(2)}) collective-permute-start(f32[224,128]{1,0:T(8,128)S(1)} %get-tuple-element.62), channel_id=1, source_target_pairs={{0,1},{1,0},{2,3},{3,2},{4,5},{5,4},{6,7},{7,6},{8,9},{9,8},{10,11... | collective-permute-start | bytes 344072 | tf_op jit(solution)/shard_map/ppermute | solution.py:78
